TPU v7x, 32 devices: a whole 2x2x4 slice. The times are simulated.
32 devices in a mesh: ctx: 2 (over y), exp: 16 (over z, x, core).
Axes of the slice: x: 2, y: 2, z: 4, core: 2. Of those that a mesh axis runs over, the one named last changes fastest.
Arguments:
- block_input: bfloat16 [16, 1024, 2560], P('exp', 'ctx'), may hold values from -6 to 6
- attn_gain: float32 [2560], replicated, may hold values from 0.25 to 1.75
- query_weight: bfloat16 [2560, 2560], P(('ctx', 'exp')), may hold values from -0.125 to 0.125
- key_matrix: bfloat16 [2560, 512], P(('ctx', 'exp')), may hold values from -0.125 to 0.125
- value_matrix: bfloat16 [2560, 512], P(('ctx', 'exp')), may hold values from -0.125 to 0.125
- output_weight: bfloat16 [2560, 2560], P(('ctx', 'exp')), may hold values from -0.5 to 0.5
- ffn_gain: float32 [2560], replicated, may hold values from 0.25 to 1.75
- shared_gate: bfloat16 [2560, 3072], P(('ctx', 'exp')), may hold values from -0.125 to 0.125
- shared_up: bfloat16 [2560, 3072], P(('ctx', 'exp')), may hold values from -0.125 to 0.125
- shared_down: bfloat16 [3072, 2560], P(('ctx', 'exp')), may hold values from -0.21875 to 0.21875
- expert_gate: bfloat16 [16, 2560, 1536], P('exp', 'ctx'), may hold values from -0.125 to 0.125
- expert_up: bfloat16 [16, 2560, 1536], P('exp', 'ctx'), may hold values from -0.125 to 0.125
- expert_down: bfloat16 [16, 1536, 2560], P('exp', None, 'ctx'), may hold values from -0.625 to 0.625
- routes: int32 [16, 1024, 6], P('exp', 'ctx'), may hold values from 0 to 15, all different within a row; in each aligned block of 512 rows (0 to 511, 512 to 1023, ..., all dimensions but the last counted through in order) at most 256 rows name the same one
- route_weights: float32 [16, 1024, 6], P('exp', 'ctx'), may hold values from 0.05 to 0.3
- cotangent: bfloat16 [16, 1024, 2560], P('exp', 'ctx'), may hold values from -6 to 6
Outputs:
- block_output: bfloat16 [16, 1024, 2560], P('exp', 'ctx')
- input_grad: float32 [16, 1024, 2560], P('exp', 'ctx')
- attn_gain_grad: float32 [2560], P(('ctx', 'exp'))
- query_grad: float32 [2560, 2560], P(('ctx', 'exp'))
- key_grad: float32 [2560, 512], P(('ctx', 'exp'))
- value_grad: float32 [2560, 512], P(('ctx', 'exp'))
- output_grad: float32 [2560, 2560], P(None, ('ctx', 'exp'))
- ffn_gain_grad: float32 [2560], P(('ctx', 'exp'))
- shared_gate_grad: float32 [2560, 3072], P(('ctx', 'exp'))
- shared_up_grad: float32 [2560, 3072], P(('ctx', 'exp'))
- shared_down_grad: float32 [3072, 2560], P(('ctx', 'exp'))
- expert_gate_grad: float32 [16, 2560, 1536], P('exp', 'ctx')
- expert_up_grad: float32 [16, 2560, 1536], P('exp', 'ctx')
- expert_down_grad: float32 [16, 1536, 2560], P('exp', None, 'ctx')
Inputs may be any that keep to these rules, and one draw needn't show every extreme that they name: `routes`: A token names 6 different experts. Within the rows of one device each expert is named by at most 256 rows, and by exactly 256 in some devices' rows.
All inputs are finite; a program needn't handle non-finite values.
Results may differ from a plain program's by a relative error of at most 0.025.
Values may be sent and summed in bfloat16 or wider, within the bound.
No kernel may reach another device: no remote copies, remote signals or barrier semaphores. Data moves between devices by JAX's collectives and lax.ppermute only.
A program may use at most 576 MiB of HBM per device.

v0:
```python
import jax
import jax.numpy as jnp
from jax import lax
from jax.sharding import PartitionSpec as P

MODEL_WIDTH = 2560
QUERY_HEADS = 20
KEY_VALUE_HEADS = 4
HEAD_SIZE = 128
TOP = 6


norm_eps = 1e-05
rope_base = 500000.0
causal_masked_score = -1e30


def rotary_apply(value_rows_all, token_positions, head_count, direction):
    row_count = value_rows_all.shape[0]
    head_width = value_rows_all.shape[1] // head_count
    half_width = head_width // 2
    shaped = value_rows_all.reshape(row_count, head_count, head_width)
    frequency = rope_base ** (-(jnp.arange(half_width, dtype=jnp.float32) * 2.0 / head_width))
    angles = token_positions[:, None].astype(jnp.float32) * frequency[None, :]
    cosine = jnp.cos(angles)[:, None, :]
    sine_part = direction * jnp.sin(angles)[:, None, :]
    first_half = shaped[:, :, :half_width]
    second = shaped[:, :, half_width:]
    turned = jnp.concatenate(
        [first_half * cosine - second * sine_part, first_half * sine_part + second * cosine],
        axis=-1,
    )
    return turned.reshape(row_count, head_count * head_width)


def rms_scale(value_rows_all):
    return lax.rsqrt(jnp.mean(value_rows_all * value_rows_all, axis=-1, keepdims=True) + norm_eps)


def norm_back(grad_normed, source, inverse, gain_vector):
    scaled = grad_normed * gain_vector
    return inverse * scaled - source * inverse**3 * jnp.mean(
        scaled * source, axis=-1, keepdims=True
    )


def silu_back(grad_act, gate_val, up_val):
    sigmoid_val = jax.nn.sigmoid(gate_val)
    grad_gate = grad_act * up_val * sigmoid_val * (1.0 + gate_val * (1.0 - sigmoid_val))
    grad_up = grad_act * gate_val * sigmoid_val
    return (grad_gate.astype(jnp.bfloat16), grad_up.astype(jnp.bfloat16))


def shared_pass(rows_in, grad_rows, gate_w, up_w, down_w):
    shared_g = jnp.dot(rows_in, gate_w, preferred_element_type=jnp.float32)
    shared_u = jnp.dot(rows_in, up_w, preferred_element_type=jnp.float32)
    shared_act = (jax.nn.silu(shared_g) * shared_u).astype(jnp.bfloat16)
    shared_out = jnp.dot(shared_act, down_w, preferred_element_type=jnp.float32)
    shared_grad_act = jnp.einsum("td,sd->ts", grad_rows, down_w, preferred_element_type=jnp.float32)
    grad_sg, grad_su = silu_back(shared_grad_act, shared_g, shared_u)
    shared_in_grad = jnp.einsum(
        "ts,ds->td", grad_sg, gate_w, preferred_element_type=jnp.float32
    ) + jnp.einsum("ts,ds->td", grad_su, up_w, preferred_element_type=jnp.float32)
    sgate_term = jnp.einsum("td,ts->ds", rows_in, grad_sg, preferred_element_type=jnp.float32)
    sup_term = jnp.einsum("td,ts->ds", rows_in, grad_su, preferred_element_type=jnp.float32)
    sdown_term = jnp.einsum("ts,td->sd", shared_act, grad_rows, preferred_element_type=jnp.float32)
    return (shared_out, shared_in_grad, sgate_term, sup_term, sdown_term)


def split_into_heads(value_rows_all, kv_heads, group_width):
    row_count = value_rows_all.shape[0]
    head_width = value_rows_all.shape[1] // (kv_heads * group_width)
    shaped = value_rows_all.reshape(row_count, kv_heads, group_width, head_width)
    return jnp.transpose(shaped, (1, 2, 0, 3)).reshape(
        kv_heads, group_width * row_count, head_width
    )


def from_heads(value_rows_all, group_width):
    kv_heads = value_rows_all.shape[0]
    row_count = value_rows_all.shape[1] // group_width
    head_width = value_rows_all.shape[2]
    shaped = value_rows_all.reshape(kv_heads, group_width, row_count, head_width)
    return jnp.transpose(shaped, (2, 0, 1, 3)).reshape(
        row_count, kv_heads * group_width * head_width
    )


def attend_block(running, key_rows, value_rows, query_rows, query_pos):
    top_score, denominator, weighted_sum = running
    row_count = key_rows.shape[0]
    kv_heads = query_rows.shape[0]
    head_width = query_rows.shape[2]
    key_head_split = key_rows.reshape(row_count, kv_heads, head_width)
    value_head_split = value_rows.reshape(row_count, kv_heads, head_width)
    scores = jnp.einsum(
        "hrd,nhd->hrn", query_rows, key_head_split, preferred_element_type=jnp.float32
    ) * head_width ** (-0.5)
    allowed = query_pos[:, None] >= jnp.arange(row_count, dtype=jnp.int32)[None, :]
    scores = jnp.where(allowed[None], scores, causal_masked_score)
    new_top = jnp.maximum(top_score, jnp.max(scores, axis=-1))
    weights = jnp.where(allowed[None], jnp.exp(scores - new_top[:, :, None]), 0.0)
    denominator = jnp.sum(weights, axis=-1)
    weighted_sum = jnp.einsum(
        "hrn,nhd->hrd",
        weights.astype(jnp.bfloat16),
        value_head_split,
        preferred_element_type=jnp.float32,
    )
    return (new_top, denominator, weighted_sum)


def attend_back(
    query_grad_sum,
    key_rows,
    value_rows,
    offset,
    query_rows,
    query_pos,
    head_gradient,
    log_total,
    row_delta,
):
    row_count = key_rows.shape[0]
    kv_heads = query_rows.shape[0]
    head_width = query_rows.shape[2]
    head_scale = head_width ** (-0.5)
    key_head_split = key_rows.reshape(row_count, kv_heads, head_width)
    value_head_split = value_rows.reshape(row_count, kv_heads, head_width)
    scores = (
        jnp.einsum("hrd,nhd->hrn", query_rows, key_head_split, preferred_element_type=jnp.float32)
        * head_scale
    )
    allowed = query_pos[:, None] >= (offset + jnp.arange(row_count, dtype=jnp.int32))[None, :]
    probabilities = jnp.where(allowed[None], jnp.exp(scores - log_total[:, :, None]), 0.0)
    grad_prob = jnp.einsum(
        "hrd,nhd->hrn", head_gradient, value_head_split, preferred_element_type=jnp.float32
    )
    grad_score = (probabilities * (grad_prob - row_delta[:, :, None])).astype(jnp.bfloat16)
    query_grad_sum = (
        query_grad_sum
        + jnp.einsum("hrn,nhd->hrd", grad_score, key_head_split, preferred_element_type=jnp.float32)
        * head_scale
    )
    grad_key = (
        jnp.einsum("hrn,hrd->nhd", grad_score, query_rows, preferred_element_type=jnp.float32)
        * head_scale
    )
    grad_value = jnp.einsum(
        "hrn,hrd->nhd",
        probabilities.astype(jnp.bfloat16),
        head_gradient,
        preferred_element_type=jnp.float32,
    )
    return (
        query_grad_sum,
        (
            grad_key.reshape(row_count, kv_heads * head_width),
            grad_value.reshape(row_count, kv_heads * head_width),
        ),
    )


def on_device(
    block_input,
    attn_gain,
    query_weight,
    key_matrix,
    value_matrix,
    output_weight,
    ffn_gain,
    shared_gate,
    shared_up,
    shared_down,
    expert_gate,
    expert_up,
    expert_down,
    routes,
    route_weights,
    cotangent,
):
    input_rows = block_input[0].astype(jnp.float32)
    local_token_rows = input_rows.shape[0]
    ctx_count = lax.axis_size("ctx")
    exp_count = lax.axis_size("exp")
    group_width = QUERY_HEADS // KEY_VALUE_HEADS
    token_positions = lax.axis_index("ctx") * local_token_rows + jnp.arange(
        local_token_rows, dtype=jnp.int32
    )
    query_pos = jnp.tile(token_positions, group_width)
    block_starts = jnp.arange(ctx_count, dtype=jnp.int32) * local_token_rows
    full_query, full_key, full_value, full_output = (
        lax.all_gather(query_weight, ("ctx", "exp"), axis=0, tiled=True),
        lax.all_gather(key_matrix, ("ctx", "exp"), axis=0, tiled=True),
        lax.all_gather(value_matrix, ("ctx", "exp"), axis=0, tiled=True),
        lax.all_gather(output_weight, ("ctx", "exp"), axis=0, tiled=True),
    )
    inverse_one = rms_scale(input_rows)
    normed_one = (input_rows * inverse_one * attn_gain).astype(jnp.bfloat16)
    query_raw = jnp.dot(normed_one, full_query, preferred_element_type=jnp.float32)
    unrotated_key = jnp.dot(normed_one, full_key, preferred_element_type=jnp.float32)
    value_raw = jnp.dot(normed_one, full_value, preferred_element_type=jnp.float32)
    rotated_query = rotary_apply(query_raw, token_positions, QUERY_HEADS, 1.0).astype(jnp.bfloat16)
    rotated_key = rotary_apply(unrotated_key, token_positions, KEY_VALUE_HEADS, 1.0).astype(
        jnp.bfloat16
    )
    value_low = value_raw.astype(jnp.bfloat16)
    query_head_split = split_into_heads(rotated_query, KEY_VALUE_HEADS, group_width)
    start_state = (
        jnp.full(
            (KEY_VALUE_HEADS, group_width * local_token_rows), causal_masked_score, jnp.float32
        ),
        jnp.zeros((KEY_VALUE_HEADS, group_width * local_token_rows), jnp.float32),
        jnp.zeros((KEY_VALUE_HEADS, group_width * local_token_rows, HEAD_SIZE), jnp.float32),
    )
    folded = attend_block(
        start_state,
        lax.all_gather(rotated_key, "ctx", axis=0, tiled=True),
        lax.all_gather(value_low, "ctx", axis=0, tiled=True),
        query_head_split,
        query_pos,
    )
    top_score, denominator, weighted_sum = folded
    log_total = top_score + jnp.log(denominator)
    attended = weighted_sum / denominator[:, :, None]
    attended_low = from_heads(attended, group_width).astype(jnp.bfloat16)
    attn_out = jnp.dot(attended_low, full_output, preferred_element_type=jnp.float32)
    middle = input_rows + attn_out
    inverse_two = rms_scale(middle)
    normed_two = (middle * inverse_two * ffn_gain).astype(jnp.bfloat16)
    grad_low = cotangent[0]
    grad_top = grad_low.astype(jnp.float32)
    whole_sgate, whole_sup, whole_sdown = (
        lax.all_gather(shared_gate, ("ctx", "exp"), axis=0, tiled=True),
        lax.all_gather(shared_up, ("ctx", "exp"), axis=0, tiled=True),
        lax.all_gather(shared_down, ("ctx", "exp"), axis=0, tiled=True),
    )
    shared_out, shared_in_grad, sgate_term, sup_term, sdown_term = shared_pass(
        normed_two, grad_low, whole_sgate, whole_sup, whole_sdown
    )
    capacity = local_token_rows * TOP * 4 // (3 * exp_count)
    flat_routes = routes[0].reshape(-1)
    onehot = (flat_routes[:, None] == jnp.arange(exp_count, dtype=jnp.int32)[None, :]).astype(
        jnp.int32
    )
    before = jnp.cumsum(onehot, axis=0) - onehot
    slot_index = flat_routes * capacity + jnp.sum(before * onehot, axis=1)
    dispatch = (
        jnp.zeros((exp_count * capacity, MODEL_WIDTH), jnp.bfloat16)
        .at[slot_index]
        .set(jnp.repeat(normed_two, TOP, axis=0))
    )
    received = lax.all_to_all(
        dispatch.reshape(exp_count, capacity, MODEL_WIDTH),
        "exp",
        split_axis=0,
        concat_axis=0,
        tiled=True,
    ).reshape(exp_count * capacity, MODEL_WIDTH)
    gate_full, up_full, down_full = (
        lax.all_gather(expert_gate[0], "ctx", axis=0, tiled=True),
        lax.all_gather(expert_up[0], "ctx", axis=0, tiled=True),
        lax.all_gather(expert_down[0], "ctx", axis=1, tiled=True),
    )
    expert_g = jnp.dot(received, gate_full, preferred_element_type=jnp.float32)
    expert_u = jnp.dot(received, up_full, preferred_element_type=jnp.float32)
    expert_act = (jax.nn.silu(expert_g) * expert_u).astype(jnp.bfloat16)
    expert_out = jnp.dot(expert_act, down_full, preferred_element_type=jnp.float32).astype(
        jnp.bfloat16
    )
    returned = lax.all_to_all(
        expert_out.reshape(exp_count, capacity, MODEL_WIDTH),
        "exp",
        split_axis=0,
        concat_axis=0,
        tiled=True,
    ).reshape(exp_count * capacity, MODEL_WIDTH)
    picked = returned[slot_index].reshape(local_token_rows, TOP, MODEL_WIDTH).astype(jnp.float32)
    gate_values = route_weights[0]
    routed_out = jnp.sum(gate_values[:, :, None] * picked, axis=1)
    output = middle + shared_out + routed_out
    weighted = (
        (gate_values[:, :, None] * grad_top[:, None, :])
        .reshape(local_token_rows * TOP, MODEL_WIDTH)
        .astype(jnp.bfloat16)
    )
    grad_buffer = (
        jnp.zeros((exp_count * capacity, MODEL_WIDTH), jnp.bfloat16).at[slot_index].set(weighted)
    )
    grad_expert = lax.all_to_all(
        grad_buffer.reshape(exp_count, capacity, MODEL_WIDTH),
        "exp",
        split_axis=0,
        concat_axis=0,
        tiled=True,
    ).reshape(exp_count * capacity, MODEL_WIDTH)
    grad_act = jnp.einsum("rd,fd->rf", grad_expert, down_full, preferred_element_type=jnp.float32)
    grad_eg, grad_eu = silu_back(grad_act, expert_g, expert_u)
    grad_rows = (
        jnp.einsum("rf,df->rd", grad_eg, gate_full, preferred_element_type=jnp.float32)
        + jnp.einsum("rf,df->rd", grad_eu, up_full, preferred_element_type=jnp.float32)
    ).astype(jnp.bfloat16)
    grad_back = lax.all_to_all(
        grad_rows.reshape(exp_count, capacity, MODEL_WIDTH),
        "exp",
        split_axis=0,
        concat_axis=0,
        tiled=True,
    ).reshape(exp_count * capacity, MODEL_WIDTH)
    routed_grad = jnp.sum(
        grad_back[slot_index].reshape(local_token_rows, TOP, MODEL_WIDTH).astype(jnp.float32),
        axis=1,
    )
    gate_term = jnp.einsum("rd,rf->df", received, grad_eg, preferred_element_type=jnp.float32)
    up_term = jnp.einsum("rd,rf->df", received, grad_eu, preferred_element_type=jnp.float32)
    down_term = jnp.einsum("rf,rd->fd", expert_act, grad_expert, preferred_element_type=jnp.float32)
    expert_gate_grad, expert_up_grad, expert_down_grad = (
        lax.psum_scatter(
            gate_term[None].astype(jnp.bfloat16), "ctx", scatter_dimension=1, tiled=True
        ).astype(jnp.float32),
        lax.psum_scatter(
            up_term[None].astype(jnp.bfloat16), "ctx", scatter_dimension=1, tiled=True
        ).astype(jnp.float32),
        lax.psum_scatter(
            down_term[None].astype(jnp.bfloat16), "ctx", scatter_dimension=2, tiled=True
        ).astype(jnp.float32),
    )
    sum_sg, sum_su, sum_sd = (
        lax.psum_scatter(sgate_term, ("ctx", "exp"), scatter_dimension=0, tiled=True),
        lax.psum_scatter(sup_term, ("ctx", "exp"), scatter_dimension=0, tiled=True),
        lax.psum_scatter(sdown_term, ("ctx", "exp"), scatter_dimension=0, tiled=True),
    )
    grad_two = shared_in_grad + routed_grad
    ffn_gain_term = jnp.sum(grad_two * middle * inverse_two, axis=0)
    grad_middle = grad_top + norm_back(grad_two, middle, inverse_two, ffn_gain)
    grad_middle_low = grad_middle.astype(jnp.bfloat16)
    output_term = jnp.einsum(
        "tq,td->qd", attended_low, grad_middle_low, preferred_element_type=jnp.float32
    )
    attended_gradient = jnp.einsum(
        "td,qd->tq", grad_middle_low, full_output, preferred_element_type=jnp.float32
    ).astype(jnp.bfloat16)
    head_gradient = split_into_heads(attended_gradient, KEY_VALUE_HEADS, group_width)
    row_delta = jnp.sum(head_gradient.astype(jnp.float32) * attended, axis=-1)
    key_source, value_source = (
        lax.all_gather(rotated_key, "ctx", axis=0, tiled=True),
        lax.all_gather(value_low, "ctx", axis=0, tiled=True),
    )

    def scan_back(running, block_item):
        return attend_back(
            running,
            block_item[0],
            block_item[1],
            block_item[2],
            query_head_split,
            query_pos,
            head_gradient,
            log_total,
            row_delta,
        )

    query_grad_heads, key_value_terms = lax.scan(
        scan_back,
        jnp.zeros((KEY_VALUE_HEADS, group_width * local_token_rows, HEAD_SIZE), jnp.float32),
        (
            key_source.reshape(ctx_count, local_token_rows, -1),
            value_source.reshape(ctx_count, local_token_rows, -1),
            block_starts,
        ),
    )
    key_terms = key_value_terms[0].reshape(ctx_count * local_token_rows, -1)
    value_terms = key_value_terms[1].reshape(ctx_count * local_token_rows, -1)
    local_key_gradient, value_grad_local = (
        lax.psum_scatter(
            key_terms.astype(jnp.bfloat16), "ctx", scatter_dimension=0, tiled=True
        ).astype(jnp.float32),
        lax.psum_scatter(
            value_terms.astype(jnp.bfloat16), "ctx", scatter_dimension=0, tiled=True
        ).astype(jnp.float32),
    )
    grad_query_raw = rotary_apply(
        from_heads(query_grad_heads, group_width), token_positions, QUERY_HEADS, -1.0
    ).astype(jnp.bfloat16)
    unrotated_key_gradient = rotary_apply(
        local_key_gradient, token_positions, KEY_VALUE_HEADS, -1.0
    ).astype(jnp.bfloat16)
    grad_value_raw = value_grad_local.astype(jnp.bfloat16)
    query_term = jnp.einsum(
        "td,tq->dq", normed_one, grad_query_raw, preferred_element_type=jnp.float32
    )
    key_term = jnp.einsum(
        "td,tq->dq", normed_one, unrotated_key_gradient, preferred_element_type=jnp.float32
    )
    value_term = jnp.einsum(
        "td,tq->dq", normed_one, grad_value_raw, preferred_element_type=jnp.float32
    )
    grad_one = (
        jnp.einsum("tq,dq->td", grad_query_raw, full_query, preferred_element_type=jnp.float32)
        + jnp.einsum(
            "tq,dq->td", unrotated_key_gradient, full_key, preferred_element_type=jnp.float32
        )
        + jnp.einsum("tq,dq->td", grad_value_raw, full_value, preferred_element_type=jnp.float32)
    )
    attn_gain_term = jnp.sum(grad_one * input_rows * inverse_one, axis=0)
    input_grad = grad_middle + norm_back(grad_one, input_rows, inverse_one, attn_gain)
    sum_ag, sum_fg, sum_q, sum_k, sum_v, sum_o = (
        lax.psum_scatter(attn_gain_term, ("ctx", "exp"), scatter_dimension=0, tiled=True),
        lax.psum_scatter(ffn_gain_term, ("ctx", "exp"), scatter_dimension=0, tiled=True),
        lax.psum_scatter(query_term, ("ctx", "exp"), scatter_dimension=0, tiled=True),
        lax.psum_scatter(key_term, ("ctx", "exp"), scatter_dimension=0, tiled=True),
        lax.psum_scatter(value_term, ("ctx", "exp"), scatter_dimension=0, tiled=True),
        lax.psum_scatter(output_term, ("ctx", "exp"), scatter_dimension=1, tiled=True),
    )
    return (
        output.astype(jnp.bfloat16)[None],
        input_grad[None],
        sum_ag,
        sum_q,
        sum_k,
        sum_v,
        sum_o,
        sum_fg,
        sum_sg,
        sum_su,
        sum_sd,
        expert_gate_grad,
        expert_up_grad,
        expert_down_grad,
    )


def solution(mesh):
    return jax.shard_map(
        on_device,
        mesh=mesh,
        in_specs=(
            P("exp", "ctx", None),
            P(),
            P(("ctx", "exp"), None),
            P(("ctx", "exp"), None),
            P(("ctx", "exp"), None),
            P(("ctx", "exp"), None),
            P(),
            P(("ctx", "exp"), None),
            P(("ctx", "exp"), None),
            P(("ctx", "exp"), None),
            P("exp", "ctx", None),
            P("exp", "ctx", None),
            P("exp", None, "ctx"),
            P("exp", "ctx", None),
            P("exp", "ctx", None),
            P("exp", "ctx", None),
        ),
        out_specs=(
            P("exp", "ctx", None),
            P("exp", "ctx", None),
            P(("ctx", "exp")),
            P(("ctx", "exp"), None),
            P(("ctx", "exp"), None),
            P(("ctx", "exp"), None),
            P(None, ("ctx", "exp")),
            P(("ctx", "exp")),
            P(("ctx", "exp"), None),
            P(("ctx", "exp"), None),
            P(("ctx", "exp"), None),
            P("exp", "ctx", None),
            P("exp", "ctx", None),
            P("exp", None, "ctx"),
        ),
        check_vma=False,
    )
```

profile of v0, /device:TPU:0, one launch (start us, length us, event | category | flops | bytes accessed | tf_op | source)
XLA Modules:
  0.0 4804.3 jit_solution(14480490643654791583)
XLA Ops:
  13.6 58.0 %all-gather.18.cloned.1.call-done = bf16[2560,512]{1,0:T(8,128)(2,1)} async-done(((bf16[80,512]{1,0:T(8,128)(2,1)}), bf16[2560,512]{1,0:T(8,128)(2,1)}) %all-gather.18.cloned.1.call-update) | async-done | bytes 2621456 | tf_op jit(solution)/shard_map/all_gather | solution.py:194
  80.4 50.9 %all-gather.22.cloned.1.call-done = bf16[2560,512]{1,0:T(8,128)(2,1)} async-done(((bf16[80,512]{1,0:T(8,128)(2,1)}), bf16[2560,512]{1,0:T(8,128)(2,1)}) %all-gather.22.cloned.1.call-update) | async-done | bytes 2621456 | tf_op jit(solution)/shard_map/all_gather | solution.py:195
  146.6 85.1 %all-gather.16.cloned.1.call-done = bf16[2560,2560]{1,0:T(8,128)(2,1)} async-done(((bf16[80,2560]{1,0:T(8,128)(2,1)}), bf16[2560,2560]{1,0:T(8,128)(2,1)}) %all-gather.16.cloned.1.call-update) | async-done | bytes 13107216 | tf_op jit(solution)/shard_map/all_gather | solution.py:193
  332.7 45.1 all-gather.26.cloned.1.call-done
  575.9 293.1 %all-to-all-done = bf16[16,256,2560]{2,1,0:T(8,128)(2,1)} async-done(((bf16[16,256,2560]{2,1,0:T(8,128)(2,1)}), bf16[16,256,2560]{2,1,0:T(8,128)(2,1)}, u32[]{:S(2)}, u32[]{:S(2)}) %all-to-all-start) | async-done | bytes 20971552 | tf_op jit(solution)/shard_map/all_to_all | solution.py:253
  869.1 129.0 %all-to-all-start.2 = ((bf16[16,256,2560]{2,1,0:T(8,128)(2,1)}), bf16[16,256,2560]{2,1,0:T(8,128)(2,1)}, u32[]{:S(2)}, u32[]{:S(2)}) async-start(bf16[16,256,2560]{2,1,0:T(8,128)(2,1)} %bitcast.267), calls=%async_computation.2 | async-start | bytes 41943040 | tf_op jit(solution)/shard_map/all_to_all | solution.py:290
  1080.0 361.6 %all-to-all-done.2 = bf16[16,256,2560]{2,1,0:T(8,128)(2,1)} async-done(((bf16[16,256,2560]{2,1,0:T(8,128)(2,1)}), bf16[16,256,2560]{2,1,0:T(8,128)(2,1)}, u32[]{:S(2)}, u32[]{:S(2)}) %all-to-all-start.2) | async-done | bytes 20971552 | tf_op jit(solution)/shard_map/all_to_all | solution.py:290
  1441.6 51.3 %multiply_convert_fusion.1 = (bf16[4096,1536]{1,0:T(8,128)(2,1)}, bf16[4096,1536]{1,0:T(8,128)(2,1)}, bf16[4096,1536]{1,0:T(8,128)(2,1)}) fusion(f32[4096,1536]{1,0:T(8,128)} %fusion.30, f32[4096,1536]{1,0:T(8,128)} %fusion.26, bf16[4096,2560]{1,0:T(8,128)(2,1)} %bitcast.29, bf16[1,1536,2560]{2,1,0:T(8,128)(2,1)} %all-gather.38.cloned.1.call-done), kind=kOutput, calls=%fused_computation.29 | convolution fusion | flops 32312918016 | bytes 116916224 | tf_op jit(solution)/shard_map/rd,fd->rf/dot_general | solution.py:297
  1492.9 41.7 fusion.28
  1534.6 43.5 add_convert_fusion
  1578.1 87.8 %all-to-all-start.3 = ((bf16[16,256,2560]{2,1,0:T(8,128)(2,1)}), bf16[16,256,2560]{2,1,0:T(8,128)(2,1)}, u32[]{:S(2)}, u32[]{:S(2)}) async-start(bf16[16,256,2560]{2,1,0:T(8,128)(2,1)} %bitcast.269), calls=%async_computation.3 | async-start | bytes 41943040 | tf_op jit(solution)/shard_map/all_to_all | solution.py:303
  1702.4 368.4 %all-gather.32.cloned.1.call-done = bf16[3072,2560]{1,0:T(8,128)(2,1)} async-done(((bf16[96,2560]{1,0:T(8,128)(2,1)}), bf16[3072,2560]{1,0:T(8,128)(2,1)}) %all-gather.32.cloned.1.call-update) | async-done | bytes 15728656 | tf_op jit(solution)/shard_map/all_gather | solution.py:236
  2250.2 135.1 %while.15 = (s32[]{:T(128)}, f32[4,2560,128]{2,1,0:T(8,128)}, bf16[2,512,512]{2,1,0:T(8,128)(2,1)}, bf16[2,512,512]{2,1,0:T(8,128)(2,1)}, s32[2]{0:T(128)S(1)}, ...) while((s32[]{:T(128)}, f32[4,2560,128]{2,1,0:T(8,128)}, ...), condition=%wide.region_14.15_spmd.clone, body=%wide.region_13.14_spmd.clone.sunk | while | flops 6769082880 | bytes 129407656 | solution.py:363
  2656.8 87.7 %all-to-all-start.1 = ((bf16[16,256,2560]{2,1,0:T(8,128)(2,1)}), bf16[16,256,2560]{2,1,0:T(8,128)(2,1)}, u32[]{:S(2)}, u32[]{:S(2)}) async-start(bf16[16,256,2560]{2,1,0:T(8,128)(2,1)} %bitcast.270), calls=%async_computation.1 | async-start | bytes 41943040 | tf_op jit(solution)/shard_map/all_to_all | solution.py:271
  2757.5 43.5 reduce-scatter.35.cloned.1.call-done
  2806.9 391.8 %all-to-all-done.1 = bf16[16,256,2560]{2,1,0:T(8,128)(2,1)} async-done(((bf16[16,256,2560]{2,1,0:T(8,128)(2,1)}), bf16[16,256,2560]{2,1,0:T(8,128)(2,1)}, u32[]{:S(2)}, u32[]{:S(2)}) %all-to-all-start.1) | async-done | bytes 20971552 | tf_op jit(solution)/shard_map/all_to_all | solution.py:271
  3277.0 56.6 %multiply_reduce_fusion = f32[512,2560]{1,0:T(8,128)} fusion(f32[512,6,2560]{2,1,0:T(8,128)} %reshape.458, f32[512,6]{1,0:T(8,128)S(1)} %bitcast.295), kind=kLoop, calls=%fused_computation.22 | loop fusion | flops 14417920 | bytes 36712448 | tf_op jit(solution)/shard_map/reduce_sum | solution.py:280
  3356.1 171.1 %all-reduce.2 = (f32[2560]{0:T(1024)S(1)}, f32[2560]{0:T(1024)S(1)}) all-reduce(f32[2560]{0:T(1024)S(1)} %get-tuple-element.161, f32[2560]{0:T(1024)S(1)} %copy-done.47), channel_id=7, replica_groups=mesh['ctx'=2,'exp'=16] {'ctx','exp'}, use_global_device_ids=true, to_apply=%region_19.20.clone | all-reduce | flops 5120 | bytes 40960
  3534.7 119.4 %reduce-scatter.27.cloned.1.call-done = f32[80,3072]{1,0:T(8,128)} async-done(((f32[2560,3072]{1,0:T(8,128)}), f32[80,3072]{1,0:T(8,128)}) %reduce-scatter.27.cloned.1.call-update) | async-done | bytes 983056 | tf_op jit(solution)/shard_map/reduce_scatter | solution.py:330
  3654.1 291.1 %reduce-scatter.29.cloned.1.call-done = f32[96,2560]{1,0:T(8,128)} async-done(((f32[3072,2560]{1,0:T(8,128)}), f32[96,2560]{1,0:T(8,128)}) %reduce-scatter.29.cloned.1.call-update) | async-done | bytes 983056 | tf_op jit(solution)/shard_map/reduce_scatter | solution.py:331
  3945.3 145.7 %reduce-scatter.19.cloned.1.call-done = f32[80,512]{1,0:T(8,128)} async-done(((f32[2560,512]{1,0:T(8,128)}), f32[80,512]{1,0:T(8,128)}) %reduce-scatter.19.cloned.1.call-update) | async-done | bytes 163856 | tf_op jit(solution)/shard_map/reduce_scatter | solution.py:411
  4091.0 142.6 %reduce-scatter.21.cloned.1.call-done = f32[80,512]{1,0:T(8,128)} async-done(((f32[2560,512]{1,0:T(8,128)}), f32[80,512]{1,0:T(8,128)}) %reduce-scatter.21.cloned.1.call-update) | async-done | bytes 163856 | tf_op jit(solution)/shard_map/reduce_scatter | solution.py:412
  4233.6 279.5 %reduce-scatter.23.cloned.1.call-done = f32[2560,80]{0,1:T(8,128)} async-done(((f32[2560,2560]{0,1:T(8,128)}), f32[2560,80]{0,1:T(8,128)}) %reduce-scatter.23.cloned.1.call-update) | async-done | bytes 819216 | tf_op jit(solution)/shard_map/reduce_scatter | solution.py:413
  4513.1 284.2 %reduce-scatter.17.cloned.1.call-done = f32[80,2560]{1,0:T(8,128)} async-done(((f32[2560,2560]{1,0:T(8,128)}), f32[80,2560]{1,0:T(8,128)}) %reduce-scatter.17.cloned.1.call-update) | async-done | bytes 819216 | tf_op jit(solution)/shard_map/reduce_scatter | solution.py:410
  (311 shorter events, 1159.9 us)
Async XLA Ops:
  9.4 257.5 %all-gather.20.cloned.1.call-start = ((), (), s32[]{:S(2)}) async-start(), calls=%async_computation.18 | async-start | bytes 1572864 | tf_op jit(solution)/shard_map/all_gather | solution.py:218
  80.4 225.4 %all-gather.24.cloned.1.call-start = ((), (), s32[]{:S(2)}) async-start(), calls=%async_computation.20 | async-start | bytes 1572864 | tf_op jit(solution)/shard_map/all_gather | solution.py:219
  135.5 242.3 %all-gather.26.cloned.1.call-start = ((), (), s32[]{:S(2)}) async-start(), calls=%async_computation.21 | async-start | bytes 13516800 | tf_op jit(solution)/shard_map/all_gather | solution.py:196
  462.2 406.9 %all-to-all-start = ((bf16[16,256,2560]{2,1,0:T(8,128)(2,1)}), bf16[16,256,2560]{2,1,0:T(8,128)(2,1)}, u32[]{:S(2)}, u32[]{:S(2)}) async-start(bf16[16,256,2560]{2,1,0:T(8,128)(2,1)} %bitcast.266), calls=%async_computation | async-start | bytes 41943040 | tf_op jit(solution)/shard_map/all_to_all | solution.py:253
  467.6 531.3 %all-gather.36.cloned.1.call-start = ((), (), s32[]{:S(2)}) async-start(), calls=%async_computation.38 | async-start | bytes 11796480 | tf_op jit(solution)/shard_map/all_gather | solution.py:262
  468.3 571.1 %all-gather.34.cloned.1.call-start = ((), (), s32[]{:S(2)}) async-start(), calls=%async_computation.37 | async-start | bytes 11796480 | tf_op jit(solution)/shard_map/all_gather | solution.py:261
  469.1 610.9 %all-gather.38.cloned.1.call-start = ((), (), s32[]{:S(2)}) async-start(), calls=%async_computation.39 | async-start | bytes 11796480 | tf_op jit(solution)/shard_map/all_gather | solution.py:263
  469.8 1202.9 %all-gather.28.cloned.1.call-start = ((), (), s32[]{:S(2)}) async-start(), calls=%async_computation.22 | async-start | bytes 16220160 | tf_op jit(solution)/shard_map/all_gather | solution.py:234
  869.1 572.5 %all-to-all-start.2 = ((bf16[16,256,2560]{2,1,0:T(8,128)(2,1)}), bf16[16,256,2560]{2,1,0:T(8,128)(2,1)}, u32[]{:S(2)}, u32[]{:S(2)}) async-start(bf16[16,256,2560]{2,1,0:T(8,128)(2,1)} %bitcast.267), calls=%async_computation.2 | async-start | bytes 41943040 | tf_op jit(solution)/shard_map/all_to_all | solution.py:290
  998.1 690.8 %all-gather.30.cloned.1.call-start = ((), (), s32[]{:S(2)}) async-start(), calls=%async_computation.23 | async-start | bytes 16220160 | tf_op jit(solution)/shard_map/all_gather | solution.py:235
  1578.1 531.3 %all-to-all-start.3 = ((bf16[16,256,2560]{2,1,0:T(8,128)(2,1)}), bf16[16,256,2560]{2,1,0:T(8,128)(2,1)}, u32[]{:S(2)}, u32[]{:S(2)}) async-start(bf16[16,256,2560]{2,1,0:T(8,128)(2,1)} %bitcast.269), calls=%async_computation.3 | async-start | bytes 41943040 | tf_op jit(solution)/shard_map/all_to_all | solution.py:303
  1665.9 404.9 %all-gather.32.cloned.1.call-start = ((), (), s32[]{:S(2)}) async-start(), calls=%async_computation.24 | async-start | bytes 16220160 | tf_op jit(solution)/shard_map/all_gather | solution.py:236
  1666.5 897.2 %reduce-scatter.13.cloned.1.call-start = ((), (), s32[]{:S(2)}) async-start(), calls=%async_computation.25 | async-start | bytes 1572864 | tf_op jit(solution)/shard_map/reduce_scatter | solution.py:375
  2386.0 358.6 %reduce-scatter.31.cloned.1.call-start = ((), (), s32[]{:S(2)}) async-start(), calls=%async_computation.34 | async-start | bytes 11796480 | tf_op jit(solution)/shard_map/reduce_scatter | solution.py:318
  2426.8 324.3 %reduce-scatter.33.cloned.1.call-start = ((), (), s32[]{:S(2)}) async-start(), calls=%async_computation.35 | async-start | bytes 11796480 | tf_op jit(solution)/shard_map/reduce_scatter | solution.py:321
  2467.6 333.4 %reduce-scatter.35.cloned.1.call-start = ((), (), s32[]{:S(2)}) async-start(), calls=%async_computation.36 | async-start | bytes 11796480 | tf_op jit(solution)/shard_map/reduce_scatter | solution.py:324
  2509.0 1025.8 %reduce-scatter.25.cloned.1.call-start = ((), (), s32[]{:S(2)}) async-start(), calls=%async_computation.31 | async-start | bytes 32440320 | tf_op jit(solution)/shard_map/reduce_scatter | solution.py:329
  2528.1 1126.0 %reduce-scatter.27.cloned.1.call-start = ((), (), s32[]{:S(2)}) async-start(), calls=%async_computation.32 | async-start | bytes 32440320 | tf_op jit(solution)/shard_map/reduce_scatter | solution.py:330
  2545.1 1400.2 %reduce-scatter.29.cloned.1.call-start = ((), (), s32[]{:S(2)}) async-start(), calls=%async_computation.33 | async-start | bytes 32440320 | tf_op jit(solution)/shard_map/reduce_scatter | solution.py:331
  2563.6 1527.4 %reduce-scatter.19.cloned.1.call-start = ((), (), s32[]{:S(2)}) async-start(), calls=%async_computation.28 | async-start | bytes 5406720 | tf_op jit(solution)/shard_map/reduce_scatter | solution.py:411
  2572.4 1661.2 %reduce-scatter.21.cloned.1.call-start = ((), (), s32[]{:S(2)}) async-start(), calls=%async_computation.29 | async-start | bytes 5406720 | tf_op jit(solution)/shard_map/reduce_scatter | solution.py:412
  2577.8 1935.4 %reduce-scatter.23.cloned.1.call-start = ((), (), s32[]{:S(2)}) async-start(), calls=%async_computation.30 | async-start | bytes 27033600 | tf_op jit(solution)/shard_map/reduce_scatter | solution.py:413
  2593.0 2204.3 %reduce-scatter.17.cloned.1.call-start = ((), (), s32[]{:S(2)}) async-start(), calls=%async_computation.27 | async-start | bytes 27033600 | tf_op jit(solution)/shard_map/reduce_scatter | solution.py:410
  2656.8 541.9 %all-to-all-start.1 = ((bf16[16,256,2560]{2,1,0:T(8,128)(2,1)}), bf16[16,256,2560]{2,1,0:T(8,128)(2,1)}, u32[]{:S(2)}, u32[]{:S(2)}) async-start(bf16[16,256,2560]{2,1,0:T(8,128)(2,1)} %bitcast.270), calls=%async_computation.1 | async-start | bytes 41943040 | tf_op jit(solution)/shard_map/all_to_all | solution.py:271
  (59 other events, 3474.4 us)
Sparse Core Ops, SparseCore 0:
  11.0 60.5 all-gather.17
  74.5 56.8 all-gather.21
  134.2 97.4 all-gather.15
  233.7 19.4 all-gather.19
  255.2 21.2 all-gather.23
  279.2 98.4 all-gather.25
  469.9 99.2 all-gather.35
  570.8 98.0 all-gather.33
  670.5 98.0 all-gather.37
  771.4 167.6 all-gather.27
  1001.8 401.1 all-gather.29
  1669.3 401.4 all-gather.31
  2385.5 102.6 reduce-scatter.12
  2490.4 20.3 reduce-scatter.14
  2513.5 94.1 reduce-scatter.30
  2610.5 94.1 reduce-scatter.32
  2706.8 94.1 reduce-scatter.34
  2808.9 552.3 reduce-scatter.24
  3369.4 284.6 reduce-scatter.26
  3662.1 283.1 reduce-scatter.28
  3948.3 142.6 reduce-scatter.18
  4094.0 139.6 reduce-scatter.20
  4236.6 276.4 reduce-scatter.22
  4516.0 281.2 reduce-scatter.16
where the time goes:
time: 4820 us; the launch traced here: 4800 us
  waiting for transfers between devices  2970 us (62%)
  matrix products  773 us (16%)
  local copies, waits for them, and re-layouts  382 us (8%)
  starting transfers between devices  311 us (6%)
  other arithmetic  180 us (4%)
  blocking collectives  171 us (4%)
    all_to_all x1, waiting for transfers between devices, on_device(): lax.all_to_all(expert_out.reshape(exp_count, capacity, MODEL_WIDTH), 'exp...  392 us
    all_gather x1, waiting for transfers between devices, on_device(): lax.all_gather(shared_down, ('ctx', 'exp'), axis=0, tiled=True)  368 us
    all_to_all x1, waiting for transfers between devices, on_device(): lax.all_to_all(grad_buffer.reshape(exp_count, capacity, MODEL_WIDTH), 'ex...  362 us
    all_to_all x1, waiting for transfers between devices, on_device(): lax.all_to_all(dispatch.reshape(exp_count, capacity, MODEL_WIDTH), 'exp',...  293 us
    reduce_scatter x1, waiting for transfers between devices, on_device(): lax.psum_scatter(sdown_term, ('ctx', 'exp'), scatter_dimension=0, tiled=T...  291 us
    reduce_scatter x1, waiting for transfers between devices, on_device(): lax.psum_scatter(query_term, ('ctx', 'exp'), scatter_dimension=0, tiled=T...  284 us
    reduce_scatter x1, waiting for transfers between devices, on_device(): lax.psum_scatter(output_term, ('ctx', 'exp'), scatter_dimension=1, tiled=...  280 us
    unnamed x1, blocking collectives  171 us
  transfers between devices with their start and end apart: 28, of which 16 were waited for; matrix products, arithmetic and copies ran while one was open for 20% of the time, Pallas kernels for 0%

commit v1 on v0

v1 whole, which is shorter than its diff:
```python
import functools

import jax
import jax.numpy as jnp
import numpy as np
from jax import lax
from jax.experimental import pallas as pl
from jax.experimental.pallas import tpu as pltpu
from jax.sharding import PartitionSpec as P

MODEL_WIDTH = 2560
QUERY_HEADS = 20
KEY_VALUE_HEADS = 4
HEAD_SIZE = 128
TOP = 6
GROUP = QUERY_HEADS // KEY_VALUE_HEADS
QUERY_WIDTH = QUERY_HEADS * HEAD_SIZE
KEY_WIDTH = KEY_VALUE_HEADS * HEAD_SIZE
KERNEL_VMEM = 56 * 1024 * 1024


norm_eps = 1e-05
rope_base = 500000.0
causal_masked_score = -1e30


def rope_tables(token_positions):
    half_width = HEAD_SIZE // 2
    frequency = rope_base ** (-(jnp.arange(half_width, dtype=jnp.float32) * 2.0 / HEAD_SIZE))
    angles = token_positions[:, None].astype(jnp.float32) * frequency[None, :]
    cosine, sine = jnp.cos(angles), jnp.sin(angles)
    return (
        jnp.concatenate([cosine, cosine], axis=1),
        jnp.concatenate([-sine, sine], axis=1),
    )


def rms_scale(value_rows_all):
    return lax.rsqrt(jnp.mean(value_rows_all * value_rows_all, axis=-1, keepdims=True) + norm_eps)


def norm_back(grad_normed, source, inverse, gain_vector):
    scaled = grad_normed * gain_vector
    return inverse * scaled - source * inverse**3 * jnp.mean(
        scaled * source, axis=-1, keepdims=True
    )


def silu_back(grad_act, gate_val, up_val):
    sigmoid_val = jax.nn.sigmoid(gate_val)
    grad_gate = grad_act * up_val * sigmoid_val * (1.0 + gate_val * (1.0 - sigmoid_val))
    grad_up = grad_act * gate_val * sigmoid_val
    return (grad_gate.astype(jnp.bfloat16), grad_up.astype(jnp.bfloat16))


def dot32(left, right):
    return jnp.dot(left, right, preferred_element_type=jnp.float32)


def dot_t(left, right):
    return lax.dot_general(
        left, right, (((1,), (1,)), ((), ())), preferred_element_type=jnp.float32
    )


def t_dot(left, right):
    return lax.dot_general(
        left, right, (((0,), (0,)), ((), ())), preferred_element_type=jnp.float32
    )


def tie(*values):
    return lax.optimization_barrier(values)


def kernel_params():
    return pltpu.CompilerParams(vmem_limit_bytes=KERNEL_VMEM)


def cost(flops, bytes_accessed, transcendentals=0):
    return pl.CostEstimate(
        flops=int(flops), bytes_accessed=int(bytes_accessed), transcendentals=int(transcendentals)
    )


def turn(values, cosine, sine):
    return values * cosine + pltpu.roll(values, HEAD_SIZE // 2, 1) * sine


def project_kernel(plain_from, rows_ref, weight_ref, cos_ref, sin_ref, out_ref):
    product = dot32(rows_ref[...], weight_ref[...])
    plain = pl.program_id(0) >= plain_from
    cosine = jnp.where(plain, 1.0, cos_ref[...])
    sine = jnp.where(plain, 0.0, sin_ref[...])
    for head in range(product.shape[1] // HEAD_SIZE):
        lanes = slice(head * HEAD_SIZE, (head + 1) * HEAD_SIZE)
        out_ref[:, lanes] = turn(product[:, lanes], cosine, sine).astype(jnp.bfloat16)


def project(rows, weight, tables, first_block, blocks, plain_from):
    count = rows.shape[0]
    return pl.pallas_call(
        functools.partial(project_kernel, plain_from),
        grid=(blocks,),
        in_specs=[
            pl.BlockSpec(rows.shape, lambda j: (0, 0)),
            pl.BlockSpec((weight.shape[0], KEY_WIDTH), lambda j: (0, first_block + j)),
            pl.BlockSpec(tables[0].shape, lambda j: (0, 0)),
            pl.BlockSpec(tables[1].shape, lambda j: (0, 0)),
        ],
        out_specs=pl.BlockSpec((count, KEY_WIDTH), lambda j: (0, j)),
        out_shape=jax.ShapeDtypeStruct((count, blocks * KEY_WIDTH), jnp.bfloat16),
        compiler_params=kernel_params(),
        cost_estimate=cost(
            2 * count * weight.shape[0] * blocks * KEY_WIDTH,
            2 * weight.shape[0] * (blocks * KEY_WIDTH + count),
        ),
        name="project",
    )(rows, weight, *tables)


def attend_probs(offset, first_row, query, keys):
    scores = dot_t(query, keys) * HEAD_SIZE ** (-0.5)
    rows = lax.broadcasted_iota(jnp.int32, scores.shape, 0) + (offset + first_row)
    places = lax.broadcasted_iota(jnp.int32, scores.shape, 1)
    scores = jnp.where(rows >= places, scores, causal_masked_score)
    weights = jnp.exp(scores - jnp.max(scores, axis=1, keepdims=True))
    return weights * (1.0 / jnp.sum(weights, axis=1, keepdims=True))


def attend_kernel(tile, offset_ref, query_ref, key_ref, value_ref, out_ref):
    keys, values = key_ref[...], value_ref[...]
    for head in range(GROUP):
        lanes = slice(head * HEAD_SIZE, (head + 1) * HEAD_SIZE)
        for start in range(0, query_ref.shape[0], tile):
            rows = slice(start, start + tile)
            probs = attend_probs(offset_ref[0], start, query_ref[rows, lanes], keys)
            out_ref[rows, lanes] = dot32(probs.astype(jnp.bfloat16), values).astype(jnp.bfloat16)


def attend(offset, query, key_value):
    count, places = query.shape[0], key_value.shape[0]
    work = count * places * HEAD_SIZE * QUERY_HEADS
    return pl.pallas_call(
        functools.partial(attend_kernel, min(count, 256)),
        grid=(KEY_VALUE_HEADS,),
        in_specs=[
            pl.BlockSpec(memory_space=pltpu.SMEM),
            pl.BlockSpec((count, GROUP * HEAD_SIZE), lambda g: (0, g)),
            pl.BlockSpec((places, HEAD_SIZE), lambda g: (0, g)),
            pl.BlockSpec((places, HEAD_SIZE), lambda g: (0, KEY_VALUE_HEADS + g)),
        ],
        out_specs=pl.BlockSpec((count, GROUP * HEAD_SIZE), lambda g: (0, g)),
        out_shape=jax.ShapeDtypeStruct(query.shape, jnp.bfloat16),
        compiler_params=kernel_params(),
        cost_estimate=cost(4 * work, 4 * query.size + 2 * key_value.size, work // HEAD_SIZE),
        name="attend",
    )(offset, query, key_value, key_value)


def attend_back_kernel(
    tile,
    offset_ref,
    query_ref,
    key_ref,
    value_ref,
    grad_ref,
    cos_ref,
    sin_ref,
    key_cos_ref,
    key_sin_ref,
    query_out,
    key_out,
    value_out,
):
    scale = HEAD_SIZE ** (-0.5)
    keys, values = key_ref[...], value_ref[...]
    key_sum = jnp.zeros(keys.shape, jnp.float32)
    value_sum = jnp.zeros(values.shape, jnp.float32)
    for head in range(GROUP):
        lanes = slice(head * HEAD_SIZE, (head + 1) * HEAD_SIZE)
        for start in range(0, query_ref.shape[0], tile):
            rows = slice(start, start + tile)
            query, grad = query_ref[rows, lanes], grad_ref[rows, lanes]
            probs = attend_probs(offset_ref[0], start, query, keys)
            grad_probs = dot_t(grad, values)
            delta = jnp.sum(probs * grad_probs, axis=1, keepdims=True)
            grad_scores = (probs * (grad_probs - delta)).astype(jnp.bfloat16)
            query_grad = dot32(grad_scores, keys) * scale
            query_out[rows, lanes] = turn(
                query_grad, cos_ref[rows, :], -sin_ref[rows, :]
            ).astype(jnp.bfloat16)
            key_sum = key_sum + t_dot(grad_scores, query)
            value_sum = value_sum + t_dot(probs.astype(jnp.bfloat16), grad)
    key_out[...] = turn(key_sum * scale, key_cos_ref[...], -key_sin_ref[...])
    value_out[...] = value_sum


def attend_back(offset, query, key_value, grad, tables, key_tables):
    count, places = query.shape[0], key_value.shape[0]
    work = count * places * HEAD_SIZE * QUERY_HEADS
    heads = pl.BlockSpec((count, GROUP * HEAD_SIZE), lambda g: (0, g))
    table = pl.BlockSpec((count, HEAD_SIZE), lambda g: (0, 0))
    key_table = pl.BlockSpec((places, HEAD_SIZE), lambda g: (0, 0))
    key_heads = pl.BlockSpec((places, HEAD_SIZE), lambda g: (0, g))
    return pl.pallas_call(
        functools.partial(attend_back_kernel, min(count, 256)),
        grid=(KEY_VALUE_HEADS,),
        in_specs=[
            pl.BlockSpec(memory_space=pltpu.SMEM),
            heads,
            key_heads,
            pl.BlockSpec((places, HEAD_SIZE), lambda g: (0, KEY_VALUE_HEADS + g)),
            heads,
            table,
            table,
            key_table,
            key_table,
        ],
        out_specs=[heads, key_heads, key_heads],
        out_shape=[
            jax.ShapeDtypeStruct(query.shape, jnp.bfloat16),
            jax.ShapeDtypeStruct((places, KEY_WIDTH), jnp.float32),
            jax.ShapeDtypeStruct((places, KEY_WIDTH), jnp.float32),
        ],
        compiler_params=kernel_params(),
        cost_estimate=cost(
            10 * work, 6 * query.size + 6 * key_value.size, work // HEAD_SIZE
        ),
        name="attend_back",
    )(offset, query, key_value, key_value, grad, *tables, *key_tables)


def combine_kernel(scaled, unit_ref, info_ref, rows_ref, act_ref, weight_ref, *rest):
    *added_refs, out_ref = rest
    slot = info_ref[0, :, 0:1]
    capacity = rows_ref.shape[1]
    lanes = lax.broadcasted_iota(jnp.int32, (slot.shape[0], capacity), 1).astype(jnp.float32)
    pick = jnp.where(slot == lanes, 1.0, 0.0).astype(jnp.bfloat16)
    total = dot32(pick, rows_ref[0])
    if scaled:
        total = total * info_ref[0, :, 1:2]
    total = total + dot32(act_ref[0], weight_ref[...])
    for added in added_refs:
        total = total + added[0].astype(jnp.float32)
    out_ref[0] = total.astype(out_ref.dtype)


def combine(units, info, rows, act, weight, scaled, added=(), out_dtype=jnp.bfloat16):
    count = units.shape[0]
    half, width = info.shape[1], rows.shape[2]
    columns = width // 2
    hidden = act.shape[2]
    in_specs = [
        pl.BlockSpec((1, half, info.shape[2]), lambda j, i, u: (u[i], 0, 0)),
        pl.BlockSpec((1, rows.shape[1], columns), lambda j, i, u: (u[i] // 2, 0, j)),
        pl.BlockSpec((1, half, hidden), lambda j, i, u: (u[i], 0, 0)),
        pl.BlockSpec((hidden, columns), lambda j, i, u: (0, j)),
    ]
    for _, at in added:
        in_specs.append(pl.BlockSpec((1, half, columns), lambda j, i, u, at=at: (at + i, 0, j)))
    return pl.pallas_call(
        functools.partial(combine_kernel, scaled),
        grid_spec=pltpu.PrefetchScalarGridSpec(
            num_scalar_prefetch=1,
            grid=(2, count),
            in_specs=in_specs,
            out_specs=pl.BlockSpec((1, half, columns), lambda j, i, u: (i, 0, j)),
        ),
        out_shape=jax.ShapeDtypeStruct((count, half, width), out_dtype),
        compiler_params=kernel_params(),
        cost_estimate=cost(
            2 * count * half * width * (rows.shape[1] + hidden),
            2 * count * width * (rows.shape[1] + half * (1 + len(added))),
        ),
        name="combine",
    )(units, info, rows, act, weight, *[array for array, _ in added])


def exp_ring(chips):
    if chips % 2:
        return list(range(chips))
    return list(range(0, chips, 2)) + list(range(chips - 1, 0, -2))


def exp_sum_scatter(make, final, pieces=()):
    exp_count = lax.axis_size("exp")
    chips = exp_count // 2
    ring = exp_ring(chips)
    place_of = np.argsort(np.array(ring)).astype(np.int32)
    index = lax.axis_index("exp")
    core = index % 2
    place = jnp.asarray(place_of)[index // 2]
    ring_array = jnp.asarray(np.array(ring, np.int32))

    def unit(at, of_core, half):
        return ((ring_array[at % chips] * 2 + of_core) * 2 + half).astype(jnp.int32)

    def both_units(step, of_core):
        return [unit(place - step + chips, of_core, 0), unit(place + step, of_core, 1)]

    swap = [(i, i ^ 1) for i in range(exp_count)]
    onward, backward = [], []
    for at in range(chips):
        for of_core in range(2):
            here, there = ring[at] * 2 + of_core, ring[(at + 1) % chips] * 2 + of_core
            onward.append((here, there))
            backward.append((there, here))
    early = 2
    groups = [range(1, early + 1), range(early + 1, chips + 1)]
    partner = []
    for steps in groups:
        units = jnp.stack([u for step in steps for u in both_units(step, 1 - core)])
        sent = lax.ppermute(make(units, ()), "exp", swap)
        partner += [(sent, 2 * i + half) for i in range(len(steps)) for half in range(2)]
    arrived = [(), ()]
    done = []
    for step in range(1, chips + 1):
        units = both_units(step, core)
        totals = []
        for half in range(2):
            added = arrived[half] + (partner[2 * (step - 1) + half],)
            if step < chips:
                totals.append(make(units[half][None], added))
            else:
                totals.append(final(half, units[half][None], added))
        if step == chips:
            return jnp.concatenate(totals, axis=0), done
        if step <= len(pieces):
            operands, work = pieces[step - 1]
            totals[0], totals[1], operands = tie(totals[0], totals[1], operands(done))
        moved = [lax.ppermute(totals[0], "exp", onward), lax.ppermute(totals[1], "exp", backward)]
        if step <= len(pieces):
            moved[0], moved[1], result = tie(moved[0], moved[1], work(*operands))
            done.append(result)
        arrived = [((moved[0], 0),), ((moved[1], 0),)]


def ctx_gather(part, axis):
    if lax.axis_size("ctx") != 2:
        return lax.all_gather(part, "ctx", axis=axis, tiled=True)
    other = lax.ppermute(part, "ctx", [(0, 1), (1, 0)])
    first = lax.axis_index("ctx") == 0
    return jnp.concatenate(
        [jnp.where(first, part, other), jnp.where(first, other, part)], axis=axis
    )


def ctx_cut(left, right, axis, part):
    if lax.axis_size("ctx") == 2:
        size = (left, right)[axis].shape[1] // 2
        if axis == 0:
            left = lax.dynamic_slice_in_dim(left, part * size, size, axis=1)
        else:
            right = lax.dynamic_slice_in_dim(right, part * size, size, axis=1)
    return t_dot(left, right)


def ctx_theirs(axis):
    return lambda left, right: ctx_cut(left, right, axis, 1 - lax.axis_index("ctx")).astype(
        jnp.bfloat16
    )


def ctx_send(theirs, axis):
    if lax.axis_size("ctx") == 2:
        return lax.ppermute(theirs, "ctx", [(0, 1), (1, 0)])
    return lax.psum_scatter(theirs, "ctx", scatter_dimension=axis, tiled=True)


def ctx_total(axis):
    def total(left, right, arrived):
        if lax.axis_size("ctx") == 2:
            return ctx_cut(left, right, axis, lax.axis_index("ctx")) + arrived.astype(jnp.float32)
        return arrived.astype(jnp.float32)

    return total


def on_device(
    block_input,
    attn_gain,
    query_weight,
    key_matrix,
    value_matrix,
    output_weight,
    ffn_gain,
    shared_gate,
    shared_up,
    shared_down,
    expert_gate,
    expert_up,
    expert_down,
    routes,
    route_weights,
    cotangent,
):
    input_rows = block_input[0].astype(jnp.float32)
    tokens = input_rows.shape[0]
    ctx_count = lax.axis_size("ctx")
    exp_count = lax.axis_size("exp")
    exp_index = lax.axis_index("exp")
    both = ("ctx", "exp")
    offset = lax.axis_index("ctx") * tokens
    offset_array = jnp.full((1,), offset, jnp.int32)
    tables = rope_tables(offset + jnp.arange(tokens, dtype=jnp.int32))
    key_tables = rope_tables(jnp.arange(ctx_count * tokens, dtype=jnp.int32))

    attn_in = jnp.concatenate([query_weight, key_matrix, value_matrix], axis=1)
    full_in = lax.all_gather(attn_in, both, axis=0, tiled=True)
    routing = lax.all_gather(
        jnp.concatenate([routes[0].T.astype(jnp.float32), route_weights[0].T], axis=0),
        "exp",
        axis=0,
    )
    grad_low = cotangent[0]

    own_rows = shared_gate.shape[0]
    own_hidden = shared_down.shape[0]
    shared_columns = ctx_count * own_hidden
    shared_in = jnp.stack([shared_gate, shared_up]).reshape(
        2, own_rows, ctx_count, exp_count, own_hidden
    )
    shared_in = jnp.transpose(shared_in, (3, 1, 0, 2, 4)).reshape(
        exp_count, own_rows, 2 * shared_columns
    )
    shared_in = lax.all_to_all(shared_in, "exp", split_axis=0, concat_axis=0, tiled=True)
    shared_in = ctx_gather(shared_in.reshape(exp_count * own_rows, 2 * shared_columns), 0)
    shared_in_t = shared_in.T
    shared_out_w = ctx_gather(shared_down, 0)

    gate_w = ctx_gather(expert_gate[0], 0)
    gate_w, up_part = tie(gate_w, expert_up[0])
    up_w = ctx_gather(up_part, 0)
    up_w, down_part = tie(up_w, expert_down[0])
    down_w = ctx_gather(down_part, 1)

    capacity = tokens * TOP * 4 // (3 * exp_count)
    named = routing[:, :TOP] == exp_index.astype(jnp.float32)
    chosen = jnp.any(named, axis=1)
    token_weight = jnp.sum(jnp.where(named, routing[:, TOP:], 0.0), axis=1)
    upto = (jnp.arange(tokens)[:, None] <= jnp.arange(tokens)[None, :]).astype(jnp.bfloat16)
    slot = dot32(chosen.astype(jnp.bfloat16), upto).astype(jnp.int32) - 1
    slot = jnp.where(chosen, slot, -1)
    match = slot[:, None, :] == jnp.arange(capacity, dtype=jnp.int32)[None, :, None]
    pick = match.astype(jnp.bfloat16)
    slot_weight = jnp.sum(jnp.where(match, token_weight[:, None, :], 0.0), axis=2)
    token_info = jnp.pad(
        jnp.stack([slot.astype(jnp.float32), token_weight], axis=2), ((0, 0), (0, 0), (0, 126))
    ).reshape(2 * exp_count, tokens // 2, 128)

    inverse_one = rms_scale(input_rows)
    normed_one = (input_rows * inverse_one * attn_gain).astype(jnp.bfloat16)
    full_in, normed_one, pick, slot_weight, token_info, shared_in, shared_in_t, shared_out_w, gate_w = tie(
        full_in,
        normed_one,
        pick,
        slot_weight,
        token_info,
        shared_in,
        shared_in_t,
        shared_out_w,
        gate_w,
    )
    output_weight, full_in = tie(output_weight, full_in)
    full_output = lax.all_gather(output_weight, both, axis=0, tiled=True)
    key_value = ctx_gather(
        project(normed_one, full_in, tables, QUERY_HEADS // KEY_VALUE_HEADS, 2, 1), 0
    )
    query = project(normed_one, full_in, tables, 0, QUERY_HEADS // KEY_VALUE_HEADS, QUERY_HEADS)
    attended_low = attend(offset_array, query, key_value)
    full_output, up_w = tie(full_output, up_w)
    middle = input_rows + dot32(attended_low, full_output)
    inverse_two = rms_scale(middle)
    normed_two = (middle * inverse_two * ffn_gain).astype(jnp.bfloat16)

    rows_all = lax.all_gather(normed_two, "exp", axis=0, tiled=True)
    rows_all, down_w, grad_low = tie(rows_all, down_w, grad_low)
    grad_all = lax.all_gather(grad_low, "exp", axis=0, tiled=True)

    def to_slots(rows):
        return jnp.einsum(
            "sct,std->scd",
            pick,
            rows.reshape(exp_count, tokens, MODEL_WIDTH),
            preferred_element_type=jnp.float32,
        )

    received = to_slots(rows_all).astype(jnp.bfloat16).reshape(exp_count * capacity, MODEL_WIDTH)

    expert_g = dot32(received, gate_w)
    expert_u = dot32(received, up_w)
    expert_act = (jax.nn.silu(expert_g) * expert_u).astype(jnp.bfloat16)
    shared_gu = dot32(rows_all, shared_in)
    shared_g = shared_gu[:, :shared_columns]
    shared_u = shared_gu[:, shared_columns:]
    shared_act = (jax.nn.silu(shared_g) * shared_u).astype(jnp.bfloat16)
    expert_rows = dot32(expert_act, down_w).astype(jnp.bfloat16)

    units_all = 2 * exp_count
    half_tokens = tokens // 2

    def slots(rows):
        return rows.reshape(exp_count, capacity, MODEL_WIDTH)

    def halves(rows):
        return rows.reshape(units_all, half_tokens, rows.shape[1])

    pair = exp_count >= 4 and exp_count % 4 == 0 and ctx_count == 2

    def sum_over_exp(part, pieces, out_dtype, own=None):
        if pair:
            return exp_sum_scatter(
                lambda units, added: part(units, added=added),
                lambda half, units, added: part(
                    units,
                    added=added + (() if own is None else ((own, half),)),
                    out_dtype=out_dtype,
                ),
                pieces,
            )
        everything = part(jnp.arange(units_all, dtype=jnp.int32))
        summed = lax.psum_scatter(
            everything.reshape(exp_count * tokens, MODEL_WIDTH),
            "exp",
            scatter_dimension=0,
            tiled=True,
        ).astype(jnp.float32)
        if own is not None:
            summed = summed + own.reshape(tokens, MODEL_WIDTH)
        done = []
        for operands, work in pieces:
            done.append(work(*operands(done)))
        return summed.astype(out_dtype), done

    def back_rows(rows, weight):
        return (
            (to_slots(rows) * weight[:, :, None])
            .astype(jnp.bfloat16)
            .reshape(exp_count * capacity, MODEL_WIDTH)
        )

    def back_act(rows, weight):
        return silu_back(dot_t(rows, weight), expert_g, expert_u)

    def back_shared(rows, weight):
        return jnp.concatenate(silu_back(dot_t(rows, weight), shared_g, shared_u), axis=1)

    def back_up(earlier, rows, weight):
        return (earlier + dot_t(rows, weight)).astype(jnp.bfloat16)

    out_part = functools.partial(
        combine,
        info=token_info,
        rows=slots(expert_rows),
        act=halves(shared_act),
        weight=shared_out_w,
        scaled=True,
    )
    output, done = sum_over_exp(
        out_part,
        [
            (lambda done: (grad_all, slot_weight), back_rows),
            (lambda done: (done[0], down_w), back_act),
            (lambda done: (grad_all, shared_out_w), back_shared),
            (lambda done: (done[1][0], gate_w), dot_t),
            (lambda done: (done[3], done[1][1], up_w), back_up),
        ],
        jnp.bfloat16,
        middle.reshape(2, half_tokens, MODEL_WIDTH),
    )
    output = output.reshape(tokens, MODEL_WIDTH)
    grad_expert, (grad_eg, grad_eu), shared_back, _, grad_rows = done

    grad_part = functools.partial(
        combine,
        info=token_info,
        rows=slots(grad_rows),
        act=halves(shared_back),
        weight=shared_in_t,
        scaled=False,
    )
    sent = {}

    def arrival(name, theirs, axis):
        if name not in sent:
            sent[name] = ctx_send(theirs, axis)
        return sent[name]

    grad_two, done = sum_over_exp(
        grad_part,
        [
            (lambda done: (received, grad_eg), ctx_theirs(0)),
            (lambda done: (received, grad_eu), ctx_theirs(0)),
            (lambda done: (expert_act, grad_expert), ctx_theirs(1)),
            (
                lambda done: (rows_all, shared_back, shared_act, grad_all),
                lambda a, b, c, d: (ctx_theirs(0)(a, b), ctx_theirs(0)(c, d)),
            ),
            (
                lambda done: (received, grad_eg, arrival("gate", done[0], 0)),
                ctx_total(0),
            ),
            (lambda done: (), lambda: ()),
            (
                lambda done: (received, grad_eu, arrival("up", done[1], 0)),
                ctx_total(0),
            ),
        ],
        jnp.float32,
    )
    grad_two = grad_two.reshape(tokens, MODEL_WIDTH)
    expert_gate_grad = done[4][None]
    expert_up_grad = done[6][None]

    ffn_gain_term = jnp.sum(grad_two * middle * inverse_two, axis=0)
    gain_term = jnp.pad(ffn_gain_term[:, None], ((0, 0), (0, 127))).astype(jnp.bfloat16)
    grad_middle = grad_low.astype(jnp.float32) + norm_back(grad_two, middle, inverse_two, ffn_gain)
    grad_middle_low = grad_middle.astype(jnp.bfloat16)
    attended_gradient = dot_t(grad_middle_low, full_output).astype(jnp.bfloat16)
    output_term = t_dot(grad_middle_low, attended_low).astype(jnp.bfloat16)
    sum_o = lax.psum_scatter(output_term, both, scatter_dimension=0, tiled=True)

    grad_query_raw, key_terms, value_terms = attend_back(
        offset_array, query, key_value, attended_gradient, tables, key_tables
    )
    key_value_grad = jnp.concatenate([key_terms, value_terms], axis=1)
    if ctx_count == 2:
        own = lax.dynamic_slice_in_dim(key_value_grad, offset, tokens, axis=0)
        other = lax.dynamic_slice_in_dim(key_value_grad, tokens - offset, tokens, axis=0)
        key_value_raw = own + ctx_send(other.astype(jnp.bfloat16), 0).astype(jnp.float32)
    else:
        key_value_raw = ctx_send(key_value_grad.astype(jnp.bfloat16), 0)
    key_value_raw = key_value_raw.astype(jnp.bfloat16)
    grad_raw = jnp.concatenate([grad_query_raw, key_value_raw], axis=1)
    in_term = t_dot(normed_one, grad_raw).astype(jnp.bfloat16)
    grad_one = dot_t(grad_raw, full_in)
    input_grad = grad_middle + norm_back(grad_one, input_rows, inverse_one, attn_gain)
    edge = QUERY_WIDTH + 2 * KEY_WIDTH
    sum_in = lax.psum_scatter(
        jnp.concatenate([in_term, gain_term], axis=1), both, scatter_dimension=0, tiled=True
    ).astype(jnp.float32)
    own_gain = lax.dynamic_slice_in_dim(
        attn_gain, (lax.axis_index("ctx") * exp_count + exp_index) * own_rows, own_rows
    )
    attn_gain_grad = jnp.sum(sum_in[:, :edge] * attn_in.astype(jnp.float32), axis=1) / own_gain

    expert_down_grad = ctx_total(1)(expert_act, grad_expert, arrival("down", done[2], 1))[None]
    sum_sd = ctx_total(0)(shared_act, grad_all, arrival("shared_down", done[3][1], 0))
    shared_in_grad = ctx_total(0)(
        rows_all, shared_back, arrival("shared_in", done[3][0], 0)
    ).astype(jnp.bfloat16)
    shared_in_grad = lax.all_to_all(
        shared_in_grad.reshape(exp_count, own_rows, 2 * shared_columns),
        "exp",
        split_axis=0,
        concat_axis=0,
        tiled=True,
    ).reshape(exp_count, own_rows, 2, ctx_count, own_hidden)
    shared_in_grad = (
        jnp.transpose(shared_in_grad, (2, 1, 3, 0, 4))
        .reshape(2, own_rows, exp_count * shared_columns)
        .astype(jnp.float32)
    )
    return (
        output[None],
        input_grad[None],
        attn_gain_grad,
        sum_in[:, :QUERY_WIDTH],
        sum_in[:, QUERY_WIDTH : QUERY_WIDTH + KEY_WIDTH],
        sum_in[:, QUERY_WIDTH + KEY_WIDTH : edge],
        sum_o.astype(jnp.float32).T,
        sum_in[:, edge],
        shared_in_grad[0],
        shared_in_grad[1],
        sum_sd,
        expert_gate_grad,
        expert_up_grad,
        expert_down_grad,
    )


def solution(mesh):
    return jax.shard_map(
        on_device,
        mesh=mesh,
        in_specs=(
            P("exp", "ctx", None),
            P(),
            P(("ctx", "exp"), None),
            P(("ctx", "exp"), None),
            P(("ctx", "exp"), None),
            P(("ctx", "exp"), None),
            P(),
            P(("ctx", "exp"), None),
            P(("ctx", "exp"), None),
            P(("ctx", "exp"), None),
            P("exp", "ctx", None),
            P("exp", "ctx", None),
            P("exp", None, "ctx"),
            P("exp", "ctx", None),
            P("exp", "ctx", None),
            P("exp", "ctx", None),
        ),
        out_specs=(
            P("exp", "ctx", None),
            P("exp", "ctx", None),
            P(("ctx", "exp")),
            P(("ctx", "exp"), None),
            P(("ctx", "exp"), None),
            P(("ctx", "exp"), None),
            P(None, ("ctx", "exp")),
            P(("ctx", "exp")),
            P(("ctx", "exp"), None),
            P(("ctx", "exp"), None),
            P(("ctx", "exp"), None),
            P("exp", "ctx", None),
            P("exp", "ctx", None),
            P("exp", None, "ctx"),
        ),
        check_vma=False,
    )
```

time: 4820 us -> 2030 us (0.42)
  waiting for transfers between devices: 2970 us -> 712 us
  Pallas kernels: 0 us -> 313 us
  local copies, waits for them, and re-layouts: 382 us -> 75.7 us
  starting transfers between devices: 311 us -> 66.2 us
  matrix products: 773 us -> 632 us
  blocking collectives: 171 us -> 38.6 us
    reduce_scatter x12 -> x2, waiting for transfers between devices: 1310 us -> 0.01 us  [the longest x1 0.01 us: on_device(): sum_o = lax.psum_scatter(output_term, both, scatter_dimension=0, tiled=True)]
    all_to_all x4 -> x2, waiting for transfers between devices: 1050 us -> 0.01 us  [the longest x1 0.01 us: on_device(): lax.all_to_all(shared_in, 'exp', split_axis=0, concat_axis=0, tiled=True)]
    ppermute x0 -> x44, waiting for transfers between devices: none -> 601 us  [the longest x6 299 us: ctx_gather(): other = lax.ppermute(part, 'ctx', [(0, 1), (1, 0)])]
    all_gather x12 -> x4, waiting for transfers between devices: 607 us -> 110 us  [the longest x1 110 us: on_device(): rows_all = lax.all_gather(normed_two, 'exp', axis=0, tiled=True)]
    pallas_call x0 -> x40, Pallas kernels: none -> 313 us  [the longest x36 216 us: combine(): pl.pallas_call(functools.partial(combine_kernel, scaled), grid_spec=pltpu...]
    all_to_all x4 -> x2, starting transfers between devices: 310 us -> 20.3 us  [the longest x1 12.9 us: on_device(): lax.all_to_all(shared_in_grad.reshape(exp_count, own_rows, 2 * shared_col...]
    unnamed x1 -> x0, blocking collectives: 171 us -> none
    dot_general x42 -> x26, matrix products: 773 us -> 632 us  [the longest x12 239 us: t_dot(): lax.dot_general(left, right, (((0,), (0,)), ((), ())), preferred_element_...]
  transfers between devices with their start and end apart: 28 -> 52, of which waited for: 16 -> 27; matrix products, arithmetic and copies ran while one was open for 20% -> 40% of each run, Pallas kernels for 0% -> 12%
where the time goes in v1:
time: 2030 us; the launch traced here: 2020 us
  waiting for transfers between devices  712 us (35%)
  matrix products  632 us (31%)
  Pallas kernels  313 us (15%)
  other arithmetic  151 us (7%)
  local copies, waits for them, and re-layouts  75.7 us (4%)
  starting transfers between devices  66.2 us (3%)
  blocking collectives  38.6 us (2%)
  between operations  28.1 us (1%)
    ppermute x6, waiting for transfers between devices, ctx_gather(): other = lax.ppermute(part, 'ctx', [(0, 1), (1, 0)])  299 us
    dot_general x12, matrix products, t_dot(): lax.dot_general(left, right, (((0,), (0,)), ((), ())), preferred_element_...  239 us
    pallas_call x36, Pallas kernels, combine(): pl.pallas_call(functools.partial(combine_kernel, scaled), grid_spec=pltpu...  216 us
    dot_general x6, matrix products, dot_t(): lax.dot_general(left, right, (((1,), (1,)), ((), ())), preferred_element_...  182 us
    ppermute x6, waiting for transfers between devices, ctx_send(): return lax.ppermute(theirs, 'ctx', [(0, 1), (1, 0)])  171 us
    dot_general x6, matrix products, dot32(): return jnp.dot(left, right, preferred_element_type=jnp.float32)  161 us
    all_gather x1, waiting for transfers between devices, on_device(): rows_all = lax.all_gather(normed_two, 'exp', axis=0, tiled=True)  110 us
    ppermute x14, waiting for transfers between devices, exp_sum_scatter(): lax.ppermute(totals[0], 'exp', onward)  105 us
  transfers between devices with their start and end apart: 52, of which 27 were waited for; matrix products, arithmetic and copies ran while one was open for 40% of the time, Pallas kernels for 12%

profile of v1, /device:TPU:0, one launch (start us, length us, event | category | flops | bytes accessed | tf_op | source)
XLA Modules:
  0.0 2016.5 jit_solution(16702304533208751964)
XLA Ops:
  34.6 38.6 %all-gather.1 = f32[16,12,512]{2,1,0:T(8,128)S(1)} all-gather(f32[1,12,512]{2,1,0:T(8,128)S(1)} %maximum_bitcast_fusion.1), channel_id=2, replica_groups=mesh['ctx'=2,'exp'=16] {'exp'}, dimensions={0}, use_global_device_ids=true | all-gather | bytes 417792 | tf_op jit(solution)/shard_map/all_gather | solution.py:411
  93.4 78.7 %collective-permute-done.1 = bf16[96,2560]{1,0:T(8,128)(2,1)} collective-permute-done((bf16[96,2560]{1,0:T(8,128)(2,1)}, bf16[96,2560]{1,0:T(8,128)(2,1)}, u32[]{:S(2)}, u32[]{:S(2)}) %collective-permute-start.1) | collective-permute-done | bytes 491552 | tf_op jit(solution)/shard_map/ppermute | solution.py:342
  212.6 115.3 %collective-permute-done.4 = bf16[1280,1536]{1,0:T(8,128)(2,1)} collective-permute-done((bf16[1280,1536]{1,0:T(8,128)(2,1)}, bf16[1280,1536]{1,0:T(8,128)(2,1)}, u32[]{:S(2)}, u32[]{:S(2)}) %collective-permute-start.4) | collective-permute-done | bytes 3932192 | tf_op jit(solution)/shard_map/ppermute | solution.py:342
  368.3 28.9 %attend.1 = bf16[512,2560]{1,0:T(8,128)(2,1)} custom-call(s32[1]{0:T(128)} %bitcast.17.offset_ref, bf16[512,2560]{1,0:T(8,128)(2,1)} %project.2.query_ref, bf16[1024,1024]{1,0:T(8,128)(2,1)} %pad_maximum_fusion.9.key_ref.value_ref, bf16[1024,1024]{1,0:T(8,128)(2,1)} %pad_maximum_fusion.9.key_ref.value_ref), custom_call_target="tpu_custom_call" | custom-call | flops 5368709120 | bytes 7340032 | tf_op jit(solution)/shard_map/attend/pallas_call | solution.py:144
  414.4 83.6 %collective-permute-done.5 = bf16[1536,1280]{1,0:T(8,128)(2,1)S(1)} collective-permute-done((bf16[1536,1280]{1,0:T(8,128)(2,1)}, bf16[1536,1280]{1,0:T(8,128)(2,1)S(1)}, u32[]{:S(2)}, u32[]{:S(2)}) %collective-permute-start.5) | collective-permute-done | bytes 3932192 | tf_op jit(solution)/shard_map/ppermute | solution.py:342
  510.3 110.4 %all-gather.11.cloned.1.call-done = bf16[8192,2560]{1,0:T(8,128)(2,1)} async-done(((bf16[512,2560]{1,0:T(8,128)(2,1)}), bf16[8192,2560]{1,0:T(8,128)(2,1)}) %all-gather.11.cloned.1.call-update) | async-done | bytes 41943056 | tf_op jit(solution)/shard_map/all_gather | solution.py:477
  636.3 26.6 %fusion.88 = f32[8192,384]{0,1:T(8,128)} fusion(bf16[8192,2560]{1,0:T(8,128)(2,1)} %all-gather.11.cloned.1.call-done, bf16[2560,384]{0,1:T(8,128)(2,1)S(1)} %copy-done.19), kind=kOutput, calls=%fused_computation.162 | convolution fusion | flops 16106127360 | bytes 56492032 | tf_op jit(solution)/shard_map/dot_general | solution.py:57
  672.9 26.3 %convolution_convert_fusion.2 = bf16[16,256,2560]{2,1,0:T(8,128)(2,1)} fusion(bf16[16,256,512]{2,1,0:T(8,128)(2,1)} %fusion.30, bf16[16,512,2560]{2,1,0:T(8,128)(2,1)} %bitcast.263), kind=kOutput, calls=%fused_computation.14 | convolution fusion | flops 10747904000 | bytes 67108864 | tf_op jit(solution)/shard_map/sct,std->scd/dot_general | solution.py:482
  699.2 41.3 %fusion.87 = f32[4096,1536]{1,0:T(8,128)} fusion(bf16[4096,2560]{1,0:T(8,128)(2,1)} %bitcast.264, bf16[2560,1536]{1,0:T(8,128)(2,1)} %pad_maximum_fusion), kind=kOutput, calls=%fused_computation.161 | convolution fusion | flops 32212254720 | bytes 54001664 | tf_op jit(solution)/shard_map/dot_general | solution.py:57
  740.5 44.2 %multiply_convert_fusion.3 = (bf16[4096,1536]{1,0:T(8,128)(2,1)}, f32[4096,1536]{1,0:T(8,128)}) fusion(f32[4096,1536]{1,0:T(8,128)} %fusion.87, bf16[4096,2560]{1,0:T(8,128)(2,1)} %bitcast.265, bf16[2560,1536]{1,0:T(8,128)(2,1)} %pad_maximum_fusion.1), kind=kOutput, calls=%fused_computation.6 | convolution fusion | flops 32250003456 | bytes 91750400 | tf_op jit(solution)/shard_map/dot_general | solution.py:57
  784.7 37.2 %convolution_convert_fusion = bf16[4096,2560]{1,0:T(8,128)(2,1)} fusion(bf16[4096,1536]{1,0:T(8,128)(2,1)} %get-tuple-element.196, bf16[1536,2560]{1,0:T(8,128)(2,1)S(1)} %bitcast.274), kind=kOutput, calls=%fused_computation.8 | convolution fusion | flops 32222740480 | bytes 41418752 | tf_op jit(solution)/shard_map/dot_general | solution.py:57
  832.6 25.8 %combine.41 = bf16[12,256,2560]{2,1,0:T(8,128)(2,1)} custom-call(s32[12]{0:T(128)} %stack.149.unit_ref, f32[32,256,128]{2,1,0:T(8,128)} %bitcast.187, bf16[16,256,2560]{2,1,0:T(8,128)(2,1)} %bitcast.169, bf16[32,256,192]{2,1,0:T(8,128)(2,1)} %bitcast.241, bf16[192,2560]{1,0:T(8,128)(2,1)} %pad_maximum_fusion.11.weight_ref), custom_call_target="tpu_custom_call" | custom-call | flops 7046430720 | bytes 31457280 | tf_op jit(solution)/shard_map/combine/pallas_call | solution.py:262
  910.0 47.7 %multiply_convert_fusion.1 = (bf16[4096,1536]{1,0:T(8,128)(2,1)}, bf16[4096,1536]{1,0:T(8,128)(2,1)}) fusion(f32[4096,1536]{1,0:T(8,128)} %fusion.87, f32[4096,1536]{1,0:T(8,128)} %get-tuple-element.284, bf16[4096,2560]{1,0:T(8,128)(2,1)} %bitcast.283, bf16[1536,2560]{1,0:T(8,128)(2,1)} %pad_maximum_fusion.2), kind=kOutput, calls=%fused_computation.4 | convolution fusion | flops 32294043648 | bytes 104333312 | tf_op jit(solution)/shard_map/dot_general | solution.py:61
  1008.3 41.4 %fusion.89 = f32[4096,2560]{1,0:T(8,128)} fusion(bf16[4096,1536]{1,0:T(8,128)(2,1)} %get-tuple-element.212, bf16[2560,1536]{1,0:T(8,128)(2,1)} %pad_maximum_fusion), kind=kOutput, calls=%fused_computation.163 | convolution fusion | flops 32212254720 | bytes 62390272 | tf_op jit(solution)/shard_map/dot_general | solution.py:61
  1069.0 41.5 %fusion.90 = f32[4096,2560]{1,0:T(8,128)} fusion(bf16[4096,1536]{1,0:T(8,128)(2,1)} %get-tuple-element.224, bf16[2560,1536]{1,0:T(8,128)(2,1)} %pad_maximum_fusion.1), kind=kOutput, calls=%fused_computation.164 | convolution fusion | flops 32212254720 | bytes 62390272 | tf_op jit(solution)/shard_map/dot_general | solution.py:61
  1110.6 34.3 %add_convert_fusion = bf16[4096,2560]{1,0:T(8,128)(2,1)} fusion(f32[4096,2560]{1,0:T(8,128)} %fusion.89, f32[4096,2560]{1,0:T(8,128)} %fusion.90), kind=kLoop, calls=%fused_computation | loop fusion | flops 20971520 | bytes 104857600 | tf_op jit(solution)/shard_map/convert_element_type | solution.py:550
  1144.9 28.3 %combine.59 = bf16[12,256,2560]{2,1,0:T(8,128)(2,1)} custom-call(s32[12]{0:T(128)} %stack.149.unit_ref, f32[32,256,128]{2,1,0:T(8,128)} %bitcast.198, bf16[16,256,2560]{2,1,0:T(8,128)(2,1)} %bitcast.150, bf16[32,256,384]{2,1,0:T(8,128)(2,1)} %bitcast.222, bf16[384,2560]{1,0:T(8,128)(2,1)} %get-tuple-element.181.weight_ref), custom_call_target="tpu_custom_call" | custom-call | flops 10066329600 | bytes 31457280 | tf_op jit(solution)/shard_map/combine/pallas_call | solution.py:262
  1457.9 24.5 %fusion.21 = f32[1280,1536]{1,0:T(8,128)} fusion(bf16[4096,1536]{1,0:T(8,128)(2,1)} %get-tuple-element.224, bf16[4096,2560]{1,0:T(8,128)(2,1)} %bitcast.269, s32[]{:T(128)S(6)} %select_n.450, bf16[1280,1536]{1,0:T(8,128)(2,1)} %collective-permute-done.37), kind=kOutput, calls=%fused_computation.35 | convolution fusion | flops 16110059520 | bytes 34865156 | tf_op jit(solution)/shard_map/dot_general | solution.py:67
  1528.9 48.4 %attend_back.1 = (bf16[512,2560]{1,0:T(8,128)(2,1)}, f32[1024,512]{1,0:T(8,128)}, f32[1024,512]{1,0:T(8,128)}) custom-call(s32[1]{0:T(128)} %bitcast.17.offset_ref, bf16[512,2560]{1,0:T(8,128)(2,1)} %project.2.query_ref, bf16[1024,1024]{1,0:T(8,128)(2,1)} %pad_maximum_fusion.9.key_ref.value_ref, bf16[1024,1024]{1,0:T(8,128)(2,1)} %pad_maximum_fusion.9.key_ref.value_ref, ...), custom_call_target="tpu_custom_call" | custom-call | flops 13421772800 | bytes 14155776 | tf_op jit(solution)/shard_map/attend_back/pallas_call | solution.py:206
  1585.0 38.0 %collective-permute-done.40 = bf16[512,1024]{1,0:T(8,128)(2,1)} collective-permute-done((bf16[512,1024]{1,0:T(8,128)(2,1)}, bf16[512,1024]{1,0:T(8,128)(2,1)}, u32[]{:S(2)}, u32[]{:S(2)}) %collective-permute-start.40) | collective-permute-done | bytes 1048608 | tf_op jit(solution)/shard_map/ppermute | solution.py:367
  1667.6 27.2 %collective-permute-done.18.rest_0_ = bf16[1,256,2560]{2,1,0:T(8,128)(2,1)S(1)} collective-permute-done((bf16[1,256,2560]{2,1,0:T(8,128)(2,1)}, bf16[1,256,2560]{2,1,0:T(8,128)(2,1)S(1)}, u32[]{:S(2)}, u32[]{:S(2)}) %collective-permute-start.18) | collective-permute-done | bytes 1310752 | tf_op jit(solution)/shard_map/ppermute | solution.py:332
  1726.2 34.1 %collective-permute-done.19.rest_0_ = bf16[1,256,2560]{2,1,0:T(8,128)(2,1)} collective-permute-done((bf16[1,256,2560]{2,1,0:T(8,128)(2,1)}, bf16[1,256,2560]{2,1,0:T(8,128)(2,1)}, u32[]{:S(2)}, u32[]{:S(2)}) %collective-permute-start.19) | collective-permute-done | bytes 1310752 | tf_op jit(solution)/shard_map/ppermute | solution.py:332
  1775.3 98.1 %collective-permute-done.42 = bf16[96,2560]{1,0:T(8,128)(2,1)S(1)} collective-permute-done((bf16[96,2560]{1,0:T(8,128)(2,1)S(1)}, bf16[96,2560]{1,0:T(8,128)(2,1)S(1)}, u32[]{:S(2)}, u32[]{:S(2)}) %collective-permute-start.42) | collective-permute-done | bytes 491552 | tf_op jit(solution)/shard_map/ppermute | solution.py:367
  1874.5 35.3 %collective-permute-done.41 = bf16[1280,384]{1,0:T(8,128)(2,1)S(1)} collective-permute-done((bf16[1280,384]{1,0:T(8,128)(2,1)S(1)}, bf16[1280,384]{1,0:T(8,128)(2,1)S(1)}, u32[]{:S(2)}, u32[]{:S(2)}) %collective-permute-start.41) | collective-permute-done | bytes 983072 | tf_op jit(solution)/shard_map/ppermute | solution.py:367
  (385 shorter events, 832.7 us)
Async XLA Ops:
  7.2 201.8 %all-gather.7.cloned.1.call-start = ((), (), s32[]{:S(2)}) async-start(), calls=%async_computation.4 | async-start | bytes 18923520 | tf_op jit(solution)/shard_map/all_gather | solution.py:410
  25.0 64.7 %all-to-all-start = ((bf16[16,80,384]{2,1,0:T(8,128)(2,1)}), bf16[16,80,384]{2,1,0:T(8,128)(2,1)}, u32[]{:S(2)}, u32[]{:S(2)}) async-start(bf16[16,80,384]{2,1,0:T(8,128)(2,1)} %reshape.182), calls=%async_computation | async-start | bytes 1966080 | tf_op jit(solution)/shard_map/all_to_all | solution.py:427
  32.4 364.8 %all-gather.9.cloned.1.call-start = ((), (), s32[]{:S(2)}) async-start(), calls=%async_computation.5 | async-start | bytes 13516800 | tf_op jit(solution)/shard_map/all_gather | solution.py:466
  32.5 163.6 %collective-permute-start.2 = (bf16[1280,1536]{1,0:T(8,128)(2,1)}, bf16[1280,1536]{1,0:T(8,128)(2,1)}, u32[]{:S(2)}, u32[]{:S(2)}) collective-permute-start(bf16[1280,1536]{1,0:T(8,128)(2,1)} %bitcast.275), channel_id=1, source_target_pairs={{0,16},{16,0},{1,17},{17,1},{2,18},{18,2},{3,19},{19,3},{4,20},{20... | collective-permute-start | bytes 11796488 | tf_op jit(solution)/shard_map/ppermute | solution.py:342
  34.1 138.0 %collective-permute-start.1 = (bf16[96,2560]{1,0:T(8,128)(2,1)}, bf16[96,2560]{1,0:T(8,128)(2,1)}, u32[]{:S(2)}, u32[]{:S(2)}) collective-permute-start(bf16[96,2560]{1,0:T(8,128)(2,1)} %param.29), channel_id=1, source_target_pairs={{0,16},{16,0},{1,17},{17,1},{2,18},{18,2},{3,19},{19,3},{4,20},{20... | collective-permute-start | bytes 1474568 | tf_op jit(solution)/shard_map/ppermute | solution.py:342
  91.9 100.6 %collective-permute-start = (bf16[1280,384]{0,1:T(8,128)(2,1)}, bf16[1280,384]{0,1:T(8,128)(2,1)S(1)}, u32[]{:S(2)}, u32[]{:S(2)}) collective-permute-start(bf16[1280,384]{0,1:T(8,128)(2,1)} %copy.56), channel_id=1, source_target_pairs={{0,16},{16,0},{1,17},{17,1},{2,18},{18,2},{3,19},{19,3},{4,20},{20... | collective-permute-start | bytes 2949128 | tf_op jit(solution)/shard_map/ppermute | solution.py:342
  209.0 411.7 %all-gather.11.cloned.1.call-start = ((), (), s32[]{:S(2)}) async-start(), calls=%async_computation.6 | async-start | bytes 44564480 | tf_op jit(solution)/shard_map/all_gather | solution.py:477
  209.0 118.9 %collective-permute-start.4 = (bf16[1280,1536]{1,0:T(8,128)(2,1)}, bf16[1280,1536]{1,0:T(8,128)(2,1)}, u32[]{:S(2)}, u32[]{:S(2)}) collective-permute-start(bf16[1280,1536]{1,0:T(8,128)(2,1)} %bitcast.276), channel_id=1, source_target_pairs={{0,16},{16,0},{1,17},{17,1},{2,18},{18,2},{3,19},{19,3},{4,20},{20... | collective-permute-start | bytes 11796488 | tf_op jit(solution)/shard_map/ppermute | solution.py:342
  412.9 453.4 %all-gather.13.cloned.1.call-start = ((), (), s32[]{:S(2)}) async-start(), calls=%async_computation.7 | async-start | bytes 44564480 | tf_op jit(solution)/shard_map/all_gather | solution.py:479
  413.0 85.0 %collective-permute-start.5 = (bf16[1536,1280]{1,0:T(8,128)(2,1)}, bf16[1536,1280]{1,0:T(8,128)(2,1)S(1)}, u32[]{:S(2)}, u32[]{:S(2)}) collective-permute-start(bf16[1536,1280]{1,0:T(8,128)(2,1)} %bitcast.278), channel_id=1, source_target_pairs={{0,16},{16,0},{1,17},{17,1},{2,18},{18,2},{3,19},{19,3},{4,20},{20... | collective-permute-start | bytes 11796488 | tf_op jit(solution)/shard_map/ppermute | solution.py:342
  620.7 1381.3 %reduce-scatter.5.cloned.1.call-start = ((), (), s32[]{:S(2)}) async-start(), calls=%async_computation.9 | async-start | bytes 13516800 | tf_op jit(solution)/shard_map/reduce_scatter | solution.py:622
  858.5 99.3 %collective-permute-start.11 = (bf16[12,256,2560]{2,1,0:T(8,128)(2,1)}, bf16[12,256,2560]{2,1,0:T(8,128)(2,1)}, u32[]{:S(2)}, u32[]{:S(2)}) collective-permute-start(bf16[12,256,2560]{2,1,0:T(8,128)(2,1)} %combine.41), channel_id=1, source_target_pairs={{0,1},{1,0},{2,3},{3,2},{4,5},{5,4},{6,7},{7,6},{8,9},{9,8},{10,11... | collective-permute-start | bytes 47185928 | tf_op jit(solution)/shard_map/ppermute | solution.py:314
  1006.3 52.1 %collective-permute-start.14 = (bf16[1,256,2560]{2,1,0:T(8,128)(2,1)}, bf16[1,256,2560]{2,1,0:T(8,128)(2,1)S(1)}, u32[]{:S(2)}, u32[]{:S(2)}) collective-permute-start(bf16[1,256,2560]{2,1,0:T(8,128)(2,1)} %combine.44), channel_id=1, source_target_pairs={{0,4},{1,5},{4,8},{5,9},{8,12},{9,13},{12,14},{13,15},{14,10},{15,... | collective-permute-start | bytes 3932168 | tf_op jit(solution)/shard_map/ppermute | solution.py:332
  1067.0 77.9 %collective-permute-start.16 = (bf16[1,256,2560]{2,1,0:T(8,128)(2,1)}, bf16[1,256,2560]{2,1,0:T(8,128)(2,1)S(1)}, u32[]{:S(2)}, u32[]{:S(2)}) collective-permute-start(bf16[1,256,2560]{2,1,0:T(8,128)(2,1)} %combine.46), channel_id=1, source_target_pairs={{0,4},{1,5},{4,8},{5,9},{8,12},{9,13},{12,14},{13,15},{14,10},{15,... | collective-permute-start | bytes 3932168 | tf_op jit(solution)/shard_map/ppermute | solution.py:332
  1068.5 76.4 %collective-permute-start.17 = (bf16[1,256,2560]{2,1,0:T(8,128)(2,1)}, bf16[1,256,2560]{2,1,0:T(8,128)(2,1)S(1)}, u32[]{:S(2)}, u32[]{:S(2)}) collective-permute-start(bf16[1,256,2560]{2,1,0:T(8,128)(2,1)} %combine.47), channel_id=1, source_target_pairs={{4,0},{5,1},{8,4},{9,5},{12,8},{13,9},{14,12},{15,13},{10,14},{11,... | collective-permute-start | bytes 3932168 | tf_op jit(solution)/shard_map/ppermute | solution.py:332
  1173.2 114.0 %collective-permute-start.27 = (bf16[12,256,2560]{2,1,0:T(8,128)(2,1)}, bf16[12,256,2560]{2,1,0:T(8,128)(2,1)}, u32[]{:S(2)}, u32[]{:S(2)}) collective-permute-start(bf16[12,256,2560]{2,1,0:T(8,128)(2,1)} %combine.59), channel_id=1, source_target_pairs={{0,1},{1,0},{2,3},{3,2},{4,5},{5,4},{6,7},{7,6},{8,9},{9,8},{10,11... | collective-permute-start | bytes 47185928 | tf_op jit(solution)/shard_map/ppermute | solution.py:314
  1257.5 124.6 %collective-permute-start.32 = (bf16[1280,1536]{1,0:T(8,128)(2,1)}, bf16[1280,1536]{1,0:T(8,128)(2,1)}, u32[]{:S(2)}, u32[]{:S(2)}) collective-permute-start(bf16[1280,1536]{1,0:T(8,128)(2,1)} %fusion.31), channel_id=1, source_target_pairs={{0,16},{16,0},{1,17},{17,1},{2,18},{18,2},{3,19},{19,3},{4,20},{20... | collective-permute-start | bytes 11796488 | tf_op jit(solution)/shard_map/ppermute | solution.py:367
  1285.7 170.2 %collective-permute-start.37 = (bf16[1280,1536]{1,0:T(8,128)(2,1)}, bf16[1280,1536]{1,0:T(8,128)(2,1)}, u32[]{:S(2)}, u32[]{:S(2)}) collective-permute-start(bf16[1280,1536]{1,0:T(8,128)(2,1)} %fusion.34), channel_id=1, source_target_pairs={{0,16},{16,0},{1,17},{17,1},{2,18},{18,2},{3,19},{19,3},{4,20},{20... | collective-permute-start | bytes 11796488 | tf_op jit(solution)/shard_map/ppermute | solution.py:367
  1512.2 491.8 %reduce-scatter.3.cloned.1.call-start = ((), (), s32[]{:S(2)}) async-start(), calls=%async_computation.8 | async-start | bytes 19599360 | tf_op jit(solution)/shard_map/reduce_scatter | solution.py:640
  1700.0 60.3 %collective-permute-start.19 = (bf16[1,256,2560]{2,1,0:T(8,128)(2,1)}, bf16[1,256,2560]{2,1,0:T(8,128)(2,1)}, u32[]{:S(2)}, u32[]{:S(2)}) collective-permute-start(bf16[1,256,2560]{2,1,0:T(8,128)(2,1)} %combine.49), channel_id=1, source_target_pairs={{0,4},{1,5},{4,8},{5,9},{8,12},{9,13},{12,14},{13,15},{14,10},{15,... | collective-permute-start | bytes 3932168 | tf_op jit(solution)/shard_map/ppermute | solution.py:332
  1705.5 60.0 %collective-permute-start.21 = (bf16[1,256,2560]{2,1,0:T(8,128)(2,1)}, bf16[1,256,2560]{2,1,0:T(8,128)(2,1)}, u32[]{:S(2)}, u32[]{:S(2)}) collective-permute-start(bf16[1,256,2560]{2,1,0:T(8,128)(2,1)} %combine.52), channel_id=1, source_target_pairs={{4,0},{5,1},{8,4},{9,5},{12,8},{13,9},{14,12},{15,13},{10,14},{11,... | collective-permute-start | bytes 3932168 | tf_op jit(solution)/shard_map/ppermute | solution.py:332
  1707.1 233.6 %collective-permute-start.43 = (bf16[1536,1280]{1,0:T(8,128)(2,1)}, bf16[1536,1280]{1,0:T(8,128)(2,1)}, u32[]{:S(2)}, u32[]{:S(2)}) collective-permute-start(bf16[1536,1280]{1,0:T(8,128)(2,1)} %fusion.37), channel_id=1, source_target_pairs={{0,16},{16,0},{1,17},{17,1},{2,18},{18,2},{3,19},{19,3},{4,20},{20... | collective-permute-start | bytes 11796488 | tf_op jit(solution)/shard_map/ppermute | solution.py:367
  1725.6 147.9 %collective-permute-start.42 = (bf16[96,2560]{1,0:T(8,128)(2,1)S(1)}, bf16[96,2560]{1,0:T(8,128)(2,1)S(1)}, u32[]{:S(2)}, u32[]{:S(2)}) collective-permute-start(bf16[96,2560]{1,0:T(8,128)(2,1)S(1)} %copy-done.51), channel_id=1, source_target_pairs={{0,16},{16,0},{1,17},{17,1},{2,18},{18,2},{3,19},{19,3},{4,20},{20... | collective-permute-start | bytes 1474568 | tf_op jit(solution)/shard_map/ppermute | solution.py:367
  1770.6 139.2 %collective-permute-start.41 = (bf16[1280,384]{1,0:T(8,128)(2,1)S(1)}, bf16[1280,384]{1,0:T(8,128)(2,1)S(1)}, u32[]{:S(2)}, u32[]{:S(2)}) collective-permute-start(bf16[1280,384]{1,0:T(8,128)(2,1)S(1)} %copy-done.68), channel_id=1, source_target_pairs={{0,16},{16,0},{1,17},{17,1},{2,18},{18,2},{3,19},{19,3},{4,20},{20... | collective-permute-start | bytes 2949128 | tf_op jit(solution)/shard_map/ppermute | solution.py:367
  (103 other events, 2099.0 us)
Sparse Core Ops, SparseCore 0:
  11.5 171.3 all-gather.6
  209.1 127.4 all-gather.8
  413.0 207.6 all-gather.10
  622.2 207.5 all-gather.12
  1512.3 161.5 reduce-scatter.4
  1676.2 244.7 reduce-scatter.2

commit v2 on v1

v2 whole, which is shorter than its diff:
```python
import functools

import jax
import jax.numpy as jnp
import numpy as np
from jax import lax
from jax.experimental import pallas as pl
from jax.experimental.pallas import tpu as pltpu
from jax.sharding import PartitionSpec as P

MODEL_WIDTH = 2560
QUERY_HEADS = 20
KEY_VALUE_HEADS = 4
HEAD_SIZE = 128
TOP = 6
GROUP = QUERY_HEADS // KEY_VALUE_HEADS
QUERY_WIDTH = QUERY_HEADS * HEAD_SIZE
KEY_WIDTH = KEY_VALUE_HEADS * HEAD_SIZE
KERNEL_VMEM = 56 * 1024 * 1024
COMBINE_VMEM = 36 * 1024 * 1024


norm_eps = 1e-05
rope_base = 500000.0
causal_masked_score = -1e30


def rope_tables(token_positions):
    half_width = HEAD_SIZE // 2
    frequency = rope_base ** (-(jnp.arange(half_width, dtype=jnp.float32) * 2.0 / HEAD_SIZE))
    angles = token_positions[:, None].astype(jnp.float32) * frequency[None, :]
    cosine, sine = jnp.cos(angles), jnp.sin(angles)
    return (
        jnp.concatenate([cosine, cosine], axis=1),
        jnp.concatenate([-sine, sine], axis=1),
    )


def rms_scale(value_rows_all):
    return lax.rsqrt(jnp.mean(value_rows_all * value_rows_all, axis=-1, keepdims=True) + norm_eps)


def norm_back(grad_normed, source, inverse, gain_vector):
    scaled = grad_normed * gain_vector
    return inverse * scaled - source * inverse**3 * jnp.mean(
        scaled * source, axis=-1, keepdims=True
    )


def dot32(left, right):
    return jnp.dot(left, right, preferred_element_type=jnp.float32)


def dot_t(left, right):
    return lax.dot_general(
        left, right, (((1,), (1,)), ((), ())), preferred_element_type=jnp.float32
    )


def t_dot(left, right):
    return lax.dot_general(
        left, right, (((0,), (0,)), ((), ())), preferred_element_type=jnp.float32
    )


def tie(*values):
    return lax.optimization_barrier(values)


def kernel_params(limit=KERNEL_VMEM):
    return pltpu.CompilerParams(vmem_limit_bytes=limit)


def cost(flops, bytes_accessed, transcendentals=0):
    return pl.CostEstimate(
        flops=int(flops), bytes_accessed=int(bytes_accessed), transcendentals=int(transcendentals)
    )


def turn(values, cosine, sine):
    return values * cosine + pltpu.roll(values, HEAD_SIZE // 2, 1) * sine


def project_kernel(plain_from, rows_ref, weight_ref, cos_ref, sin_ref, out_ref):
    product = dot32(rows_ref[...], weight_ref[...])
    plain = pl.program_id(0) >= plain_from
    cosine = jnp.where(plain, 1.0, cos_ref[...])
    sine = jnp.where(plain, 0.0, sin_ref[...])
    for head in range(product.shape[1] // HEAD_SIZE):
        lanes = slice(head * HEAD_SIZE, (head + 1) * HEAD_SIZE)
        out_ref[:, lanes] = turn(product[:, lanes], cosine, sine).astype(jnp.bfloat16)


def project(rows, weight, tables, first_block, blocks, plain_from):
    count = rows.shape[0]
    return pl.pallas_call(
        functools.partial(project_kernel, plain_from),
        grid=(blocks,),
        in_specs=[
            pl.BlockSpec(rows.shape, lambda j: (0, 0)),
            pl.BlockSpec((weight.shape[0], KEY_WIDTH), lambda j: (0, first_block + j)),
            pl.BlockSpec(tables[0].shape, lambda j: (0, 0)),
            pl.BlockSpec(tables[1].shape, lambda j: (0, 0)),
        ],
        out_specs=pl.BlockSpec((count, KEY_WIDTH), lambda j: (0, j)),
        out_shape=jax.ShapeDtypeStruct((count, blocks * KEY_WIDTH), jnp.bfloat16),
        compiler_params=kernel_params(),
        cost_estimate=cost(
            2 * count * weight.shape[0] * blocks * KEY_WIDTH,
            2 * weight.shape[0] * (blocks * KEY_WIDTH + count),
        ),
        name="project",
    )(rows, weight, *tables)


def attend_probs(offset, first_row, query, keys):
    scores = dot_t(query, keys) * HEAD_SIZE ** (-0.5)
    rows = lax.broadcasted_iota(jnp.int32, scores.shape, 0) + (offset + first_row)
    places = lax.broadcasted_iota(jnp.int32, scores.shape, 1)
    scores = jnp.where(rows >= places, scores, causal_masked_score)
    weights = jnp.exp(scores - jnp.max(scores, axis=1, keepdims=True))
    return weights * (1.0 / jnp.sum(weights, axis=1, keepdims=True))


def attend_kernel(tile, offset_ref, query_ref, key_ref, value_ref, out_ref):
    keys, values = key_ref[...], value_ref[...]
    for head in range(GROUP):
        lanes = slice(head * HEAD_SIZE, (head + 1) * HEAD_SIZE)
        for start in range(0, query_ref.shape[0], tile):
            rows = slice(start, start + tile)
            probs = attend_probs(offset_ref[0], start, query_ref[rows, lanes], keys)
            out_ref[rows, lanes] = dot32(probs.astype(jnp.bfloat16), values).astype(jnp.bfloat16)


def attend(offset, query, key_value):
    count, places = query.shape[0], key_value.shape[0]
    work = count * places * HEAD_SIZE * QUERY_HEADS
    return pl.pallas_call(
        functools.partial(attend_kernel, min(count, 256)),
        grid=(KEY_VALUE_HEADS,),
        in_specs=[
            pl.BlockSpec(memory_space=pltpu.SMEM),
            pl.BlockSpec((count, GROUP * HEAD_SIZE), lambda g: (0, g)),
            pl.BlockSpec((places, HEAD_SIZE), lambda g: (0, g)),
            pl.BlockSpec((places, HEAD_SIZE), lambda g: (0, KEY_VALUE_HEADS + g)),
        ],
        out_specs=pl.BlockSpec((count, GROUP * HEAD_SIZE), lambda g: (0, g)),
        out_shape=jax.ShapeDtypeStruct(query.shape, jnp.bfloat16),
        compiler_params=kernel_params(),
        cost_estimate=cost(4 * work, 4 * query.size + 2 * key_value.size, work // HEAD_SIZE),
        name="attend",
    )(offset, query, key_value, key_value)


def attend_back_kernel(
    tile,
    offset_ref,
    query_ref,
    key_ref,
    value_ref,
    grad_ref,
    cos_ref,
    sin_ref,
    key_cos_ref,
    key_sin_ref,
    query_out,
    key_out,
    value_out,
):
    scale = HEAD_SIZE ** (-0.5)
    keys, values = key_ref[...], value_ref[...]
    key_sum = jnp.zeros(keys.shape, jnp.float32)
    value_sum = jnp.zeros(values.shape, jnp.float32)
    for head in range(GROUP):
        lanes = slice(head * HEAD_SIZE, (head + 1) * HEAD_SIZE)
        for start in range(0, query_ref.shape[0], tile):
            rows = slice(start, start + tile)
            query, grad = query_ref[rows, lanes], grad_ref[rows, lanes]
            probs = attend_probs(offset_ref[0], start, query, keys)
            grad_probs = dot_t(grad, values)
            delta = jnp.sum(probs * grad_probs, axis=1, keepdims=True)
            grad_scores = (probs * (grad_probs - delta)).astype(jnp.bfloat16)
            query_grad = dot32(grad_scores, keys) * scale
            query_out[rows, lanes] = turn(
                query_grad, cos_ref[rows, :], -sin_ref[rows, :]
            ).astype(jnp.bfloat16)
            key_sum = key_sum + t_dot(grad_scores, query)
            value_sum = value_sum + t_dot(probs.astype(jnp.bfloat16), grad)
    key_out[...] = turn(key_sum * scale, key_cos_ref[...], -key_sin_ref[...])
    value_out[...] = value_sum


def attend_back(offset, query, key_value, grad, tables, key_tables):
    count, places = query.shape[0], key_value.shape[0]
    work = count * places * HEAD_SIZE * QUERY_HEADS
    heads = pl.BlockSpec((count, GROUP * HEAD_SIZE), lambda g: (0, g))
    table = pl.BlockSpec((count, HEAD_SIZE), lambda g: (0, 0))
    key_table = pl.BlockSpec((places, HEAD_SIZE), lambda g: (0, 0))
    key_heads = pl.BlockSpec((places, HEAD_SIZE), lambda g: (0, g))
    return pl.pallas_call(
        functools.partial(attend_back_kernel, min(count, 256)),
        grid=(KEY_VALUE_HEADS,),
        in_specs=[
            pl.BlockSpec(memory_space=pltpu.SMEM),
            heads,
            key_heads,
            pl.BlockSpec((places, HEAD_SIZE), lambda g: (0, KEY_VALUE_HEADS + g)),
            heads,
            table,
            table,
            key_table,
            key_table,
        ],
        out_specs=[heads, key_heads, key_heads],
        out_shape=[
            jax.ShapeDtypeStruct(query.shape, jnp.bfloat16),
            jax.ShapeDtypeStruct((places, KEY_WIDTH), jnp.float32),
            jax.ShapeDtypeStruct((places, KEY_WIDTH), jnp.float32),
        ],
        compiler_params=kernel_params(),
        cost_estimate=cost(
            10 * work, 6 * query.size + 6 * key_value.size, work // HEAD_SIZE
        ),
        name="attend_back",
    )(offset, query, key_value, key_value, grad, *tables, *key_tables)


def silu_parts(gate_val, up_val):
    sigmoid_val = jax.nn.sigmoid(gate_val)
    silu_val = gate_val * sigmoid_val
    slope = up_val * sigmoid_val * (1.0 + gate_val * (1.0 - sigmoid_val))
    return [part.astype(jnp.bfloat16) for part in (silu_val * up_val, slope, silu_val)]


def row_chunks(count):
    return [slice(start, start + min(count, 256)) for start in range(0, count, min(count, 256))]


def slot_match(slots, capacity):
    places = lax.broadcasted_iota(jnp.int32, (capacity, slots.shape[1]), 0).astype(jnp.float32)
    return slots == places


def enter_kernel(slot_ref, rows_ref, weight_ref, picked_ref, act_ref, slope_ref):
    hidden = act_ref.shape[2]
    for chunk in row_chunks(rows_ref.shape[1]):
        product = dot32(rows_ref[0, chunk, :], weight_ref[...])
        act, slope, silu_val = silu_parts(product[:, :hidden], product[:, hidden:])
        act_ref[0, chunk, :] = act
        slope_ref[0, chunk, :hidden] = slope
        slope_ref[0, chunk, hidden:] = silu_val
    pick = jnp.where(slot_match(slot_ref[0, 0:1, :], picked_ref.shape[1]), 1.0, 0.0)
    picked_ref[0] = dot32(pick.astype(jnp.bfloat16), rows_ref[0]).astype(jnp.bfloat16)


def enter(slot_rows, rows, weight, capacity):
    count, tokens, width = rows.shape
    hidden = weight.shape[1] // 2
    block = lambda a, b: pl.BlockSpec((1, a, b), lambda i: (i, 0, 0))
    return pl.pallas_call(
        enter_kernel,
        grid=(count,),
        in_specs=[
            block(2, tokens),
            block(tokens, width),
            pl.BlockSpec(weight.shape, lambda i: (0, 0)),
        ],
        out_specs=[block(capacity, width), block(tokens, hidden), block(tokens, 2 * hidden)],
        out_shape=[
            jax.ShapeDtypeStruct((count, capacity, width), jnp.bfloat16),
            jax.ShapeDtypeStruct((count, tokens, hidden), jnp.bfloat16),
            jax.ShapeDtypeStruct((count, tokens, 2 * hidden), jnp.bfloat16),
        ],
        compiler_params=kernel_params(),
        cost_estimate=cost(
            2 * count * tokens * width * (capacity + 2 * hidden),
            2 * count * width * (tokens + capacity),
        ),
        name="enter",
    )(slot_rows, rows, weight)


def enter_back_kernel(slot_ref, rows_ref, weight_ref, slope_ref, picked_ref, grad_ref):
    rows = rows_ref[0]
    hidden = weight_ref.shape[0]
    for chunk in row_chunks(rows_ref.shape[1]):
        product = dot_t(rows_ref[0, chunk, :], weight_ref[...])
        for lanes in (slice(0, hidden), slice(hidden, 2 * hidden)):
            slope = slope_ref[0, chunk, lanes].astype(jnp.float32)
            grad_ref[0, chunk, lanes] = (product * slope).astype(jnp.bfloat16)
    match = slot_match(slot_ref[0, 0:1, :], picked_ref.shape[1])
    slot_weight = jnp.sum(jnp.where(match, slot_ref[0, 1:2, :], 0.0), axis=1, keepdims=True)
    pick = jnp.where(match, 1.0, 0.0).astype(jnp.bfloat16)
    picked_ref[0] = (dot32(pick, rows) * slot_weight).astype(jnp.bfloat16)


def enter_back(slot_rows, rows, weight, slope, capacity):
    count, tokens, width = rows.shape
    hidden = weight.shape[0]
    block = lambda a, b: pl.BlockSpec((1, a, b), lambda i: (i, 0, 0))
    return pl.pallas_call(
        enter_back_kernel,
        grid=(count,),
        in_specs=[
            block(2, tokens),
            block(tokens, width),
            pl.BlockSpec(weight.shape, lambda i: (0, 0)),
            block(tokens, 2 * hidden),
        ],
        out_specs=[block(capacity, width), block(tokens, 2 * hidden)],
        out_shape=[
            jax.ShapeDtypeStruct((count, capacity, width), jnp.bfloat16),
            jax.ShapeDtypeStruct((count, tokens, 2 * hidden), jnp.bfloat16),
        ],
        compiler_params=kernel_params(),
        cost_estimate=cost(
            2 * count * tokens * width * (capacity + hidden),
            2 * count * width * (tokens + capacity),
        ),
        name="enter_back",
    )(slot_rows, rows, weight, slope)


def expert_in_kernel(rows_ref, gate_ref, up_ref, act_ref, slope_ref, silu_ref):
    for chunk in row_chunks(rows_ref.shape[0]):
        rows = rows_ref[chunk, :]
        parts = silu_parts(dot32(rows, gate_ref[...]), dot32(rows, up_ref[...]))
        act_ref[chunk, :], slope_ref[chunk, :], silu_ref[chunk, :] = parts


def expert_in(rows, gate, up):
    count, width = rows.shape
    hidden = gate.shape[1]
    high, wide = min(count, 1024), 512
    weight = pl.BlockSpec((width, wide), lambda m, n: (0, n))
    out = pl.BlockSpec((high, wide), lambda m, n: (m, n))
    return pl.pallas_call(
        expert_in_kernel,
        grid=(count // high, hidden // wide),
        in_specs=[pl.BlockSpec((high, width), lambda m, n: (m, 0)), weight, weight],
        out_specs=[out] * 3,
        out_shape=[jax.ShapeDtypeStruct((count, hidden), jnp.bfloat16)] * 3,
        compiler_params=kernel_params(),
        cost_estimate=cost(4 * count * width * hidden, 2 * count * (width + 3 * hidden)),
        name="expert_in",
    )(rows, gate, up)


def expert_back_kernel(rows_ref, weight_ref, slope_ref, silu_ref, *rest):
    gate_out, up_out = rest[-2:]
    for chunk in row_chunks(rows_ref.shape[0]):
        product = dot_t(rows_ref[chunk, :], weight_ref[...])
        slope = slope_ref[chunk, :].astype(jnp.float32)
        silu_val = silu_ref[chunk, :].astype(jnp.float32)
        gate_out[chunk, :] = (product * slope).astype(jnp.bfloat16)
        up_out[chunk, :] = (product * silu_val).astype(jnp.bfloat16)


def expert_back(rows, weight, slope, silu_val, half, earlier=()):
    count, width = rows.shape
    hidden = weight.shape[0]
    high, wide = min(count // 2, 1024), 512
    first = half * (count // 2 // high)
    tile = pl.BlockSpec((high, wide), lambda m, n: (first + m, n))
    return pl.pallas_call(
        expert_back_kernel,
        grid=(count // 2 // high, hidden // wide),
        in_specs=[
            pl.BlockSpec((high, width), lambda m, n: (first + m, 0)),
            pl.BlockSpec((wide, width), lambda m, n: (n, 0)),
            tile,
            tile,
        ]
        + [pl.BlockSpec(memory_space=pl.ANY)] * len(earlier),
        out_specs=[tile, tile],
        out_shape=[jax.ShapeDtypeStruct((count, hidden), jnp.bfloat16)] * 2,
        input_output_aliases={4 + i: i for i in range(len(earlier))},
        compiler_params=kernel_params(),
        cost_estimate=cost(count * width * hidden, count * (width + 4 * hidden)),
        name="expert_back",
    )(rows, weight, slope, silu_val, *earlier)


def expert_rows_kernel(gate_grad_ref, up_grad_ref, gate_ref, up_ref, *rest):
    out_ref = rest[-1]
    total = dot_t(gate_grad_ref[...], gate_ref[...]) + dot_t(up_grad_ref[...], up_ref[...])
    out_ref[...] = total.astype(jnp.bfloat16)


def expert_grad_rows(gate_grad, up_grad, gate, up, column_half, half, earlier=()):
    count, hidden = gate_grad.shape
    wide = gate.shape[0] // 2
    high = min(count // 2, 512)
    first = half * (count // 2 // high)
    grad = pl.BlockSpec((high, hidden), lambda m: (first + m, 0))
    weight = pl.BlockSpec((wide, hidden), lambda m: (column_half, 0))
    return pl.pallas_call(
        expert_rows_kernel,
        grid=(count // 2 // high,),
        in_specs=[grad, grad, weight, weight] + [pl.BlockSpec(memory_space=pl.ANY)] * len(earlier),
        out_specs=pl.BlockSpec((high, wide), lambda m: (first + m, 0)),
        out_shape=jax.ShapeDtypeStruct((count, wide), jnp.bfloat16),
        input_output_aliases={4: 0} if earlier else {},
        compiler_params=kernel_params(),
        cost_estimate=cost(
            2 * count * wide * hidden, (2 * count + 4 * wide) * hidden + count * wide
        ),
        name="expert_grad_rows",
    )(gate_grad, up_grad, gate, up, *earlier)


def qkv_grad_kernel(rows_ref, query_ref, key_value_ref, gain_ref, out_ref):
    rows = rows_ref[...]
    edge = query_ref.shape[1]
    end = edge + key_value_ref.shape[1]
    out_ref[:, :edge] = dot32(rows, query_ref[...]).astype(jnp.bfloat16)
    out_ref[:, edge:end] = dot32(rows, key_value_ref[...]).astype(jnp.bfloat16)
    out_ref[:, end:] = gain_ref[...]


def qkv_grad(rows_t, query_grad, key_value_grad, gain_term):
    width, count = rows_t.shape
    high = 256
    columns = query_grad.shape[1] + key_value_grad.shape[1] + gain_term.shape[1]
    whole = lambda array: pl.BlockSpec(array.shape, lambda m: (0, 0))
    return pl.pallas_call(
        qkv_grad_kernel,
        grid=(width // high,),
        in_specs=[
            pl.BlockSpec((high, count), lambda m: (m, 0)),
            whole(query_grad),
            whole(key_value_grad),
            pl.BlockSpec((high, gain_term.shape[1]), lambda m: (m, 0)),
        ],
        out_specs=pl.BlockSpec((high, columns), lambda m: (m, 0)),
        out_shape=jax.ShapeDtypeStruct((width, columns), jnp.bfloat16),
        compiler_params=kernel_params(),
        cost_estimate=cost(2 * width * count * columns, 2 * width * (columns + count)),
        name="qkv_grad",
    )(rows_t, query_grad, key_value_grad, gain_term)


def combine_kernel(scaled, pieces, arrivals, added, unit_ref, info_ref, act_ref, weight_ref, *rest):
    rows_refs, rest = rest[:pieces], rest[pieces:]
    arrived_refs, rest = rest[:arrivals], rest[arrivals:]
    added_refs, out_refs = rest[:added], rest[added:]
    slot = info_ref[0, :, 0:1]
    capacity = rows_refs[0].shape[1]
    lanes = lax.broadcasted_iota(jnp.int32, (slot.shape[0], capacity), 1).astype(jnp.float32)
    pick = jnp.where(slot == lanes, 1.0, 0.0).astype(jnp.bfloat16)

    def store(way):
        total = dot32(pick, rows_refs[way % pieces][0])
        if scaled:
            total = total * info_ref[0, :, 1:2]
        total = total + dot32(act_ref[0], weight_ref[...])
        for added_ref in added_refs:
            total = total + added_ref[0].astype(jnp.float32)
        if arrivals:
            total = total + arrived_refs[way][0].astype(jnp.float32)
        out_ref = out_refs[way % len(out_refs)]
        out_ref[0] = total.astype(out_ref.dtype)

    if pieces == 1 and not arrivals and len(out_refs) == 1:
        store(0)
        return
    for way in range(2):

        @pl.when(pl.program_id(0) % 2 == way)
        def _(way=way):
            store(way)


def combine(
    units, info, rows, act, weight, scaled, arrived=(), partner=(), own=(), kind="units",
    out_dtype=jnp.bfloat16,
):
    count = units.shape[0]
    tokens = info.shape[1]
    width, hidden = weight.shape[1], act.shape[2]
    capacity = rows[0].shape[1]
    columns = width // 2
    unit_block = lambda array: pl.BlockSpec((1,) + array.shape[1:], lambda i, u: (u[i], 0, 0))
    fixed = pl.BlockSpec((1, tokens, columns), lambda i, u: (0, 0, 0))
    half = pl.BlockSpec((1, tokens, columns), lambda i, u: (0, 0, i % 2))
    in_specs = [
        unit_block(info),
        unit_block(act),
        pl.BlockSpec((hidden, columns), lambda i, u: (0, i % 2)),
    ]
    block = (1, capacity, columns)
    if len(rows) == 1:
        in_specs.append(pl.BlockSpec(block, lambda i, u: (u[i], 0, i % 2)))
    else:
        in_specs.append(pl.BlockSpec(block, lambda i, u: (u[i - i % 2], 0, 0)))
        in_specs.append(pl.BlockSpec(block, lambda i, u: (u[i - i % 2 + 1], 0, 0)))
    in_specs += [fixed] * len(arrived)
    added = [array for array, _ in partner] + list(own)
    for _, at in partner:
        in_specs.append(pl.BlockSpec((1, tokens, columns), lambda i, u, at=at: (at + i, 0, 0)))
    in_specs += [half] * len(own)
    out_specs, out_shape = {
        "units": (
            [pl.BlockSpec((1, tokens, columns), lambda i, u: (i, 0, 0))],
            [(count, tokens, columns)],
        ),
        "ways": ([fixed, fixed], [(1, tokens, columns)] * 2),
        "tokens": ([half], [(1, tokens, width)]),
    }[kind]
    return pl.pallas_call(
        functools.partial(combine_kernel, scaled, len(rows), len(arrived), len(added)),
        grid_spec=pltpu.PrefetchScalarGridSpec(
            num_scalar_prefetch=1, grid=(count,), in_specs=in_specs, out_specs=out_specs
        ),
        out_shape=[jax.ShapeDtypeStruct(shape, out_dtype) for shape in out_shape],
        compiler_params=kernel_params(COMBINE_VMEM),
        cost_estimate=cost(
            2 * count * tokens * columns * (capacity + hidden),
            2 * count * columns * (capacity + tokens * (1 + len(added) + len(arrived) // 2)),
        ),
        name="combine",
    )(units, info, act, weight, *rows, *arrived, *added)


def weight_grad_kernel(part_ref, left_ref, right_ref, *rest):
    *arrived_refs, out_ref, sum_ref = rest
    step = pl.program_id(0)
    product = t_dot(left_ref[...], right_ref[...])

    @pl.when(step == 0)
    def _():
        sum_ref[...] = product

    @pl.when(step > 0)
    def _():
        sum_ref[...] += product

    @pl.when(step == pl.num_programs(0) - 1)
    def _():
        total = sum_ref[...]
        for arrived_ref in arrived_refs:
            total = total + arrived_ref[...].astype(jnp.float32)
        out_ref[...] = total.astype(out_ref.dtype)


def weight_grad(left, right, axis, part, out_dtype, arrived=()):
    count = left.shape[0]
    high = min(count, 1024)
    widths = [left.shape[1], right.shape[1]]
    widths[axis] //= 2
    at = (lambda k, p: (k, p[0]), lambda k, p: (k, 0))
    whole = pl.BlockSpec(tuple(widths), lambda k, p: (0, 0))
    return pl.pallas_call(
        weight_grad_kernel,
        grid_spec=pltpu.PrefetchScalarGridSpec(
            num_scalar_prefetch=1,
            grid=(count // high,),
            in_specs=[
                pl.BlockSpec((high, widths[0]), at[axis]),
                pl.BlockSpec((high, widths[1]), at[1 - axis]),
            ]
            + [whole] * len(arrived),
            out_specs=whole,
            scratch_shapes=[pltpu.VMEM(tuple(widths), jnp.float32)],
        ),
        out_shape=jax.ShapeDtypeStruct(tuple(widths), out_dtype),
        compiler_params=kernel_params(),
        cost_estimate=cost(
            2 * count * widths[0] * widths[1], 2 * count * sum(widths) + 4 * widths[0] * widths[1]
        ),
        name="weight_grad",
    )(part, left, right, *arrived)


def exp_ring(chips):
    if chips % 2:
        return list(range(chips))
    return list(range(0, chips, 2)) + list(range(chips - 1, 0, -2))


class ChipRing:
    def __init__(self):
        exp_count = lax.axis_size("exp")
        self.chips = exp_count // 2
        ring = exp_ring(self.chips)
        place_of = np.argsort(np.array(ring)).astype(np.int32)
        index = lax.axis_index("exp")
        self.core = index % 2
        self.place = jnp.asarray(place_of)[index // 2]
        self.ring = jnp.asarray(np.array(ring, np.int32))
        self.swap = [(i, i ^ 1) for i in range(exp_count)]
        self.ways = ([], [])
        for at in range(self.chips):
            for core in range(2):
                here, there = ring[at] * 2 + core, ring[(at + 1) % self.chips] * 2 + core
                self.ways[0].append((here, there))
                self.ways[1].append((there, here))

    def targets(self, step):
        at = jnp.stack([self.place - step + self.chips, self.place + step]) % self.chips
        return self.ring[at]

    def move(self, totals):
        return [lax.ppermute(total, "exp", way) for total, way in zip(totals, self.ways)]

    def swap_cores(self, value):
        return lax.ppermute(value, "exp", self.swap)


class ExpRing:
    def __init__(self, part, out_dtype, own=(), late_from=(4,)):
        self.part, self.out_dtype, self.own = part, out_dtype, own
        self.line = ChipRing()
        self.arrived, self.step = (), 0
        self.swapped, self.partner = [], []
        edges = list(late_from) + [self.line.chips + 1]
        first = part(self.other_units(range(1, 2)))[0]
        first, units = tie(first, self.other_units(range(2, edges[0])))
        self.take(first)
        second = part(units)[0]
        second, self.late_units = tie(
            second, [self.other_units(range(*edge)) for edge in zip(edges, edges[1:])]
        )
        self.take(second)

    def units(self, step, core):
        return (self.line.targets(step) * 2 + core).astype(jnp.int32)

    def other_units(self, steps):
        return jnp.concatenate([self.units(step, 1 - self.line.core) for step in steps])

    def take(self, total):
        self.partner += [(len(self.swapped), 2 * i) for i in range(total.shape[0] // 2)]
        self.swapped.append(self.line.swap_cores(total))

    def from_partner(self, step):
        group, at = self.partner[step - 1]
        return ((self.swapped[group], at),)

    def late(self, units):
        return self.part(units)[0]

    def totals(self):
        self.step += 1
        return self.part(
            self.units(self.step, self.line.core),
            arrived=self.arrived,
            partner=self.from_partner(self.step),
            kind="ways",
        )

    def finish(self):
        return self.part(
            self.units(self.line.chips, self.line.core),
            arrived=self.arrived,
            partner=self.from_partner(self.line.chips),
            own=self.own,
            kind="tokens",
            out_dtype=self.out_dtype,
        )[0][0]


def ring_step(rings, work, *operands):
    totals = [ring.totals() for ring in rings]
    totals, operands = tie(totals, operands)
    moved = [ring.line.move(total) for ring, total in zip(rings, totals)]
    swapped = [ring.swapped for ring in rings]
    moved, swapped, result = tie(moved, swapped, work(*operands))
    for ring, arrived, ring.swapped in zip(rings, moved, swapped):
        ring.arrived = tuple(arrived)
    return result


class SpreadSum:
    def __init__(self, term):
        self.line = ChipRing()
        rows = term.shape[0] // (4 * self.line.chips)
        self.term = term.reshape(2, self.line.chips, 2, rows, term.shape[1])
        self.arrived = self.line.swap_cores(self.pick(self.term, 1 - self.line.core, 2))

    def pick(self, array, index, axis):
        return lax.dynamic_index_in_dim(array, index, axis, keepdims=False)

    def add(self, *values):
        return sum(value.astype(jnp.float32) for value in values)

    def ctx_done(self, arrived):
        value = self.add(self.pick(self.term, self.line.core, 2), arrived).astype(jnp.bfloat16)
        index = lax.axis_index("ctx")
        arrived = ctx_send(self.pick(value, 1 - index, 0), 0)
        return self.add(self.pick(value, index, 0), arrived).astype(jnp.bfloat16)

    def finish(self, value, pieces):
        done = []
        columns = value.shape[2] // 2
        halves = [value[..., :columns], value[..., columns:]]
        arrived = ([], [])
        for step in range(1, self.line.chips + 1):
            targets = self.line.targets(step)
            totals = [
                self.add(self.pick(halves[way], targets[way], 0), *arrived[way]) for way in range(2)
            ]
            if step == self.line.chips:
                return jnp.concatenate(totals, axis=1), done
            totals = [total.astype(jnp.bfloat16) for total in totals]
            if step <= len(pieces):
                operands, work = pieces[step - 1]
                totals, operands = tie(totals, operands)
            moved = self.line.move(totals)
            if step <= len(pieces):
                moved, result = tie(moved, work(*operands))
                done.append(result)
            arrived = tuple([value] for value in moved)


def ctx_fetch(part, axis):
    if lax.axis_size("ctx") != 2:
        return lax.all_gather(part, "ctx", axis=axis, tiled=True)
    return lax.ppermute(part, "ctx", [(0, 1), (1, 0)])


def ctx_join(part, other, axis):
    if lax.axis_size("ctx") != 2:
        return other
    return lax.dynamic_update_slice_in_dim(
        jnp.concatenate([other, other], axis=axis),
        part,
        lax.axis_index("ctx") * part.shape[axis],
        axis,
    )


def ctx_gather(part, axis):
    return ctx_join(part, ctx_fetch(part, axis), axis)


def ctx_pair_part(which):
    return jnp.full((1,), which, jnp.int32)


def ctx_theirs(left, right, axis):
    if lax.axis_size("ctx") == 2:
        part = ctx_pair_part(1 - lax.axis_index("ctx"))
        return weight_grad(left, right, axis, part, jnp.bfloat16)
    return t_dot(left, right).astype(jnp.bfloat16)


def ctx_send(theirs, axis):
    if lax.axis_size("ctx") == 2:
        return lax.ppermute(theirs, "ctx", [(0, 1), (1, 0)])
    return lax.psum_scatter(theirs, "ctx", scatter_dimension=axis, tiled=True)


def ctx_total(left, right, axis, arrived):
    if lax.axis_size("ctx") == 2:
        part = ctx_pair_part(lax.axis_index("ctx"))
        return weight_grad(left, right, axis, part, jnp.float32, (arrived,))
    return arrived.astype(jnp.float32)


def on_device(
    block_input,
    attn_gain,
    query_weight,
    key_matrix,
    value_matrix,
    output_weight,
    ffn_gain,
    shared_gate,
    shared_up,
    shared_down,
    expert_gate,
    expert_up,
    expert_down,
    routes,
    route_weights,
    cotangent,
):
    input_rows = block_input[0].astype(jnp.float32)
    tokens = input_rows.shape[0]
    ctx_count = lax.axis_size("ctx")
    exp_count = lax.axis_size("exp")
    exp_index = lax.axis_index("exp")
    both = ("ctx", "exp")
    offset = lax.axis_index("ctx") * tokens
    offset_array = jnp.full((1,), offset, jnp.int32)
    tables = rope_tables(offset + jnp.arange(tokens, dtype=jnp.int32))
    key_tables = rope_tables(jnp.arange(ctx_count * tokens, dtype=jnp.int32))

    own_rows = shared_gate.shape[0]
    attn_in = jnp.concatenate([query_weight, key_matrix, value_matrix], axis=1)
    edge = attn_in.shape[1]
    own_weights = route_weights[0].T
    (weights_high,) = tie(own_weights.astype(jnp.bfloat16))
    weights_low = (own_weights - weights_high.astype(jnp.float32)).astype(jnp.bfloat16)
    routing = jnp.concatenate(
        [routes[0].T.astype(jnp.bfloat16), weights_high, weights_low], axis=0
    ).reshape(-1)
    routing_columns = -(-routing.shape[0] // (own_rows * 128)) * 128
    routing = jnp.pad(routing, (0, own_rows * routing_columns - routing.shape[0]))
    full_in = lax.all_gather(
        jnp.concatenate([attn_in, routing.reshape(own_rows, routing_columns)], axis=1),
        both,
        axis=0,
        tiled=True,
    )
    routing = lax.dynamic_slice(
        full_in,
        (lax.axis_index("ctx") * exp_count * own_rows, edge),
        (exp_count * own_rows, routing_columns),
    ).reshape(exp_count, own_rows * routing_columns)
    routing = routing[:, : 3 * TOP * tokens].reshape(exp_count, 3 * TOP, tokens)
    routing = routing.astype(jnp.float32)
    grad_low = cotangent[0]

    own_hidden = shared_down.shape[0]
    padded = -(-ctx_count * own_hidden // 256) * 256
    padded_own = padded // ctx_count
    shared_in = jnp.stack([shared_gate, shared_up]).reshape(
        2, own_rows, ctx_count, exp_count, own_hidden
    )
    shared_in = jnp.transpose(shared_in, (3, 1, 0, 2, 4)).reshape(
        exp_count, own_rows, 2 * ctx_count * own_hidden
    )
    shared_in = lax.all_to_all(shared_in, "exp", split_axis=0, concat_axis=0, tiled=True)
    shared_in = jnp.pad(
        shared_in.reshape(exp_count * own_rows, 2 * ctx_count, own_hidden),
        ((0, 0), (0, 0), (0, padded_own - own_hidden)),
    ).reshape(exp_count * own_rows, 2 * padded)
    shared_in = ctx_gather(shared_in, 0)
    shared_in_t = shared_in.T
    shared_out_w = ctx_gather(jnp.pad(shared_down, ((0, padded_own - own_hidden), (0, 0))), 0)

    capacity = tokens * TOP * 4 // (3 * exp_count)
    named = routing[:, :TOP] == exp_index.astype(jnp.float32)
    chosen = jnp.any(named, axis=1)
    token_weight = jnp.sum(
        jnp.where(named, routing[:, TOP : 2 * TOP] + routing[:, 2 * TOP :], 0.0), axis=1
    )
    upto = (jnp.arange(tokens)[:, None] <= jnp.arange(tokens)[None, :]).astype(jnp.bfloat16)
    slot = dot32(chosen.astype(jnp.bfloat16), upto).astype(jnp.int32) - 1
    slot = jnp.where(chosen, slot, -1)
    slot_rows = jnp.stack([slot.astype(jnp.float32), token_weight], axis=1)
    token_info = jnp.pad(
        jnp.stack([slot.astype(jnp.float32), token_weight], axis=2), ((0, 0), (0, 0), (0, 126))
    )

    inverse_one = rms_scale(input_rows)
    normed_one = (input_rows * inverse_one * attn_gain).astype(jnp.bfloat16)
    full_in, normed_one, shared_in, shared_in_t, shared_out_w = tie(
        full_in, normed_one, shared_in, shared_in_t, shared_out_w
    )
    output_weight, full_in = tie(output_weight, full_in)
    full_output = lax.all_gather(output_weight, both, axis=0, tiled=True)
    key_value = ctx_gather(
        project(normed_one, full_in, tables, QUERY_HEADS // KEY_VALUE_HEADS, 2, 1), 0
    )
    normed_one_t = normed_one.T
    query = project(normed_one, full_in, tables, 0, QUERY_HEADS // KEY_VALUE_HEADS, QUERY_HEADS)
    attended_low = attend(offset_array, query, key_value)

    full_output, gate_part, up_part, down_part = tie(
        full_output, expert_gate[0], expert_up[0], expert_down[0]
    )
    gate_w = ctx_gather(gate_part, 0)
    up_w = ctx_gather(up_part, 0)
    down_other = ctx_fetch(down_part, 1)

    middle = input_rows + dot32(attended_low, full_output)
    inverse_two = rms_scale(middle)
    normed_two = (middle * inverse_two * ffn_gain).astype(jnp.bfloat16)

    rows_all = lax.all_gather(normed_two, "exp", axis=0, tiled=True)
    rows_all, gate_w, up_w, grad_low, slot_rows, token_info = tie(
        rows_all, gate_w, up_w, grad_low, slot_rows, token_info
    )
    grad_all = lax.all_gather(grad_low, "exp", axis=0, tiled=True)

    def blocks(rows):
        return rows.reshape(exp_count, tokens, MODEL_WIDTH)

    def flat(rows):
        return rows.reshape(rows.shape[0] * rows.shape[1], rows.shape[2])

    received, shared_act, shared_slope = enter(slot_rows, blocks(rows_all), shared_in, capacity)
    received = flat(received)
    expert_act, expert_slope, expert_silu = expert_in(received, gate_w, up_w)
    expert_act, down_other = tie(expert_act, down_other)
    down_w = ctx_join(down_part, down_other, 1)
    expert_rows = dot32(expert_act, down_w).astype(jnp.bfloat16)

    def slots(rows):
        return rows.reshape(exp_count, capacity, rows.shape[1])

    pair = exp_count >= 4 and exp_count % 4 == 0 and ctx_count == 2

    def sum_over_exp(part):
        units = jnp.repeat(jnp.arange(exp_count, dtype=jnp.int32), 2)
        everything = part(units)[0].reshape(exp_count, 2, tokens, MODEL_WIDTH // 2)
        return lax.psum_scatter(
            jnp.swapaxes(everything, 1, 2).reshape(exp_count * tokens, MODEL_WIDTH),
            "exp",
            scatter_dimension=0,
            tiled=True,
        ).astype(jnp.float32)

    out_part = functools.partial(
        combine,
        info=token_info,
        rows=(slots(expert_rows),),
        act=shared_act,
        weight=shared_out_w,
        scaled=True,
    )
    shared_act = flat(shared_act)
    rings = []
    if pair:
        out_ring = ExpRing(out_part, jnp.bfloat16, (middle[None],))
        rings = [out_ring]
        out_ring.take(ring_step(rings, out_ring.late, out_ring.late_units[0]))
    grad_expert, shared_back = ring_step(
        rings,
        lambda *operands: enter_back(*operands, capacity),
        slot_rows,
        blocks(grad_all),
        shared_out_w,
        shared_slope,
    )
    grad_expert = flat(grad_expert)
    grad_eu = ()
    for half in range(2):
        grad_eu = ring_step(
            rings,
            lambda *operands: expert_back(*operands[:4], half, operands[4:]),
            grad_expert,
            down_w,
            expert_slope,
            expert_silu,
            *grad_eu,
        )
    grad_eg, grad_eu = grad_eu
    pieces = [(), ()]
    for column_half, half in ((0, 0), (0, 1), (1, 0), (1, 1)):
        if (column_half, half) == (1, 1):
            rings = []
        piece = ring_step(
            rings,
            lambda *operands: expert_grad_rows(*operands[:4], column_half, half, operands[4:]),
            grad_eg,
            grad_eu,
            gate_w,
            up_w,
            *pieces[column_half],
        )
        pieces[column_half] = (piece,)
    grad_rows = [slots(piece) for (piece,) in pieces]

    grad_part = functools.partial(
        combine,
        info=token_info,
        rows=tuple(grad_rows),
        act=shared_back,
        weight=shared_in_t,
        scaled=False,
    )
    shared_back = flat(shared_back)
    theirs = lambda axis: lambda left, right: ctx_theirs(left, right, axis)
    total = lambda axis: lambda left, right, arrived: ctx_total(left, right, axis, arrived)
    if pair:
        output = out_ring.finish()
        grad_ring = ExpRing(grad_part, jnp.float32, late_from=(4, 6))
        rings = [grad_ring]
    else:
        output = (middle + sum_over_exp(out_part)).astype(jnp.bfloat16)

    def theirs_and_late(which, *operands):
        if not pair:
            return ring_step(rings, theirs(0), *operands)
        result, late = ring_step(
            rings,
            lambda units, *operands: (theirs(0)(*operands), grad_ring.late(units)),
            grad_ring.late_units[which],
            *operands,
        )
        grad_ring.take(late)
        return result

    gate_theirs = theirs_and_late(0, received, grad_eg)
    gate_arrived = ctx_send(gate_theirs, 0)
    up_theirs = theirs_and_late(1, received, grad_eu)
    up_arrived = ctx_send(up_theirs, 0)
    down_theirs = ring_step(rings, theirs(1), expert_act, grad_expert)
    down_arrived = ctx_send(down_theirs, 1)
    shared_in_theirs, shared_down_theirs = ring_step(
        rings,
        lambda a, b, c, d: (ctx_theirs(a, b, 0), ctx_theirs(c, d, 0)),
        rows_all,
        shared_back,
        shared_act,
        grad_all,
    )
    shared_in_arrived = ctx_send(shared_in_theirs, 0)
    shared_down_arrived = ctx_send(shared_down_theirs, 0)
    expert_gate_grad = ring_step(rings, total(0), received, grad_eg, gate_arrived)[None]
    if pair:
        ring_step(rings, lambda: ())
    expert_up_grad = ring_step(rings, total(0), received, grad_eu, up_arrived)[None]
    if pair:
        grad_two = grad_ring.finish()
    else:
        grad_two = sum_over_exp(grad_part)
    grad_two, down_arrived = tie(grad_two, down_arrived)

    ffn_gain_term = jnp.sum(grad_two * middle * inverse_two, axis=0)
    gain_term = jnp.pad(ffn_gain_term[:, None], ((0, 0), (0, 127))).astype(jnp.bfloat16)
    grad_middle = grad_low.astype(jnp.float32) + norm_back(grad_two, middle, inverse_two, ffn_gain)
    grad_middle_low = grad_middle.astype(jnp.bfloat16)
    output_term = t_dot(grad_middle_low, attended_low).astype(jnp.bfloat16)
    if pair:
        output_sum = SpreadSum(output_term)
        attended_gradient = dot_t(grad_middle_low, full_output).astype(jnp.bfloat16)
    else:
        attended_gradient = dot_t(grad_middle_low, full_output).astype(jnp.bfloat16)
        sum_o = lax.psum_scatter(output_term, both, scatter_dimension=0, tiled=True)

    grad_query_raw, key_terms, value_terms = attend_back(
        offset_array, query, key_value, attended_gradient, tables, key_tables
    )
    key_value_grad = jnp.concatenate([key_terms, value_terms], axis=1)
    if pair:
        own = lax.dynamic_slice_in_dim(key_value_grad, offset, tokens, axis=0)
        other = lax.dynamic_slice_in_dim(key_value_grad, tokens - offset, tokens, axis=0)
        other, swapped = tie(other.astype(jnp.bfloat16), output_sum.arrived)
        key_value_raw = own + ctx_send(other, 0).astype(jnp.float32)
        swapped = output_sum.ctx_done(swapped)
    else:
        key_value_raw = ctx_send(key_value_grad.astype(jnp.bfloat16), 0)
    key_value_raw = key_value_raw.astype(jnp.bfloat16)
    in_term = qkv_grad(normed_one_t, grad_query_raw, key_value_raw, gain_term)
    grad_raw = jnp.concatenate(
        [grad_query_raw, key_value_raw, jnp.zeros((tokens, routing_columns), jnp.bfloat16)], axis=1
    )
    grad_one = dot_t(grad_raw, full_in)
    input_grad = grad_middle + norm_back(grad_one, input_rows, inverse_one, attn_gain)
    sum_in = lax.psum_scatter(in_term, both, scatter_dimension=0, tiled=True).astype(jnp.float32)
    own_gain = lax.dynamic_slice_in_dim(
        attn_gain, (lax.axis_index("ctx") * exp_count + exp_index) * own_rows, own_rows
    )
    attn_gain_grad = jnp.sum(sum_in[:, :edge] * attn_in.astype(jnp.float32), axis=1) / own_gain

    rest = [
        ((expert_act, grad_expert, down_arrived), total(1)),
        ((rows_all, shared_back, shared_in_arrived), total(0)),
        ((shared_act, grad_all, shared_down_arrived), total(0)),
    ]
    if pair:
        sum_o, rest = output_sum.finish(swapped, rest)
    else:
        rest = [work(*operands) for operands, work in rest]
    expert_down_grad = rest[0][None]
    shared_in_grad = rest[1].astype(jnp.bfloat16)
    sum_sd = rest[2][:own_hidden]
    shared_in_grad = lax.all_to_all(
        shared_in_grad.reshape(exp_count, own_rows, 2 * padded),
        "exp",
        split_axis=0,
        concat_axis=0,
        tiled=True,
    ).reshape(exp_count, own_rows, 2, ctx_count, padded_own)[..., :own_hidden]
    shared_in_grad = (
        jnp.transpose(shared_in_grad, (2, 1, 3, 0, 4))
        .reshape(2, own_rows, exp_count * ctx_count * own_hidden)
        .astype(jnp.float32)
    )
    return (
        output[None],
        input_grad[None],
        attn_gain_grad,
        sum_in[:, :QUERY_WIDTH],
        sum_in[:, QUERY_WIDTH : QUERY_WIDTH + KEY_WIDTH],
        sum_in[:, QUERY_WIDTH + KEY_WIDTH : edge],
        sum_o.astype(jnp.float32).T,
        sum_in[:, edge],
        shared_in_grad[0],
        shared_in_grad[1],
        sum_sd,
        expert_gate_grad,
        expert_up_grad,
        expert_down_grad,
    )


def solution(mesh):
    return jax.shard_map(
        on_device,
        mesh=mesh,
        in_specs=(
            P("exp", "ctx", None),
            P(),
            P(("ctx", "exp"), None),
            P(("ctx", "exp"), None),
            P(("ctx", "exp"), None),
            P(("ctx", "exp"), None),
            P(),
            P(("ctx", "exp"), None),
            P(("ctx", "exp"), None),
            P(("ctx", "exp"), None),
            P("exp", "ctx", None),
            P("exp", "ctx", None),
            P("exp", None, "ctx"),
            P("exp", "ctx", None),
            P("exp", "ctx", None),
            P("exp", "ctx", None),
        ),
        out_specs=(
            P("exp", "ctx", None),
            P("exp", "ctx", None),
            P(("ctx", "exp")),
            P(("ctx", "exp"), None),
            P(("ctx", "exp"), None),
            P(("ctx", "exp"), None),
            P(None, ("ctx", "exp")),
            P(("ctx", "exp")),
            P(("ctx", "exp"), None),
            P(("ctx", "exp"), None),
            P(("ctx", "exp"), None),
            P("exp", "ctx", None),
            P("exp", "ctx", None),
            P("exp", None, "ctx"),
        ),
        check_vma=False,
    )
```

time: 2030 us -> 1930 us (0.951)
  matrix products: 632 us -> 92.3 us
  Pallas kernels: 313 us -> 806 us
  local copies, waits for them, and re-layouts: 75.7 us -> 140 us
  other arithmetic: 151 us -> 87.3 us
  waiting for transfers between devices: 712 us -> 661 us
  blocking collectives: 38.6 us -> 0 us
  between operations: 28.1 us -> 51.6 us
    pallas_call x36 -> x43, Pallas kernels: 216 us -> 709 us  [the longest x10 232 us: weight_grad(): pl.pallas_call(weight_grad_kernel, grid_spec=pltpu.PrefetchScalarGridSpec...]
    dot_general x12 -> x1, matrix products: 239 us -> 10.9 us  [t_dot(): lax.dot_general(left, right, (((0,), (0,)), ((), ())), preferred_element_...]
    dot_general x6 -> x2, matrix products: 182 us -> 30.1 us  [dot_t(): lax.dot_general(left, right, (((1,), (1,)), ((), ())), preferred_element_...]
    ppermute x38 -> x56, waiting for transfers between devices: 430 us -> 302 us  [the longest x6 194 us: ctx_fetch(): return lax.ppermute(part, 'ctx', [(0, 1), (1, 0)])]
    dot_general x6 -> x3, matrix products: 161 us -> 51.2 us  [dot32(): return jnp.dot(left, right, preferred_element_type=jnp.float32)]
    all_gather x1, waiting for transfers between devices: 110 us -> 22.7 us  [on_device(): rows_all = lax.all_gather(normed_two, 'exp', axis=0, tiled=True)]
    all_gather x1, waiting for transfers between devices: 0.01 us -> 60.2 us  [on_device(): lax.all_gather(jnp.concatenate([attn_in, routing.reshape(own_rows, routin...]
    dot_general x2 -> x0, matrix products: 50.5 us -> none  [to_slots(): jnp.einsum('sct,std->scd', pick, rows.reshape(exp_count, tokens, MODEL_WI...]
  transfers between devices with their start and end apart: 52 -> 70, of which waited for: 27 -> 38; matrix products, arithmetic and copies ran while one was open for 40% -> 12% of each run, Pallas kernels for 12% -> 38%
where the time goes in v2:
time: 1930 us; the launch traced here: 1910 us
  Pallas kernels  806 us (42%)
  waiting for transfers between devices  661 us (34%)
  local copies, waits for them, and re-layouts  140 us (7%)
  matrix products  92.3 us (5%)
  other arithmetic  87.3 us (5%)
  starting transfers between devices  76 us (4%)
  between operations  51.6 us (3%)
    pallas_call x10, Pallas kernels, weight_grad(): pl.pallas_call(weight_grad_kernel, grid_spec=pltpu.PrefetchScalarGridSpec...  232 us
    ppermute x7, waiting for transfers between devices, ctx_send(): return lax.ppermute(theirs, 'ctx', [(0, 1), (1, 0)])  217 us
    ppermute x6, waiting for transfers between devices, ctx_fetch(): return lax.ppermute(part, 'ctx', [(0, 1), (1, 0)])  194 us
    pallas_call x23, Pallas kernels, combine(): pl.pallas_call(functools.partial(combine_kernel, scaled, len(rows), len(a...  167 us
    pallas_call x4, Pallas kernels, expert_grad_rows(): pl.pallas_call(expert_rows_kernel, grid=(count // 2 // high,), in_specs=[...  89.9 us
    ppermute x42, waiting for transfers between devices, move(): lax.ppermute(total, 'exp', way)  85.4 us
    pallas_call x1, Pallas kernels, expert_in(): pl.pallas_call(expert_in_kernel, grid=(count // high, hidden // wide), in...  75.9 us
    all_gather x1, waiting for transfers between devices, on_device(): lax.all_gather(jnp.concatenate([attn_in, routing.reshape(own_rows, routin...  60.2 us
  transfers between devices with their start and end apart: 70, of which 38 were waited for; matrix products, arithmetic and copies ran while one was open for 12% of the time, Pallas kernels for 38%

profile of v2, /device:TPU:0, one launch (start us, length us, event | category | flops | bytes accessed | tf_op | source)
XLA Modules:
  0.0 1914.3 jit_solution(12521538603404829057)
XLA Ops:
  33.8 25.9 %all-to-all-done = bf16[16,80,384]{2,1,0:T(8,128)(2,1)} async-done(((bf16[16,80,384]{2,1,0:T(8,128)(2,1)}), bf16[16,80,384]{2,1,0:T(8,128)(2,1)}, u32[]{:S(2)}, u32[]{:S(2)}) %all-to-all-start) | async-done | bytes 983072 | tf_op jit(solution)/shard_map/all_to_all | solution.py:825
  74.2 31.0 %collective-permute-done = bf16[1280,512]{0,1:T(8,128)(2,1)S(1)} collective-permute-done((bf16[1280,512]{0,1:T(8,128)(2,1)S(1)}, bf16[1280,512]{0,1:T(8,128)(2,1)S(1)}, u32[]{:S(2)}, u32[]{:S(2)}) %collective-permute-start) | collective-permute-done | bytes 1310752 | tf_op jit(solution)/shard_map/ppermute | solution.py:719
  105.5 60.2 %all-gather.5.cloned.1.call-done.weight_ref = bf16[2560,3712]{1,0:T(8,128)(2,1)} async-done(((bf16[80,3712]{1,0:T(8,128)(2,1)}), bf16[2560,3712]{1,0:T(8,128)(2,1)}) %all-gather.5.cloned.1.call-update) | async-done | bytes 19005456 | tf_op jit(solution)/shard_map/all_gather | solution.py:801
  208.9 28.9 %attend.1 = bf16[512,2560]{1,0:T(8,128)(2,1)} custom-call(s32[1]{0:T(128)} %bitcast.4.offset_ref, bf16[512,2560]{1,0:T(8,128)(2,1)} %project.2.query_ref, bf16[1024,1024]{1,0:T(8,128)(2,1)} %copy-done.40, bf16[1024,1024]{1,0:T(8,128)(2,1)} %copy-done.40), custom_call_target="tpu_custom_call" | custom-call | flops 5368709120 | bytes 7340032 | tf_op jit(solution)/shard_map/attend/pallas_call | solution.py:138
  237.8 32.7 %all-gather.7.cloned.1.call-done = bf16[2560,2560]{1,0:T(8,128)(2,1)} async-done(((bf16[80,2560]{1,0:T(8,128)(2,1)}), bf16[2560,2560]{1,0:T(8,128)(2,1)}) %all-gather.7.cloned.1.call-update) | async-done | bytes 13107216 | tf_op jit(solution)/shard_map/all_gather | solution.py:854
  300.5 74.0 %collective-permute-done.3 = bf16[1280,1536]{1,0:T(8,128)(2,1)} collective-permute-done((bf16[1280,1536]{1,0:T(8,128)(2,1)}, bf16[1280,1536]{1,0:T(8,128)(2,1)}, u32[]{:S(2)}, u32[]{:S(2)}) %collective-permute-start.3) | collective-permute-done | bytes 3932192 | tf_op jit(solution)/shard_map/ppermute | solution.py:719
  385.9 72.3 %collective-permute-done.4 = bf16[1280,1536]{1,0:T(8,128)(2,1)} collective-permute-done((bf16[1280,1536]{1,0:T(8,128)(2,1)}, bf16[1280,1536]{1,0:T(8,128)(2,1)}, u32[]{:S(2)}, u32[]{:S(2)}) %collective-permute-start.4) | collective-permute-done | bytes 3932192 | tf_op jit(solution)/shard_map/ppermute | solution.py:719
  469.6 22.7 %all-gather.9.cloned.1.call-done.left_ref = bf16[8192,2560]{1,0:T(8,128)(2,1)} async-done(((bf16[512,2560]{1,0:T(8,128)(2,1)}), bf16[8192,2560]{1,0:T(8,128)(2,1)}) %all-gather.9.cloned.1.call-update) | async-done | bytes 41943056 | tf_op jit(solution)/shard_map/all_gather | solution.py:873
  517.7 39.9 %enter.1 = (bf16[16,256,2560]{2,1,0:T(8,128)(2,1)}, bf16[16,512,256]{2,1,0:T(8,128)(2,1)}, bf16[16,512,512]{2,1,0:T(8,128)(2,1)}) custom-call(f32[16,2,512]{2,1,0:T(2,128)} %pad_maximum_fusion.11.slot_ref, bf16[16,512,2560]{2,1,0:T(8,128)(2,1)} %bitcast.223, bf16[2560,512]{1,0:T(8,128)(2,1)} %copy.76.weight_ref), custom_call_target="tpu_custom_call" | custom-call | flops 32212254720 | bytes 62914560 | tf_op jit(solution)/shard_map/enter/pallas_call | solution.py:260
  557.6 75.9 %expert_in.1 = (bf16[4096,1536]{1,0:T(8,128)(2,1)}, bf16[4096,1536]{1,0:T(8,128)(2,1)}, bf16[4096,1536]{1,0:T(8,128)(2,1)}) custom-call(bf16[4096,2560]{1,0:T(8,128)(2,1)} %bitcast.248, bf16[2560,1536]{1,0:T(8,128)(2,1)} %constant_dynamic-update-slice_fusion.2.gate_ref, bf16[2560,1536]{1,0:T(8,128)(2,1)} %constant_dynamic-update-slice_fusion.1.up_ref), custom_call_target="tpu_custom_call" | custom-call | flops 64424509440 | bytes 58720256 | tf_op jit(solution)/shard_map/expert_in/pallas_call | solution.py:337
  644.9 39.6 %convolution_convert_fusion = bf16[4096,2560]{1,0:T(8,128)(2,1)} fusion(bf16[4096,1536]{1,0:T(8,128)(2,1)} %get-tuple-element.470.left_ref, bf16[1536,2560]{1,0:T(8,128)(2,1)} %constant_dynamic-update-slice_fusion.weight_ref), kind=kOutput, calls=%fused_computation.8 | convolution fusion | flops 32222740480 | bytes 41418752 | tf_op jit(solution)/shard_map/dot_general | solution.py:51
  750.9 36.5 %enter_back.1 = (bf16[16,256,2560]{2,1,0:T(8,128)(2,1)}, bf16[16,512,512]{2,1,0:T(8,128)(2,1)}) custom-call(f32[16,2,512]{2,1,0:T(2,128)} %pad_maximum_fusion.11.slot_ref, bf16[16,512,2560]{2,1,0:T(8,128)(2,1)} %bitcast.224, bf16[256,2560]{1,0:T(8,128)(2,1)} %copy-done.15, bf16[16,512,512]{2,1,0:T(8,128)(2,1)} %get-tuple-element.297.slope_ref), custom_call_target="tpu_custom_call" | custom-call | flops 21474836480 | bytes 62914560 | tf_op jit(solution)/shard_map/enter_back/pallas_call | solution.py:301
  799.8 26.0 %expert_back.2 = (bf16[4096,1536]{1,0:T(8,128)(2,1)}, bf16[4096,1536]{1,0:T(8,128)(2,1)}) custom-call(bf16[4096,2560]{1,0:T(8,128)(2,1)} %bitcast.226, bf16[1536,2560]{1,0:T(8,128)(2,1)} %constant_dynamic-update-slice_fusion.weight_ref, bf16[4096,1536]{1,0:T(8,128)(2,1)} %get-tuple-element.328.slope_ref, bf16[4096,1536]{1,0:T(8,128)(2,1)} %get-tuple-element.329.silu_ref), custom_call_target="tpu_custom_call" | custom-call | flops 16106127360 | bytes 35651584 | tf_op jit(solution)/shard_map/expert_back/pallas_call | solution.py:365
  842.2 25.6 %expert_back.3 = (bf16[4096,1536]{1,0:T(8,128)(2,1)}, bf16[4096,1536]{1,0:T(8,128)(2,1)}) custom-call(bf16[4096,2560]{1,0:T(8,128)(2,1)} %bitcast.227, bf16[1536,2560]{1,0:T(8,128)(2,1)} %constant_dynamic-update-slice_fusion.weight_ref, bf16[4096,1536]{1,0:T(8,128)(2,1)} %get-tuple-element.328.slope_ref, ...), custom_call_target="tpu_custom_call", output_to_operand_aliasing={{0}: (4, {}), {1}: (5, {})} | custom-call | flops 16106127360 | bytes 35651584 | tf_op jit(solution)/shard_map/expert_back/pallas_call | solution.py:365
  1062.6 25.1 %weight_grad.10 = bf16[1280,1536]{1,0:T(8,128)(2,1)} custom-call(s32[1]{0:T(128)} %bitcast.41.part_ref, bf16[4096,2560]{1,0:T(8,128)(2,1)} %bitcast.249, bf16[4096,1536]{1,0:T(8,128)(2,1)} %get-tuple-element.439.gate_grad_ref.right_ref), custom_call_target="tpu_custom_call" | custom-call | flops 16106127360 | bytes 30932992 | tf_op jit(solution)/shard_map/weight_grad/pallas_call | solution.py:553
  1111.7 25.0 %weight_grad.11 = bf16[1280,1536]{1,0:T(8,128)(2,1)} custom-call(s32[1]{0:T(128)} %bitcast.41.part_ref, bf16[4096,2560]{1,0:T(8,128)(2,1)} %bitcast.250, bf16[4096,1536]{1,0:T(8,128)(2,1)} %get-tuple-element.455.up_grad_ref.right_ref), custom_call_target="tpu_custom_call" | custom-call | flops 16106127360 | bytes 30932992 | tf_op jit(solution)/shard_map/weight_grad/pallas_call | solution.py:553
  1148.6 25.2 %weight_grad.12 = bf16[1536,1280]{1,0:T(8,128)(2,1)} custom-call(s32[1]{0:T(128)} %bitcast.41.part_ref, bf16[4096,1536]{1,0:T(8,128)(2,1)} %get-tuple-element.470.left_ref, bf16[4096,2560]{1,0:T(8,128)(2,1)} %bitcast.228), custom_call_target="tpu_custom_call" | custom-call | flops 16106127360 | bytes 30932992 | tf_op jit(solution)/shard_map/weight_grad/pallas_call | solution.py:553
  1233.5 28.1 %weight_grad.15 = f32[1280,1536]{1,0:T(8,128)} custom-call(s32[1]{0:T(128)} %bitcast.44.part_ref, bf16[4096,2560]{1,0:T(8,128)(2,1)} %bitcast.251, bf16[4096,1536]{1,0:T(8,128)(2,1)} %get-tuple-element.439.gate_grad_ref.right_ref, bf16[1280,1536]{1,0:T(8,128)(2,1)} %collective-permute-done.35.rest_0_), custom_call_target="tpu_custom_call" | custom-call | flops 16106127360 | bytes 30932992 | tf_op jit(solution)/shard_map/weight_grad/pallas_call | solution.py:553
  1271.4 26.6 %collective-permute-done.38.rest_2_ = bf16[1,512,1280]{2,1,0:T(8,128)(2,1)} collective-permute-done((bf16[1,512,1280]{2,1,0:T(8,128)(2,1)}, bf16[1,512,1280]{2,1,0:T(8,128)(2,1)}, u32[]{:S(2)}, u32[]{:S(2)}) %collective-permute-start.38) | collective-permute-done | bytes 1310752 | tf_op jit(solution)/shard_map/ppermute | solution.py:604
  1311.2 27.8 %weight_grad.16 = f32[1280,1536]{1,0:T(8,128)} custom-call(s32[1]{0:T(128)} %bitcast.44.part_ref, bf16[4096,2560]{1,0:T(8,128)(2,1)} %bitcast.252, bf16[4096,1536]{1,0:T(8,128)(2,1)} %get-tuple-element.455.up_grad_ref.right_ref, bf16[1280,1536]{1,0:T(8,128)(2,1)} %collective-permute-done.40.rest_0_), custom_call_target="tpu_custom_call" | custom-call | flops 16106127360 | bytes 30932992 | tf_op jit(solution)/shard_map/weight_grad/pallas_call | solution.py:553
  1346.3 46.7 %collective-permute-done.43.rest_0_ = bf16[1536,1280]{1,0:T(8,128)(2,1)} collective-permute-done((bf16[1536,1280]{1,0:T(8,128)(2,1)}, bf16[1536,1280]{1,0:T(8,128)(2,1)}, u32[]{:S(2)}, u32[]{:S(2)}) %collective-permute-start.43) | collective-permute-done | bytes 3932192 | tf_op jit(solution)/shard_map/ppermute | solution.py:750
  1434.3 48.6 %attend_back.1 = (bf16[512,2560]{1,0:T(8,128)(2,1)}, f32[1024,512]{1,0:T(8,128)}, f32[1024,512]{1,0:T(8,128)}) custom-call(s32[1]{0:T(128)} %bitcast.4.offset_ref, bf16[512,2560]{1,0:T(8,128)(2,1)} %project.2.query_ref, bf16[1024,1024]{1,0:T(8,128)(2,1)} %copy-done.40, bf16[1024,1024]{1,0:T(8,128)(2,1)} %copy-done.40, ...), custom_call_target="tpu_custom_call" | custom-call | flops 13421772800 | bytes 14155776 | tf_op jit(solution)/shard_map/attend_back/pallas_call | solution.py:200
  1624.6 148.8 %collective-permute-done.46 = bf16[8,80,2560]{2,1,0:T(8,128)(2,1)} collective-permute-done((bf16[8,80,2560]{2,1,0:T(8,128)(2,1)}, bf16[8,80,2560]{2,1,0:T(8,128)(2,1)}, u32[]{:S(2)}, u32[]{:S(2)}) %collective-permute-start.46) | collective-permute-done | bytes 3276832 | tf_op jit(solution)/shard_map/ppermute | solution.py:750
  1778.6 27.8 %weight_grad.17 = f32[1536,1280]{1,0:T(8,128)} custom-call(s32[1]{0:T(128)} %bitcast.44.part_ref, bf16[4096,1536]{1,0:T(8,128)(2,1)} %get-tuple-element.470.left_ref, bf16[4096,2560]{1,0:T(8,128)(2,1)} %bitcast.229, bf16[1536,1280]{1,0:T(8,128)(2,1)} %collective-permute-done.43.rest_0_), custom_call_target="tpu_custom_call" | custom-call | flops 16106127360 | bytes 30932992 | tf_op jit(solution)/shard_map/weight_grad/pallas_call | solution.py:553
  (490 shorter events, 841.8 us)
Async XLA Ops:
  7.2 158.6 %all-gather.5.cloned.1.call-start = ((), (), s32[]{:S(2)}) async-start(), calls=%async_computation.3 | async-start | bytes 19599360 | tf_op jit(solution)/shard_map/all_gather | solution.py:801
  29.8 240.7 %all-gather.7.cloned.1.call-start = ((), (), s32[]{:S(2)}) async-start(), calls=%async_computation.4 | async-start | bytes 13516800 | tf_op jit(solution)/shard_map/all_gather | solution.py:854
  31.0 40.7 %collective-permute-start.1 = (bf16[128,2560]{1,0:T(8,128)(2,1)S(1)}, bf16[128,2560]{1,0:T(8,128)(2,1)}, u32[]{:S(2)}, u32[]{:S(2)}) collective-permute-start(bf16[128,2560]{1,0:T(8,128)(2,1)S(1)} %pad.23), channel_id=1, source_target_pairs={{0,16},{16,0},{1,17},{17,1},{2,18},{18,2},{3,19},{19,3},{4,20},{20... | collective-permute-start | bytes 1966088 | tf_op jit(solution)/shard_map/ppermute | solution.py:719
  165.8 326.5 %all-gather.9.cloned.1.call-start = ((), (), s32[]{:S(2)}) async-start(), calls=%async_computation.5 | async-start | bytes 44564480 | tf_op jit(solution)/shard_map/all_gather | solution.py:873
  286.3 462.5 %all-gather.11.cloned.1.call-start = ((), (), s32[]{:S(2)}) async-start(), calls=%async_computation.6 | async-start | bytes 44564480 | tf_op jit(solution)/shard_map/all_gather | solution.py:877
  286.4 88.2 %collective-permute-start.3 = (bf16[1280,1536]{1,0:T(8,128)(2,1)}, bf16[1280,1536]{1,0:T(8,128)(2,1)}, u32[]{:S(2)}, u32[]{:S(2)}) collective-permute-start(bf16[1280,1536]{1,0:T(8,128)(2,1)} %bitcast.238), channel_id=1, source_target_pairs={{0,16},{16,0},{1,17},{17,1},{2,18},{18,2},{3,19},{19,3},{4,20},{20... | collective-permute-start | bytes 11796488 | tf_op jit(solution)/shard_map/ppermute | solution.py:719
  289.1 169.1 %collective-permute-start.4 = (bf16[1280,1536]{1,0:T(8,128)(2,1)}, bf16[1280,1536]{1,0:T(8,128)(2,1)}, u32[]{:S(2)}, u32[]{:S(2)}) collective-permute-start(bf16[1280,1536]{1,0:T(8,128)(2,1)} %bitcast.240), channel_id=1, source_target_pairs={{0,16},{16,0},{1,17},{17,1},{2,18},{18,2},{3,19},{19,3},{4,20},{20... | collective-permute-start | bytes 11796488 | tf_op jit(solution)/shard_map/ppermute | solution.py:719
  492.3 1410.6 %reduce-scatter.2.cloned.1.call-start = ((), (), s32[]{:S(2)}) async-start(), calls=%async_computation.7 | async-start | bytes 19599360 | tf_op jit(solution)/shard_map/reduce_scatter | solution.py:1045
  516.2 117.3 %collective-permute-start.5 = (bf16[1536,1280]{1,0:T(8,128)(2,1)}, bf16[1536,1280]{1,0:T(8,128)(2,1)}, u32[]{:S(2)}, u32[]{:S(2)}) collective-permute-start(bf16[1536,1280]{1,0:T(8,128)(2,1)} %bitcast.242), channel_id=1, source_target_pairs={{0,16},{16,0},{1,17},{17,1},{2,18},{18,2},{3,19},{19,3},{4,20},{20... | collective-permute-start | bytes 11796488 | tf_op jit(solution)/shard_map/ppermute | solution.py:719
  693.8 48.1 %collective-permute-start.9 = (bf16[4,512,1280]{2,1,0:T(8,128)(2,1)S(1)}, bf16[4,512,1280]{2,1,0:T(8,128)(2,1)}, u32[]{:S(2)}, u32[]{:S(2)}) collective-permute-start(bf16[4,512,1280]{2,1,0:T(8,128)(2,1)S(1)} %combine.25), channel_id=1, source_target_pairs={{0,1},{1,0},{2,3},{3,2},{4,5},{5,4},{6,7},{7,6},{8,9},{9,8},{10,11... | collective-permute-start | bytes 15728648 | tf_op jit(solution)/shard_map/ppermute | solution.py:607
  741.8 45.5 %collective-permute-start.12 = (bf16[10,512,1280]{2,1,0:T(8,128)(2,1)}, bf16[10,512,1280]{2,1,0:T(8,128)(2,1)}, u32[]{:S(2)}, u32[]{:S(2)}) collective-permute-start(bf16[10,512,1280]{2,1,0:T(8,128)(2,1)} %combine.26), channel_id=1, source_target_pairs={{0,1},{1,0},{2,3},{3,2},{4,5},{5,4},{6,7},{7,6},{8,9},{9,8},{10,11... | collective-permute-start | bytes 39321608 | tf_op jit(solution)/shard_map/ppermute | solution.py:607
  1028.4 59.3 %collective-permute-start.26 = (bf16[4,512,1280]{2,1,0:T(8,128)(2,1)}, bf16[4,512,1280]{2,1,0:T(8,128)(2,1)}, u32[]{:S(2)}, u32[]{:S(2)}) collective-permute-start(bf16[4,512,1280]{2,1,0:T(8,128)(2,1)} %combine.36), channel_id=1, source_target_pairs={{0,1},{1,0},{2,3},{3,2},{4,5},{5,4},{6,7},{7,6},{8,9},{9,8},{10,11... | collective-permute-start | bytes 15728648 | tf_op jit(solution)/shard_map/ppermute | solution.py:607
  1087.7 49.0 %collective-permute-start.29 = (bf16[4,512,1280]{2,1,0:T(8,128)(2,1)}, bf16[4,512,1280]{2,1,0:T(8,128)(2,1)}, u32[]{:S(2)}, u32[]{:S(2)}) collective-permute-start(bf16[4,512,1280]{2,1,0:T(8,128)(2,1)} %copy-done.26), channel_id=1, source_target_pairs={{0,1},{1,0},{2,3},{3,2},{4,5},{5,4},{6,7},{7,6},{8,9},{9,8},{10,11... | collective-permute-start | bytes 15728648 | tf_op jit(solution)/shard_map/ppermute | solution.py:607
  1095.6 41.1 %collective-permute-start.27 = (bf16[1,512,1280]{2,1,0:T(8,128)(2,1)}, bf16[1,512,1280]{2,1,0:T(8,128)(2,1)}, u32[]{:S(2)}, u32[]{:S(2)}) collective-permute-start(bf16[1,512,1280]{2,1,0:T(8,128)(2,1)} %get-tuple-element.400), channel_id=1, source_target_pairs={{0,4},{1,5},{4,8},{5,9},{8,12},{9,13},{12,14},{13,15},{14,10},{15,... | collective-permute-start | bytes 3932168 | tf_op jit(solution)/shard_map/ppermute | solution.py:604
  1096.2 40.5 %collective-permute-start.28 = (bf16[1,512,1280]{2,1,0:T(8,128)(2,1)}, bf16[1,512,1280]{2,1,0:T(8,128)(2,1)}, u32[]{:S(2)}, u32[]{:S(2)}) collective-permute-start(bf16[1,512,1280]{2,1,0:T(8,128)(2,1)} %get-tuple-element.401), channel_id=1, source_target_pairs={{4,0},{5,1},{8,4},{9,5},{12,8},{13,9},{14,12},{15,13},{10,14},{11,... | collective-permute-start | bytes 3932168 | tf_op jit(solution)/shard_map/ppermute | solution.py:604
  1136.7 40.1 %collective-permute-start.32 = (bf16[6,512,1280]{2,1,0:T(8,128)(2,1)}, bf16[6,512,1280]{2,1,0:T(8,128)(2,1)}, u32[]{:S(2)}, u32[]{:S(2)}) collective-permute-start(bf16[6,512,1280]{2,1,0:T(8,128)(2,1)} %copy-done.25), channel_id=1, source_target_pairs={{0,1},{1,0},{2,3},{3,2},{4,5},{5,4},{6,7},{7,6},{8,9},{9,8},{10,11... | collective-permute-start | bytes 23592968 | tf_op jit(solution)/shard_map/ppermute | solution.py:607
  1136.8 94.7 %collective-permute-start.35 = (bf16[1280,1536]{1,0:T(8,128)(2,1)}, bf16[1280,1536]{1,0:T(8,128)(2,1)}, u32[]{:S(2)}, u32[]{:S(2)}) collective-permute-start(bf16[1280,1536]{1,0:T(8,128)(2,1)} %weight_grad.10), channel_id=1, source_target_pairs={{0,16},{16,0},{1,17},{17,1},{2,18},{18,2},{3,19},{19,3},{4,20},{20... | collective-permute-start | bytes 11796488 | tf_op jit(solution)/shard_map/ppermute | solution.py:750
  1147.2 162.0 %collective-permute-start.40 = (bf16[1280,1536]{1,0:T(8,128)(2,1)}, bf16[1280,1536]{1,0:T(8,128)(2,1)}, u32[]{:S(2)}, u32[]{:S(2)}) collective-permute-start(bf16[1280,1536]{1,0:T(8,128)(2,1)} %weight_grad.11), channel_id=1, source_target_pairs={{0,16},{16,0},{1,17},{17,1},{2,18},{18,2},{3,19},{19,3},{4,20},{20... | collective-permute-start | bytes 11796488 | tf_op jit(solution)/shard_map/ppermute | solution.py:750
  1186.5 206.5 %collective-permute-start.43 = (bf16[1536,1280]{1,0:T(8,128)(2,1)}, bf16[1536,1280]{1,0:T(8,128)(2,1)}, u32[]{:S(2)}, u32[]{:S(2)}) collective-permute-start(bf16[1536,1280]{1,0:T(8,128)(2,1)} %weight_grad.12), channel_id=1, source_target_pairs={{0,16},{16,0},{1,17},{17,1},{2,18},{18,2},{3,19},{19,3},{4,20},{20... | collective-permute-start | bytes 11796488 | tf_op jit(solution)/shard_map/ppermute | solution.py:750
  1418.3 70.1 %collective-permute-start.44 = (bf16[2,8,80,2560]{3,2,1,0:T(8,128)(2,1)}, bf16[2,8,80,2560]{3,2,1,0:T(8,128)(2,1)}, u32[]{:S(2)}, u32[]{:S(2)}) collective-permute-start(bf16[2,8,80,2560]{3,2,1,0:T(8,128)(2,1)} %dynamic-slice_bitcast_fusion), channel_id=1, source_target_pairs={{0,1},{1,0},{2,3},{3,2},{4,5},{5,4},{6,7},{7,6},{8,9},{9,8},{10,11... | collective-permute-start | bytes 19660808 | tf_op jit(solution)/shard_map/ppermute | solution.py:607
  1583.0 223.5 %collective-permute-start.49 = (bf16[1280,512]{1,0:T(8,128)(2,1)}, bf16[1280,512]{1,0:T(8,128)(2,1)}, u32[]{:S(2)}, u32[]{:S(2)}) collective-permute-start(bf16[1280,512]{1,0:T(8,128)(2,1)} %weight_grad.13), channel_id=1, source_target_pairs={{0,16},{16,0},{1,17},{17,1},{2,18},{18,2},{3,19},{19,3},{4,20},{20... | collective-permute-start | bytes 3932168 | tf_op jit(solution)/shard_map/ppermute | solution.py:750
  1583.6 245.8 %collective-permute-start.52 = (bf16[128,2560]{1,0:T(8,128)(2,1)}, bf16[128,2560]{1,0:T(8,128)(2,1)}, u32[]{:S(2)}, u32[]{:S(2)}) collective-permute-start(bf16[128,2560]{1,0:T(8,128)(2,1)} %weight_grad.14), channel_id=1, source_target_pairs={{0,16},{16,0},{1,17},{17,1},{2,18},{18,2},{3,19},{19,3},{4,20},{20... | collective-permute-start | bytes 1966088 | tf_op jit(solution)/shard_map/ppermute | solution.py:750
  1598.7 174.7 %collective-permute-start.46 = (bf16[8,80,2560]{2,1,0:T(8,128)(2,1)}, bf16[8,80,2560]{2,1,0:T(8,128)(2,1)}, u32[]{:S(2)}, u32[]{:S(2)}) collective-permute-start(bf16[8,80,2560]{2,1,0:T(8,128)(2,1)} %dynamic-slice_bitcast_fusion.1), channel_id=1, source_target_pairs={{0,16},{16,0},{1,17},{17,1},{2,18},{18,2},{3,19},{19,3},{4,20},{20... | collective-permute-start | bytes 9830408 | tf_op jit(solution)/shard_map/ppermute | solution.py:750
  1834.4 60.2 %all-to-all-start.1 = ((bf16[16,80,512]{2,1,0:T(8,128)(2,1)}), bf16[16,80,512]{2,1,0:T(8,128)(2,1)}, u32[]{:S(2)}, u32[]{:S(2)}) async-start(bf16[16,80,512]{2,1,0:T(8,128)(2,1)} %bitcast.236), calls=%async_computation.2 | async-start | bytes 2621440 | tf_op jit(solution)/shard_map/all_to_all | solution.py:1063
  (132 other events, 2546.7 us)
Sparse Core Ops, SparseCore 0:
  11.6 154.1 all-gather.4
  168.6 101.8 all-gather.6
  286.5 205.7 all-gather.8
  493.7 213.5 all-gather.10
  1533.1 203.6 reduce-scatter.1

commit v3 on v2

--- a/solution.py
+++ b/solution.py
@@ -17,7 +17,7 @@
 QUERY_WIDTH = QUERY_HEADS * HEAD_SIZE
 KEY_WIDTH = KEY_VALUE_HEADS * HEAD_SIZE
 KERNEL_VMEM = 56 * 1024 * 1024
-COMBINE_VMEM = 36 * 1024 * 1024
+COMBINE_VMEM = 60 * 1024 * 1024
 
 
 norm_eps = 1e-05
@@ -244,7 +244,7 @@
 def enter_kernel(slot_ref, rows_ref, weight_ref, picked_ref, act_ref, slope_ref):
     hidden = act_ref.shape[2]
     for chunk in row_chunks(rows_ref.shape[1]):
-        product = dot32(rows_ref[0, chunk, :], weight_ref[...])
+        product = dot_t(rows_ref[0, chunk, :], weight_ref[...])
         act, slope, silu_val = silu_parts(product[:, :hidden], product[:, hidden:])
         act_ref[0, chunk, :] = act
         slope_ref[0, chunk, :hidden] = slope
@@ -255,7 +255,7 @@
 
 def enter(slot_rows, rows, weight, capacity):
     count, tokens, width = rows.shape
-    hidden = weight.shape[1] // 2
+    hidden = weight.shape[0] // 2
     block = lambda a, b: pl.BlockSpec((1, a, b), lambda i: (i, 0, 0))
     return pl.pallas_call(
         enter_kernel,
@@ -346,39 +346,76 @@
     )(rows, gate, up)
 
 
-def expert_back_kernel(rows_ref, weight_ref, slope_ref, silu_ref, *rest):
+def expert_out_kernel(part_ref, act_ref, own_ref, other_ref, out_ref):
+    for half, weight_ref in enumerate((own_ref, other_ref)):
+
+        @pl.when(pl.program_id(0) == half)
+        def _(weight_ref=weight_ref):
+            out_ref[...] = dot32(act_ref[...], weight_ref[...]).astype(jnp.bfloat16)
+
+
+def expert_out(parts, act, own, other):
+    count, hidden = act.shape
+    half = own.shape[1]
+    high = min(count, 1024)
+    whole = pl.BlockSpec((hidden, half), lambda h, m, p: (0, 0))
+    return pl.pallas_call(
+        expert_out_kernel,
+        grid_spec=pltpu.PrefetchScalarGridSpec(
+            num_scalar_prefetch=1,
+            grid=(2, count // high),
+            in_specs=[pl.BlockSpec((high, hidden), lambda h, m, p: (m, 0)), whole, whole],
+            out_specs=pl.BlockSpec((high, half), lambda h, m, p: (m, p[h])),
+        ),
+        out_shape=jax.ShapeDtypeStruct((count, 2 * half), jnp.bfloat16),
+        compiler_params=kernel_params(),
+        cost_estimate=cost(4 * count * hidden * half, 2 * count * (2 * hidden + 2 * half)),
+        name="expert_out",
+    )(parts, act, own, other)
+
+
+def expert_back_kernel(
+    part_ref, own_rows_ref, other_rows_ref, own_ref, other_ref, slope_ref, silu_ref, *rest
+):
     gate_out, up_out = rest[-2:]
-    for chunk in row_chunks(rows_ref.shape[0]):
-        product = dot_t(rows_ref[chunk, :], weight_ref[...])
+    for chunk in row_chunks(own_rows_ref.shape[0]):
+        product = dot_t(own_rows_ref[chunk, :], own_ref[...])
+        product = product + dot_t(other_rows_ref[chunk, :], other_ref[...])
         slope = slope_ref[chunk, :].astype(jnp.float32)
         silu_val = silu_ref[chunk, :].astype(jnp.float32)
         gate_out[chunk, :] = (product * slope).astype(jnp.bfloat16)
         up_out[chunk, :] = (product * silu_val).astype(jnp.bfloat16)
 
 
-def expert_back(rows, weight, slope, silu_val, half, earlier=()):
+def expert_back(parts, rows, own, other, slope, silu_val, half, earlier=()):
     count, width = rows.shape
-    hidden = weight.shape[0]
+    hidden = own.shape[0]
     high, wide = min(count // 2, 1024), 512
     first = half * (count // 2 // high)
-    tile = pl.BlockSpec((high, wide), lambda m, n: (first + m, n))
+    tile = pl.BlockSpec((high, wide), lambda m, n, p: (first + m, n))
+    weight = pl.BlockSpec((wide, width // 2), lambda m, n, p: (n, 0))
     return pl.pallas_call(
         expert_back_kernel,
-        grid=(count // 2 // high, hidden // wide),
-        in_specs=[
-            pl.BlockSpec((high, width), lambda m, n: (first + m, 0)),
-            pl.BlockSpec((wide, width), lambda m, n: (n, 0)),
-            tile,
-            tile,
-        ]
-        + [pl.BlockSpec(memory_space=pl.ANY)] * len(earlier),
-        out_specs=[tile, tile],
+        grid_spec=pltpu.PrefetchScalarGridSpec(
+            num_scalar_prefetch=1,
+            grid=(count // 2 // high, hidden // wide),
+            in_specs=[
+                pl.BlockSpec((high, width // 2), lambda m, n, p: (first + m, p[0])),
+                pl.BlockSpec((high, width // 2), lambda m, n, p: (first + m, p[1])),
+                weight,
+                weight,
+                tile,
+                tile,
+            ]
+            + [pl.BlockSpec(memory_space=pl.ANY)] * len(earlier),
+            out_specs=[tile, tile],
+        ),
         out_shape=[jax.ShapeDtypeStruct((count, hidden), jnp.bfloat16)] * 2,
-        input_output_aliases={4 + i: i for i in range(len(earlier))},
+        input_output_aliases={7 + i: i for i in range(len(earlier))},
         compiler_params=kernel_params(),
         cost_estimate=cost(count * width * hidden, count * (width + 4 * hidden)),
         name="expert_back",
-    )(rows, weight, slope, silu_val, *earlier)
+    )(parts, rows, rows, own, other, slope, silu_val, *earlier)
 
 
 def expert_rows_kernel(gate_grad_ref, up_grad_ref, gate_ref, up_ref, *rest):
@@ -475,12 +512,12 @@
     units, info, rows, act, weight, scaled, arrived=(), partner=(), own=(), kind="units",
     out_dtype=jnp.bfloat16,
 ):
-    count = units.shape[0]
+    units, first, count = units
     tokens = info.shape[1]
     width, hidden = weight.shape[1], act.shape[2]
     capacity = rows[0].shape[1]
     columns = width // 2
-    unit_block = lambda array: pl.BlockSpec((1,) + array.shape[1:], lambda i, u: (u[i], 0, 0))
+    unit_block = lambda array: pl.BlockSpec((1,) + array.shape[1:], lambda i, u: (u[first + i], 0, 0))
     fixed = pl.BlockSpec((1, tokens, columns), lambda i, u: (0, 0, 0))
     half = pl.BlockSpec((1, tokens, columns), lambda i, u: (0, 0, i % 2))
     in_specs = [
@@ -490,10 +527,10 @@
     ]
     block = (1, capacity, columns)
     if len(rows) == 1:
-        in_specs.append(pl.BlockSpec(block, lambda i, u: (u[i], 0, i % 2)))
+        in_specs.append(pl.BlockSpec(block, lambda i, u: (u[first + i], 0, i % 2)))
     else:
-        in_specs.append(pl.BlockSpec(block, lambda i, u: (u[i - i % 2], 0, 0)))
-        in_specs.append(pl.BlockSpec(block, lambda i, u: (u[i - i % 2 + 1], 0, 0)))
+        in_specs.append(pl.BlockSpec(block, lambda i, u: (u[first + i - i % 2], 0, 0)))
+        in_specs.append(pl.BlockSpec(block, lambda i, u: (u[first + i - i % 2 + 1], 0, 0)))
     in_specs += [fixed] * len(arrived)
     added = [array for array, _ in partner] + list(own)
     for _, at in partner:
@@ -587,7 +624,7 @@
         index = lax.axis_index("exp")
         self.core = index % 2
         self.place = jnp.asarray(place_of)[index // 2]
-        self.ring = jnp.asarray(np.array(ring, np.int32))
+        self.ring = np.array(ring, np.int32)
         self.swap = [(i, i ^ 1) for i in range(exp_count)]
         self.ways = ([], [])
         for at in range(self.chips):
@@ -596,9 +633,11 @@
                 self.ways[0].append((here, there))
                 self.ways[1].append((there, here))
 
-    def targets(self, step):
-        at = jnp.stack([self.place - step + self.chips, self.place + step]) % self.chips
-        return self.ring[at]
+    def table(self):
+        steps = np.arange(1, self.chips + 1)[None, :, None]
+        places = np.arange(self.chips)[:, None, None]
+        at = np.concatenate([places - steps, places + steps], axis=2) % self.chips
+        return jnp.asarray(self.ring[at].reshape(self.chips, -1), jnp.int32)[self.place]
 
     def move(self, totals):
         return [lax.ppermute(total, "exp", way) for total, way in zip(totals, self.ways)]
@@ -613,21 +652,15 @@
         self.line = ChipRing()
         self.arrived, self.step = (), 0
         self.swapped, self.partner = [], []
-        edges = list(late_from) + [self.line.chips + 1]
-        first = part(self.other_units(range(1, 2)))[0]
-        first, units = tie(first, self.other_units(range(2, edges[0])))
+        self.late_from = list(late_from) + [self.line.chips + 1]
+        chips = self.line.table() * 2
+        self.own_units, other = chips + self.line.core, chips + 1 - self.line.core
+        first = part((other, 0, 2))[0]
+        first, other = tie(first, other)
         self.take(first)
-        second = part(units)[0]
-        second, self.late_units = tie(
-            second, [self.other_units(range(*edge)) for edge in zip(edges, edges[1:])]
-        )
+        second = part((other, 2, 2 * (self.late_from[0] - 2)))[0]
+        second, self.late_units = tie(second, other)
         self.take(second)
-
-    def units(self, step, core):
-        return (self.line.targets(step) * 2 + core).astype(jnp.int32)
-
-    def other_units(self, steps):
-        return jnp.concatenate([self.units(step, 1 - self.line.core) for step in steps])
 
     def take(self, total):
         self.partner += [(len(self.swapped), 2 * i) for i in range(total.shape[0] // 2)]
@@ -637,13 +670,14 @@
         group, at = self.partner[step - 1]
         return ((self.swapped[group], at),)
 
-    def late(self, units):
-        return self.part(units)[0]
+    def late(self, which, units):
+        start, end = self.late_from[which : which + 2]
+        return self.part((units, 2 * (start - 1), 2 * (end - start)))[0]
 
     def totals(self):
         self.step += 1
         return self.part(
-            self.units(self.step, self.line.core),
+            (self.own_units, 2 * (self.step - 1), 2),
             arrived=self.arrived,
             partner=self.from_partner(self.step),
             kind="ways",
@@ -651,7 +685,7 @@
 
     def finish(self):
         return self.part(
-            self.units(self.line.chips, self.line.core),
+            (self.own_units, 2 * (self.line.chips - 1), 2),
             arrived=self.arrived,
             partner=self.from_partner(self.line.chips),
             own=self.own,
@@ -684,21 +718,28 @@
     def add(self, *values):
         return sum(value.astype(jnp.float32) for value in values)
 
+    def cores_done(self):
+        own = self.pick(self.term, self.line.core, 2)
+        return self.add(own, self.arrived).astype(jnp.bfloat16)
+
+    def ctx_start(self, value):
+        self.value = value
+        return ctx_send(self.pick(value, 1 - lax.axis_index("ctx"), 0), 0)
+
     def ctx_done(self, arrived):
-        value = self.add(self.pick(self.term, self.line.core, 2), arrived).astype(jnp.bfloat16)
-        index = lax.axis_index("ctx")
-        arrived = ctx_send(self.pick(value, 1 - index, 0), 0)
-        return self.add(self.pick(value, index, 0), arrived).astype(jnp.bfloat16)
+        own = self.pick(self.value, lax.axis_index("ctx"), 0)
+        return self.add(own, arrived).astype(jnp.bfloat16)
 
     def finish(self, value, pieces):
         done = []
+        targets = self.line.table()
         columns = value.shape[2] // 2
         halves = [value[..., :columns], value[..., columns:]]
         arrived = ([], [])
         for step in range(1, self.line.chips + 1):
-            targets = self.line.targets(step)
             totals = [
-                self.add(self.pick(halves[way], targets[way], 0), *arrived[way]) for way in range(2)
+                self.add(self.pick(halves[way], targets[2 * (step - 1) + way], 0), *arrived[way])
+                for way in range(2)
             ]
             if step == self.line.chips:
                 return jnp.concatenate(totals, axis=1), done
@@ -847,8 +888,8 @@
 
     inverse_one = rms_scale(input_rows)
     normed_one = (input_rows * inverse_one * attn_gain).astype(jnp.bfloat16)
-    full_in, normed_one, shared_in, shared_in_t, shared_out_w = tie(
-        full_in, normed_one, shared_in, shared_in_t, shared_out_w
+    full_in, normed_one, shared_in_t, shared_out_w = tie(
+        full_in, normed_one, shared_in_t, shared_out_w
     )
     output_weight, full_in = tie(output_weight, full_in)
     full_output = lax.all_gather(output_weight, both, axis=0, tiled=True)
@@ -882,12 +923,17 @@
     def flat(rows):
         return rows.reshape(rows.shape[0] * rows.shape[1], rows.shape[2])
 
-    received, shared_act, shared_slope = enter(slot_rows, blocks(rows_all), shared_in, capacity)
+    received, shared_act, shared_slope = enter(slot_rows, blocks(rows_all), shared_in_t, capacity)
     received = flat(received)
     expert_act, expert_slope, expert_silu = expert_in(received, gate_w, up_w)
     expert_act, down_other = tie(expert_act, down_other)
-    down_w = ctx_join(down_part, down_other, 1)
-    expert_rows = dot32(expert_act, down_w).astype(jnp.bfloat16)
+    if ctx_count == 2:
+        down_parts = lax.axis_index("ctx") ^ jnp.arange(2, dtype=jnp.int32)
+    else:
+        down_parts = jnp.arange(2, dtype=jnp.int32)
+        down_part = down_other[:, : MODEL_WIDTH // 2]
+        down_other = down_other[:, MODEL_WIDTH // 2 :]
+    expert_rows = expert_out(down_parts, expert_act, down_part, down_other)
 
     def slots(rows):
         return rows.reshape(exp_count, capacity, rows.shape[1])
@@ -896,7 +942,7 @@
 
     def sum_over_exp(part):
         units = jnp.repeat(jnp.arange(exp_count, dtype=jnp.int32), 2)
-        everything = part(units)[0].reshape(exp_count, 2, tokens, MODEL_WIDTH // 2)
+        everything = part((units, 0, 2 * exp_count))[0].reshape(exp_count, 2, tokens, MODEL_WIDTH // 2)
         return lax.psum_scatter(
             jnp.swapaxes(everything, 1, 2).reshape(exp_count * tokens, MODEL_WIDTH),
             "exp",
@@ -917,7 +963,6 @@
     if pair:
         out_ring = ExpRing(out_part, jnp.bfloat16, (middle[None],))
         rings = [out_ring]
-        out_ring.take(ring_step(rings, out_ring.late, out_ring.late_units[0]))
     grad_expert, shared_back = ring_step(
         rings,
         lambda *operands: enter_back(*operands, capacity),
@@ -928,20 +973,39 @@
     )
     grad_expert = flat(grad_expert)
     grad_eu = ()
+    out_late = (out_ring.late_units,) if pair else ()
+
+    def late(work, here):
+        if not (pair and here):
+            return work
+        return lambda units, *operands: (work(*operands), out_ring.late(0, units))
+
     for half in range(2):
         grad_eu = ring_step(
             rings,
-            lambda *operands: expert_back(*operands[:4], half, operands[4:]),
+            late(lambda *operands: expert_back(*operands[:6], half, operands[6:]), half == 0),
+            *out_late,
+            down_parts,
             grad_expert,
-            down_w,
+            down_part,
+            down_other,
             expert_slope,
             expert_silu,
             *grad_eu,
         )
+        if pair and half == 0:
+            grad_eu, rest = grad_eu
+            out_ring.take(rest)
+            out_late = ()
     grad_eg, grad_eu = grad_eu
     pieces = [(), ()]
+    theirs = lambda axis: lambda left, right: ctx_theirs(left, right, axis)
+    total = lambda axis: lambda left, right, arrived: ctx_total(left, right, axis, arrived)
     for column_half, half in ((0, 0), (0, 1), (1, 0), (1, 1)):
         if (column_half, half) == (1, 1):
+            down_theirs = ring_step(rings, theirs(1), expert_act, grad_expert)
+            down_theirs, grad_eg, grad_eu = tie(down_theirs, grad_eg, grad_eu)
+            down_arrived = ctx_send(down_theirs, 1)
             rings = []
         piece = ring_step(
             rings,
@@ -964,11 +1028,9 @@
         scaled=False,
     )
     shared_back = flat(shared_back)
-    theirs = lambda axis: lambda left, right: ctx_theirs(left, right, axis)
-    total = lambda axis: lambda left, right, arrived: ctx_total(left, right, axis, arrived)
     if pair:
         output = out_ring.finish()
-        grad_ring = ExpRing(grad_part, jnp.float32, late_from=(4, 6))
+        grad_ring = ExpRing(grad_part, jnp.float32, late_from=(9,))
         rings = [grad_ring]
     else:
         output = (middle + sum_over_exp(out_part)).astype(jnp.bfloat16)
@@ -976,21 +1038,12 @@
     def theirs_and_late(which, *operands):
         if not pair:
             return ring_step(rings, theirs(0), *operands)
-        result, late = ring_step(
-            rings,
-            lambda units, *operands: (theirs(0)(*operands), grad_ring.late(units)),
-            grad_ring.late_units[which],
-            *operands,
-        )
-        grad_ring.take(late)
-        return result
+        return ring_step(rings, theirs(0), *operands)
 
     gate_theirs = theirs_and_late(0, received, grad_eg)
     gate_arrived = ctx_send(gate_theirs, 0)
     up_theirs = theirs_and_late(1, received, grad_eu)
     up_arrived = ctx_send(up_theirs, 0)
-    down_theirs = ring_step(rings, theirs(1), expert_act, grad_expert)
-    down_arrived = ctx_send(down_theirs, 1)
     shared_in_theirs, shared_down_theirs = ring_step(
         rings,
         lambda a, b, c, d: (ctx_theirs(a, b, 0), ctx_theirs(c, d, 0)),
@@ -1001,6 +1054,7 @@
     )
     shared_in_arrived = ctx_send(shared_in_theirs, 0)
     shared_down_arrived = ctx_send(shared_down_theirs, 0)
+    expert_down_grad = ring_step(rings, total(1), expert_act, grad_expert, down_arrived)[None]
     expert_gate_grad = ring_step(rings, total(0), received, grad_eg, gate_arrived)[None]
     if pair:
         ring_step(rings, lambda: ())
@@ -1009,30 +1063,36 @@
         grad_two = grad_ring.finish()
     else:
         grad_two = sum_over_exp(grad_part)
-    grad_two, down_arrived = tie(grad_two, down_arrived)
-
     ffn_gain_term = jnp.sum(grad_two * middle * inverse_two, axis=0)
     gain_term = jnp.pad(ffn_gain_term[:, None], ((0, 0), (0, 127))).astype(jnp.bfloat16)
     grad_middle = grad_low.astype(jnp.float32) + norm_back(grad_two, middle, inverse_two, ffn_gain)
     grad_middle_low = grad_middle.astype(jnp.bfloat16)
-    output_term = t_dot(grad_middle_low, attended_low).astype(jnp.bfloat16)
+    middle_column = QUERY_WIDTH // 2 if pair else QUERY_WIDTH
     if pair:
-        output_sum = SpreadSum(output_term)
-        attended_gradient = dot_t(grad_middle_low, full_output).astype(jnp.bfloat16)
-    else:
-        attended_gradient = dot_t(grad_middle_low, full_output).astype(jnp.bfloat16)
-        sum_o = lax.psum_scatter(output_term, both, scatter_dimension=0, tiled=True)
+        output_sum = SpreadSum(
+            t_dot(grad_middle_low, attended_low[:, middle_column:]).astype(jnp.bfloat16)
+        )
+    output_term = t_dot(grad_middle_low, attended_low[:, :middle_column]).astype(jnp.bfloat16)
+    sum_o = lax.psum_scatter(output_term, both, scatter_dimension=0, tiled=True)
+    attended_gradient = dot_t(grad_middle_low, full_output).astype(jnp.bfloat16)
+    if pair:
+        sum_o = sum_o.astype(jnp.float32)
+        swapped, attended_gradient = tie(output_sum.cores_done(), attended_gradient)
+        swapped = output_sum.ctx_start(swapped)
 
     grad_query_raw, key_terms, value_terms = attend_back(
         offset_array, query, key_value, attended_gradient, tables, key_tables
     )
+    if pair:
+        grad_query_raw, key_terms, value_terms, swapped = tie(
+            grad_query_raw, key_terms, value_terms, swapped
+        )
+        swapped = output_sum.ctx_done(swapped)
     key_value_grad = jnp.concatenate([key_terms, value_terms], axis=1)
     if pair:
         own = lax.dynamic_slice_in_dim(key_value_grad, offset, tokens, axis=0)
         other = lax.dynamic_slice_in_dim(key_value_grad, tokens - offset, tokens, axis=0)
-        other, swapped = tie(other.astype(jnp.bfloat16), output_sum.arrived)
-        key_value_raw = own + ctx_send(other, 0).astype(jnp.float32)
-        swapped = output_sum.ctx_done(swapped)
+        key_value_raw = own + ctx_send(other.astype(jnp.bfloat16), 0).astype(jnp.float32)
     else:
         key_value_raw = ctx_send(key_value_grad.astype(jnp.bfloat16), 0)
     key_value_raw = key_value_raw.astype(jnp.bfloat16)
@@ -1049,17 +1109,16 @@
     attn_gain_grad = jnp.sum(sum_in[:, :edge] * attn_in.astype(jnp.float32), axis=1) / own_gain
 
     rest = [
-        ((expert_act, grad_expert, down_arrived), total(1)),
         ((rows_all, shared_back, shared_in_arrived), total(0)),
         ((shared_act, grad_all, shared_down_arrived), total(0)),
     ]
     if pair:
-        sum_o, rest = output_sum.finish(swapped, rest)
+        other_sum, rest = output_sum.finish(swapped, rest)
+        sum_o = jnp.concatenate([sum_o, other_sum], axis=1)
     else:
         rest = [work(*operands) for operands, work in rest]
-    expert_down_grad = rest[0][None]
-    shared_in_grad = rest[1].astype(jnp.bfloat16)
-    sum_sd = rest[2][:own_hidden]
+    shared_in_grad = rest[0].astype(jnp.bfloat16)
+    sum_sd = rest[1][:own_hidden]
     shared_in_grad = lax.all_to_all(
         shared_in_grad.reshape(exp_count, own_rows, 2 * padded),
         "exp",

time: 1930 us -> 1790 us (0.927)
  waiting for transfers between devices: 661 us -> 519 us
  Pallas kernels: 806 us -> 885 us
  local copies, waits for them, and re-layouts: 140 us -> 94.7 us
  matrix products: 92.3 us -> 54.8 us
    ppermute x7, waiting for transfers between devices: 217 us -> 35.2 us  [ctx_send(): return lax.ppermute(theirs, 'ctx', [(0, 1), (1, 0)])]
    reduce_scatter x1, waiting for transfers between devices: 0.01 us -> 50 us  [on_device(): lax.psum_scatter(in_term, both, scatter_dimension=0, tiled=True)]
    pallas_call x2 -> x3, Pallas kernels: 51.6 us -> 93.5 us  [the longest x2 53 us: expert_back(): pl.pallas_call(expert_back_kernel, grid_spec=pltpu.PrefetchScalarGridSpec...]
    dot_general x3 -> x2, matrix products: 51.2 us -> 11.3 us  [dot32(): return jnp.dot(left, right, preferred_element_type=jnp.float32)]
    pallas_call x23 -> x21, Pallas kernels: 167 us -> 194 us  [combine(): pl.pallas_call(functools.partial(combine_kernel, scaled, len(rows), len(a...]
    unnamed x175 -> x157, local copies, waits for them, and re-layouts: 56.3 us -> 41.9 us
  transfers between devices with their start and end apart: 70 -> 69, of which waited for: 38 -> 37; matrix products, arithmetic and copies ran while one was open for 12% -> 8% of each run, Pallas kernels for 38% -> 44%
where the time goes in v3:
time: 1790 us; the launch traced here: 1770 us
  Pallas kernels  885 us (49%)
  waiting for transfers between devices  519 us (29%)
  local copies, waits for them, and re-layouts  94.7 us (5%)
  starting transfers between devices  93.9 us (5%)
  other arithmetic  73.8 us (4%)
  matrix products  54.8 us (3%)
  between operations  48.2 us (3%)
    pallas_call x10, Pallas kernels, weight_grad(): pl.pallas_call(weight_grad_kernel, grid_spec=pltpu.PrefetchScalarGridSpec...  233 us
    ppermute x6, waiting for transfers between devices, ctx_fetch(): return lax.ppermute(part, 'ctx', [(0, 1), (1, 0)])  196 us
    pallas_call x21, Pallas kernels, combine(): pl.pallas_call(functools.partial(combine_kernel, scaled, len(rows), len(a...  194 us
    pallas_call x4, Pallas kernels, expert_grad_rows(): pl.pallas_call(expert_rows_kernel, grid=(count // 2 // high,), in_specs=[...  91 us
    pallas_call x1, Pallas kernels, expert_in(): pl.pallas_call(expert_in_kernel, grid=(count // high, hidden // wide), in...  75.7 us
    ppermute x42, waiting for transfers between devices, move(): lax.ppermute(total, 'exp', way)  70.7 us
    ppermute x42, starting transfers between devices, move(): lax.ppermute(total, 'exp', way)  63 us
    all_gather x1, waiting for transfers between devices, on_device(): lax.all_gather(jnp.concatenate([attn_in, routing.reshape(own_rows, routin...  60.5 us
  transfers between devices with their start and end apart: 69, of which 37 were waited for; matrix products, arithmetic and copies ran while one was open for 8% of the time, Pallas kernels for 44%

profile of v3, /device:TPU:0, one launch (start us, length us, event | category | flops | bytes accessed | tf_op | source)
XLA Modules:
  0.0 1769.7 jit_solution(4152673586645084379)
XLA Ops:
  33.7 26.0 %all-to-all-done = bf16[16,80,384]{2,1,0:T(8,128)(2,1)} async-done(((bf16[16,80,384]{2,1,0:T(8,128)(2,1)}), bf16[16,80,384]{2,1,0:T(8,128)(2,1)}, u32[]{:S(2)}, u32[]{:S(2)}) %all-to-all-start) | async-done | bytes 983072 | tf_op jit(solution)/shard_map/all_to_all | solution.py:866
  74.2 31.0 %collective-permute-done = bf16[1280,512]{0,1:T(8,128)(2,1)S(1)} collective-permute-done((bf16[1280,512]{0,1:T(8,128)(2,1)S(1)}, bf16[1280,512]{0,1:T(8,128)(2,1)S(1)}, u32[]{:S(2)}, u32[]{:S(2)}) %collective-permute-start) | collective-permute-done | bytes 1310752 | tf_op jit(solution)/shard_map/ppermute | solution.py:760
  105.6 60.5 %all-gather.5.cloned.1.call-done.weight_ref = bf16[2560,3712]{1,0:T(8,128)(2,1)} async-done(((bf16[80,3712]{1,0:T(8,128)(2,1)}), bf16[2560,3712]{1,0:T(8,128)(2,1)}) %all-gather.5.cloned.1.call-update) | async-done | bytes 19005456 | tf_op jit(solution)/shard_map/all_gather | solution.py:842
  209.5 29.0 %attend.1 = bf16[512,2560]{1,0:T(8,128)(2,1)} custom-call(s32[1]{0:T(128)} %bitcast.3.offset_ref, bf16[512,2560]{1,0:T(8,128)(2,1)} %project.2.query_ref, bf16[1024,1024]{1,0:T(8,128)(2,1)} %copy-done.23, bf16[1024,1024]{1,0:T(8,128)(2,1)} %copy-done.23), custom_call_target="tpu_custom_call" | custom-call | flops 5368709120 | bytes 7340032 | tf_op jit(solution)/shard_map/attend/pallas_call | solution.py:138
  238.6 32.1 %all-gather.7.cloned.1.call-done = bf16[2560,2560]{1,0:T(8,128)(2,1)} async-done(((bf16[80,2560]{1,0:T(8,128)(2,1)}), bf16[2560,2560]{1,0:T(8,128)(2,1)}) %all-gather.7.cloned.1.call-update) | async-done | bytes 13107216 | tf_op jit(solution)/shard_map/all_gather | solution.py:895
  298.6 75.8 %collective-permute-done.3 = bf16[1280,1536]{1,0:T(8,128)(2,1)} collective-permute-done((bf16[1280,1536]{1,0:T(8,128)(2,1)}, bf16[1280,1536]{1,0:T(8,128)(2,1)}, u32[]{:S(2)}, u32[]{:S(2)}) %collective-permute-start.3) | collective-permute-done | bytes 3932192 | tf_op jit(solution)/shard_map/ppermute | solution.py:760
  385.7 72.3 %collective-permute-done.4 = bf16[1280,1536]{1,0:T(8,128)(2,1)} collective-permute-done((bf16[1280,1536]{1,0:T(8,128)(2,1)}, bf16[1280,1536]{1,0:T(8,128)(2,1)}, u32[]{:S(2)}, u32[]{:S(2)}) %collective-permute-start.4) | collective-permute-done | bytes 3932192 | tf_op jit(solution)/shard_map/ppermute | solution.py:760
  498.0 48.5 %enter.1 = (bf16[16,256,2560]{2,1,0:T(8,128)(2,1)}, bf16[16,512,256]{2,1,0:T(8,128)(2,1)}, bf16[16,512,512]{2,1,0:T(8,128)(2,1)}) custom-call(f32[16,2,512]{2,1,0:T(2,128)} %pad_maximum_fusion.10.slot_ref, bf16[16,512,2560]{2,1,0:T(8,128)(2,1)} %bitcast.208, bf16[512,2560]{1,0:T(8,128)(2,1)} %bitcast.197), custom_call_target="tpu_custom_call" | custom-call | flops 32212254720 | bytes 62914560 | tf_op jit(solution)/shard_map/enter/pallas_call | solution.py:260
  546.5 75.7 %expert_in.1 = (bf16[4096,1536]{1,0:T(8,128)(2,1)}, bf16[4096,1536]{1,0:T(8,128)(2,1)}, bf16[4096,1536]{1,0:T(8,128)(2,1)}) custom-call(bf16[4096,2560]{1,0:T(8,128)(2,1)} %bitcast.231, bf16[2560,1536]{1,0:T(8,128)(2,1)} %constant_dynamic-update-slice_fusion.1.gate_ref, bf16[2560,1536]{1,0:T(8,128)(2,1)} %constant_dynamic-update-slice_fusion.up_ref), custom_call_target="tpu_custom_call" | custom-call | flops 64424509440 | bytes 58720256 | tf_op jit(solution)/shard_map/expert_in/pallas_call | solution.py:337
  624.1 40.5 %expert_out.1 = bf16[4096,2560]{1,0:T(8,128)(2,1)} custom-call(s32[2]{0:T(128)} %iota_xor_fusion.part_ref, bf16[4096,1536]{1,0:T(8,128)(2,1)} %get-tuple-element.421.act_ref.left_ref, bf16[1536,1280]{1,0:T(8,128)(2,1)} %bitcast.213, bf16[1536,1280]{1,0:T(8,128)(2,1)} %copy-done.9), custom_call_target="tpu_custom_call" | custom-call | flops 32212254720 | bytes 46137344 | tf_op jit(solution)/shard_map/expert_out/pallas_call | solution.py:362
  703.2 36.5 %enter_back.1 = (bf16[16,256,2560]{2,1,0:T(8,128)(2,1)}, bf16[16,512,512]{2,1,0:T(8,128)(2,1)}) custom-call(f32[16,2,512]{2,1,0:T(2,128)} %pad_maximum_fusion.10.slot_ref, bf16[16,512,2560]{2,1,0:T(8,128)(2,1)} %bitcast.209, bf16[256,2560]{1,0:T(8,128)(2,1)} %copy-done.1, bf16[16,512,512]{2,1,0:T(8,128)(2,1)} %get-tuple-element.281.slope_ref), custom_call_target="tpu_custom_call" | custom-call | flops 21474836480 | bytes 62914560 | tf_op jit(solution)/shard_map/enter_back/pallas_call | solution.py:301
  768.2 26.5 %expert_back.2 = (bf16[4096,1536]{1,0:T(8,128)(2,1)}, bf16[4096,1536]{1,0:T(8,128)(2,1)}) custom-call(s32[2]{0:T(128)} %iota_xor_fusion.part_ref, bf16[4096,2560]{1,0:T(8,128)(2,1)} %bitcast.191, bf16[4096,2560]{1,0:T(8,128)(2,1)} %bitcast.192, bf16[1536,1280]{1,0:T(8,128)(2,1)} %bitcast.214, bf16[1536,1280]{1,0:T(8,128)(2,1)} %copy-done.9, ...), custom_call_target="tpu_custom_call" | custom-call | flops 16106127360 | bytes 35651584 | tf_op jit(solution)/shard_map/expert_back/pallas_call | solution.py:397
  805.8 26.5 %expert_back.3 = (bf16[4096,1536]{1,0:T(8,128)(2,1)}, bf16[4096,1536]{1,0:T(8,128)(2,1)}) custom-call(s32[2]{0:T(128)} %iota_xor_fusion.part_ref, bf16[4096,2560]{1,0:T(8,128)(2,1)} %bitcast.193, bf16[4096,2560]{1,0:T(8,128)(2,1)} %bitcast.194, bf16[1536,1280]{1,0:T(8,128)(2,1)} %bitcast.215, ...), custom_call_target="tpu_custom_call", output_to_operand_aliasing={{0}: (7, {}), {1}: (8, {})} | custom-call | flops 16106127360 | bytes 35651584 | tf_op jit(solution)/shard_map/expert_back/pallas_call | solution.py:397
  958.8 25.1 %weight_grad.10 = bf16[1536,1280]{1,0:T(8,128)(2,1)} custom-call(s32[1]{0:T(128)} %bitcast.24.part_ref, bf16[4096,1536]{1,0:T(8,128)(2,1)} %get-tuple-element.421.act_ref.left_ref, bf16[4096,2560]{1,0:T(8,128)(2,1)} %bitcast.195), custom_call_target="tpu_custom_call" | custom-call | flops 16106127360 | bytes 30932992 | tf_op jit(solution)/shard_map/weight_grad/pallas_call | solution.py:590
  1013.7 30.3 %combine.34 = bf16[14,512,1280]{2,1,0:T(8,128)(2,1)} custom-call(s32[16]{0:T(128)} %get-tuple-element.389.unit_ref, f32[16,512,128]{2,1,0:T(8,128)} %pad.24.info_ref, bf16[16,512,512]{2,1,0:T(8,128)(2,1)} %get-tuple-element.373.act_ref, bf16[512,2560]{1,0:T(8,128)(2,1)} %bitcast.199, bf16[16,256,1280]{2,1,0:T(8,128)(2,1)} %bitcast.178, ...), custom_call_target="tpu_custom_call" | custom-call | flops 14092861440 | bytes 27525120 | tf_op jit(solution)/shard_map/combine/pallas_call | solution.py:547
  1066.8 24.9 %weight_grad.11 = bf16[1280,1536]{1,0:T(8,128)(2,1)} custom-call(s32[1]{0:T(128)} %bitcast.24.part_ref, bf16[4096,2560]{1,0:T(8,128)(2,1)} %bitcast.232, bf16[4096,1536]{1,0:T(8,128)(2,1)} %get-tuple-element.433.gate_grad_ref.right_ref), custom_call_target="tpu_custom_call" | custom-call | flops 16106127360 | bytes 30932992 | tf_op jit(solution)/shard_map/weight_grad/pallas_call | solution.py:590
  1110.4 25.1 %weight_grad.12 = bf16[1280,1536]{1,0:T(8,128)(2,1)} custom-call(s32[1]{0:T(128)} %bitcast.24.part_ref, bf16[4096,2560]{1,0:T(8,128)(2,1)} %bitcast.233, bf16[4096,1536]{1,0:T(8,128)(2,1)} %get-tuple-element.449.up_grad_ref.right_ref), custom_call_target="tpu_custom_call" | custom-call | flops 16106127360 | bytes 30932992 | tf_op jit(solution)/shard_map/weight_grad/pallas_call | solution.py:590
  1200.2 28.3 %weight_grad.15 = f32[1536,1280]{1,0:T(8,128)} custom-call(s32[1]{0:T(128)} %bitcast.30.part_ref, bf16[4096,1536]{1,0:T(8,128)(2,1)} %get-tuple-element.421.act_ref.left_ref, bf16[4096,2560]{1,0:T(8,128)(2,1)} %bitcast.196, bf16[1536,1280]{1,0:T(8,128)(2,1)} %collective-permute-done.31.rest_0_), custom_call_target="tpu_custom_call" | custom-call | flops 16106127360 | bytes 30932992 | tf_op jit(solution)/shard_map/weight_grad/pallas_call | solution.py:590
  1241.1 27.8 %weight_grad.16 = f32[1280,1536]{1,0:T(8,128)} custom-call(s32[1]{0:T(128)} %bitcast.30.part_ref, bf16[4096,2560]{1,0:T(8,128)(2,1)} %bitcast.234, bf16[4096,1536]{1,0:T(8,128)(2,1)} %get-tuple-element.433.gate_grad_ref.right_ref, bf16[1280,1536]{1,0:T(8,128)(2,1)} %collective-permute-done.34.rest_0_), custom_call_target="tpu_custom_call" | custom-call | flops 16106127360 | bytes 30932992 | tf_op jit(solution)/shard_map/weight_grad/pallas_call | solution.py:590
  1281.6 25.2 %collective-permute-done.37.rest_2_ = bf16[1,512,1280]{2,1,0:T(8,128)(2,1)S(1)} collective-permute-done((bf16[1,512,1280]{2,1,0:T(8,128)(2,1)}, bf16[1,512,1280]{2,1,0:T(8,128)(2,1)S(1)}, u32[]{:S(2)}, u32[]{:S(2)}) %collective-permute-start.37) | collective-permute-done | bytes 1310752 | tf_op jit(solution)/shard_map/ppermute | solution.py:643
  1319.7 27.8 %weight_grad.17 = f32[1280,1536]{1,0:T(8,128)} custom-call(s32[1]{0:T(128)} %bitcast.30.part_ref, bf16[4096,2560]{1,0:T(8,128)(2,1)} %bitcast.235, bf16[4096,1536]{1,0:T(8,128)(2,1)} %get-tuple-element.449.up_grad_ref.right_ref, bf16[1280,1536]{1,0:T(8,128)(2,1)} %collective-permute-done.39.rest_0_), custom_call_target="tpu_custom_call" | custom-call | flops 16106127360 | bytes 30932992 | tf_op jit(solution)/shard_map/weight_grad/pallas_call | solution.py:590
  1406.9 48.4 %attend_back.1 = (bf16[512,2560]{1,0:T(8,128)(2,1)}, f32[1024,512]{1,0:T(8,128)}, f32[1024,512]{1,0:T(8,128)}) custom-call(s32[1]{0:T(128)} %bitcast.3.offset_ref, bf16[512,2560]{1,0:T(8,128)(2,1)} %project.2.query_ref, bf16[1024,1024]{1,0:T(8,128)(2,1)} %copy-done.23, bf16[1024,1024]{1,0:T(8,128)(2,1)} %copy-done.23, ...), custom_call_target="tpu_custom_call" | custom-call | flops 13421772800 | bytes 14155776 | tf_op jit(solution)/shard_map/attend_back/pallas_call | solution.py:200
  1467.3 27.8 %collective-permute-done.44 = bf16[512,1024]{1,0:T(8,128)(2,1)} collective-permute-done((bf16[512,1024]{1,0:T(8,128)(2,1)}, bf16[512,1024]{1,0:T(8,128)(2,1)}, u32[]{:S(2)}, u32[]{:S(2)}) %collective-permute-start.44) | collective-permute-done | bytes 1048608 | tf_op jit(solution)/shard_map/ppermute | solution.py:791
  1708.0 50.0 %reduce-scatter.3.cloned.1.call-done = bf16[80,3712]{1,0:T(8,128)(2,1)} async-done(((bf16[2560,3712]{1,0:T(8,128)(2,1)}), bf16[80,3712]{1,0:T(8,128)(2,1)}) %reduce-scatter.3.cloned.1.call-update) | async-done | bytes 593936 | tf_op jit(solution)/shard_map/reduce_scatter | solution.py:1105
  (431 shorter events, 800.0 us)
Async XLA Ops:
  7.2 158.9 %all-gather.5.cloned.1.call-start = ((), (), s32[]{:S(2)}) async-start(), calls=%async_computation.4 | async-start | bytes 19599360 | tf_op jit(solution)/shard_map/all_gather | solution.py:842
  30.0 240.7 %all-gather.7.cloned.1.call-start = ((), (), s32[]{:S(2)}) async-start(), calls=%async_computation.5 | async-start | bytes 13516800 | tf_op jit(solution)/shard_map/all_gather | solution.py:895
  30.9 40.7 %collective-permute-start.1 = (bf16[128,2560]{1,0:T(8,128)(2,1)}, bf16[128,2560]{1,0:T(8,128)(2,1)}, u32[]{:S(2)}, u32[]{:S(2)}) collective-permute-start(bf16[128,2560]{1,0:T(8,128)(2,1)} %pad.23), channel_id=1, source_target_pairs={{0,16},{16,0},{1,17},{17,1},{2,18},{18,2},{3,19},{19,3},{4,20},{20... | collective-permute-start | bytes 1966088 | tf_op jit(solution)/shard_map/ppermute | solution.py:760
  166.1 326.0 %all-gather.9.cloned.1.call-start = ((), (), s32[]{:S(2)}) async-start(), calls=%async_computation.6 | async-start | bytes 44564480 | tf_op jit(solution)/shard_map/all_gather | solution.py:914
  286.2 415.1 %all-gather.11.cloned.1.call-start = ((), (), s32[]{:S(2)}) async-start(), calls=%async_computation.7 | async-start | bytes 44564480 | tf_op jit(solution)/shard_map/all_gather | solution.py:918
  286.2 88.2 %collective-permute-start.3 = (bf16[1280,1536]{1,0:T(8,128)(2,1)}, bf16[1280,1536]{1,0:T(8,128)(2,1)}, u32[]{:S(2)}, u32[]{:S(2)}) collective-permute-start(bf16[1280,1536]{1,0:T(8,128)(2,1)} %bitcast.223), channel_id=1, source_target_pairs={{0,16},{16,0},{1,17},{17,1},{2,18},{18,2},{3,19},{19,3},{4,20},{20... | collective-permute-start | bytes 11796488 | tf_op jit(solution)/shard_map/ppermute | solution.py:760
  288.9 169.1 %collective-permute-start.4 = (bf16[1280,1536]{1,0:T(8,128)(2,1)}, bf16[1280,1536]{1,0:T(8,128)(2,1)}, u32[]{:S(2)}, u32[]{:S(2)}) collective-permute-start(bf16[1280,1536]{1,0:T(8,128)(2,1)} %bitcast.225), channel_id=1, source_target_pairs={{0,16},{16,0},{1,17},{17,1},{2,18},{18,2},{3,19},{19,3},{4,20},{20... | collective-permute-start | bytes 11796488 | tf_op jit(solution)/shard_map/ppermute | solution.py:760
  492.2 1213.8 %reduce-scatter.5.cloned.1.call-start = ((), (), s32[]{:S(2)}) async-start(), calls=%async_computation.9 | async-start | bytes 6758400 | tf_op jit(solution)/shard_map/reduce_scatter | solution.py:1076
  496.5 125.6 %collective-permute-start.5 = (bf16[1536,1280]{1,0:T(8,128)(2,1)}, bf16[1536,1280]{1,0:T(8,128)(2,1)S(1)}, u32[]{:S(2)}, u32[]{:S(2)}) collective-permute-start(bf16[1536,1280]{1,0:T(8,128)(2,1)} %bitcast.212), channel_id=1, source_target_pairs={{0,16},{16,0},{1,17},{17,1},{2,18},{18,2},{3,19},{19,3},{4,20},{20... | collective-permute-start | bytes 11796488 | tf_op jit(solution)/shard_map/ppermute | solution.py:760
  678.2 61.5 %collective-permute-start.9 = (bf16[4,512,1280]{2,1,0:T(8,128)(2,1)}, bf16[4,512,1280]{2,1,0:T(8,128)(2,1)}, u32[]{:S(2)}, u32[]{:S(2)}) collective-permute-start(bf16[4,512,1280]{2,1,0:T(8,128)(2,1)} %combine.23), channel_id=1, source_target_pairs={{0,1},{1,0},{2,3},{3,2},{4,5},{5,4},{6,7},{7,6},{8,9},{9,8},{10,11... | collective-permute-start | bytes 15728648 | tf_op jit(solution)/shard_map/ppermute | solution.py:646
  701.2 38.5 %collective-permute-start.7 = (bf16[1,512,1280]{2,1,0:T(8,128)(2,1)}, bf16[1,512,1280]{2,1,0:T(8,128)(2,1)S(1)}, u32[]{:S(2)}, u32[]{:S(2)}) collective-permute-start(bf16[1,512,1280]{2,1,0:T(8,128)(2,1)} %get-tuple-element.274), channel_id=1, source_target_pairs={{0,4},{1,5},{4,8},{5,9},{8,12},{9,13},{12,14},{13,15},{14,10},{15,... | collective-permute-start | bytes 3932168 | tf_op jit(solution)/shard_map/ppermute | solution.py:643
  748.9 45.7 %collective-permute-start.10 = (bf16[1,512,1280]{2,1,0:T(8,128)(2,1)}, bf16[1,512,1280]{2,1,0:T(8,128)(2,1)S(1)}, u32[]{:S(2)}, u32[]{:S(2)}) collective-permute-start(bf16[1,512,1280]{2,1,0:T(8,128)(2,1)} %get-tuple-element.293), channel_id=1, source_target_pairs={{0,4},{1,5},{4,8},{5,9},{8,12},{9,13},{12,14},{13,15},{14,10},{15,... | collective-permute-start | bytes 3932168 | tf_op jit(solution)/shard_map/ppermute | solution.py:643
  750.4 44.3 %collective-permute-start.11 = (bf16[1,512,1280]{2,1,0:T(8,128)(2,1)}, bf16[1,512,1280]{2,1,0:T(8,128)(2,1)S(1)}, u32[]{:S(2)}, u32[]{:S(2)}) collective-permute-start(bf16[1,512,1280]{2,1,0:T(8,128)(2,1)} %get-tuple-element.294), channel_id=1, source_target_pairs={{4,0},{5,1},{8,4},{9,5},{12,8},{13,9},{14,12},{15,13},{10,14},{11,... | collective-permute-start | bytes 3932168 | tf_op jit(solution)/shard_map/ppermute | solution.py:643
  794.7 40.4 %collective-permute-start.14 = (bf16[10,512,1280]{2,1,0:T(8,128)(2,1)}, bf16[10,512,1280]{2,1,0:T(8,128)(2,1)}, u32[]{:S(2)}, u32[]{:S(2)}) collective-permute-start(bf16[10,512,1280]{2,1,0:T(8,128)(2,1)} %combine.25), channel_id=1, source_target_pairs={{0,1},{1,0},{2,3},{3,2},{4,5},{5,4},{6,7},{7,6},{8,9},{9,8},{10,11... | collective-permute-start | bytes 39321608 | tf_op jit(solution)/shard_map/ppermute | solution.py:646
  1044.0 53.4 %collective-permute-start.26 = (bf16[14,512,1280]{2,1,0:T(8,128)(2,1)}, bf16[14,512,1280]{2,1,0:T(8,128)(2,1)}, u32[]{:S(2)}, u32[]{:S(2)}) collective-permute-start(bf16[14,512,1280]{2,1,0:T(8,128)(2,1)} %combine.34), channel_id=1, source_target_pairs={{0,1},{1,0},{2,3},{3,2},{4,5},{5,4},{6,7},{7,6},{8,9},{9,8},{10,11... | collective-permute-start | bytes 55050248 | tf_op jit(solution)/shard_map/ppermute | solution.py:646
  1044.5 153.6 %collective-permute-start.31 = (bf16[1536,1280]{1,0:T(8,128)(2,1)}, bf16[1536,1280]{1,0:T(8,128)(2,1)}, u32[]{:S(2)}, u32[]{:S(2)}) collective-permute-start(bf16[1536,1280]{1,0:T(8,128)(2,1)} %weight_grad.10), channel_id=1, source_target_pairs={{0,16},{16,0},{1,17},{17,1},{2,18},{18,2},{3,19},{19,3},{4,20},{20... | collective-permute-start | bytes 11796488 | tf_op jit(solution)/shard_map/ppermute | solution.py:791
  1108.9 130.2 %collective-permute-start.34 = (bf16[1280,1536]{1,0:T(8,128)(2,1)}, bf16[1280,1536]{1,0:T(8,128)(2,1)}, u32[]{:S(2)}, u32[]{:S(2)}) collective-permute-start(bf16[1280,1536]{1,0:T(8,128)(2,1)} %weight_grad.11), channel_id=1, source_target_pairs={{0,16},{16,0},{1,17},{17,1},{2,18},{18,2},{3,19},{19,3},{4,20},{20... | collective-permute-start | bytes 11796488 | tf_op jit(solution)/shard_map/ppermute | solution.py:791
  1147.9 39.8 %collective-permute-start.29 = (bf16[1,512,1280]{2,1,0:T(8,128)(2,1)}, bf16[1,512,1280]{2,1,0:T(8,128)(2,1)S(1)}, u32[]{:S(2)}, u32[]{:S(2)}) collective-permute-start(bf16[1,512,1280]{2,1,0:T(8,128)(2,1)} %get-tuple-element.407), channel_id=1, source_target_pairs={{0,4},{1,5},{4,8},{5,9},{8,12},{9,13},{12,14},{13,15},{14,10},{15,... | collective-permute-start | bytes 3932168 | tf_op jit(solution)/shard_map/ppermute | solution.py:643
  1149.2 38.4 %collective-permute-start.30 = (bf16[1,512,1280]{2,1,0:T(8,128)(2,1)}, bf16[1,512,1280]{2,1,0:T(8,128)(2,1)S(1)}, u32[]{:S(2)}, u32[]{:S(2)}) collective-permute-start(bf16[1,512,1280]{2,1,0:T(8,128)(2,1)} %get-tuple-element.408), channel_id=1, source_target_pairs={{4,0},{5,1},{8,4},{9,5},{12,8},{13,9},{14,12},{15,13},{10,14},{11,... | collective-permute-start | bytes 3932168 | tf_op jit(solution)/shard_map/ppermute | solution.py:643
  1149.9 167.7 %collective-permute-start.39 = (bf16[1280,1536]{1,0:T(8,128)(2,1)}, bf16[1280,1536]{1,0:T(8,128)(2,1)}, u32[]{:S(2)}, u32[]{:S(2)}) collective-permute-start(bf16[1280,1536]{1,0:T(8,128)(2,1)} %weight_grad.12), channel_id=1, source_target_pairs={{0,16},{16,0},{1,17},{17,1},{2,18},{18,2},{3,19},{19,3},{4,20},{20... | collective-permute-start | bytes 11796488 | tf_op jit(solution)/shard_map/ppermute | solution.py:791
  1376.4 381.6 %reduce-scatter.3.cloned.1.call-start = ((), (), s32[]{:S(2)}) async-start(), calls=%async_computation.8 | async-start | bytes 19599360 | tf_op jit(solution)/shard_map/reduce_scatter | solution.py:1105
  1403.2 52.1 %collective-permute-start.43 = (bf16[8,80,1280]{2,1,0:T(8,128)(2,1)S(1)}, bf16[8,80,1280]{2,1,0:T(8,128)(2,1)S(1)}, u32[]{:S(2)}, u32[]{:S(2)}) collective-permute-start(bf16[8,80,1280]{2,1,0:T(8,128)(2,1)S(1)} %dynamic-slice_bitcast_fusion.1), channel_id=1, source_target_pairs={{0,16},{16,0},{1,17},{17,1},{2,18},{18,2},{3,19},{19,3},{4,20},{20... | collective-permute-start | bytes 4915208 | tf_op jit(solution)/shard_map/ppermute | solution.py:791
  1513.8 51.6 %collective-permute-start.45 = (bf16[1280,512]{1,0:T(8,128)(2,1)}, bf16[1280,512]{1,0:T(8,128)(2,1)}, u32[]{:S(2)}, u32[]{:S(2)}) collective-permute-start(bf16[1280,512]{1,0:T(8,128)(2,1)} %weight_grad.13), channel_id=1, source_target_pairs={{0,16},{16,0},{1,17},{17,1},{2,18},{18,2},{3,19},{19,3},{4,20},{20... | collective-permute-start | bytes 3932168 | tf_op jit(solution)/shard_map/ppermute | solution.py:791
  1593.6 104.1 %all-to-all-start.1 = ((bf16[16,80,512]{2,1,0:T(8,128)(2,1)}), bf16[16,80,512]{2,1,0:T(8,128)(2,1)}, u32[]{:S(2)}, u32[]{:S(2)}) async-start(bf16[16,80,512]{2,1,0:T(8,128)(2,1)} %bitcast.72), calls=%async_computation.3 | async-start | bytes 2621440 | tf_op jit(solution)/shard_map/all_to_all | solution.py:1122
  (122 other events, 1968.6 us)
Sparse Core Ops, SparseCore 0:
  11.6 154.4 all-gather.4
  169.0 101.6 all-gather.6
  286.3 205.8 all-gather.8
  493.6 207.5 all-gather.10
  1376.5 144.6 reduce-scatter.4
  1523.3 234.6 reduce-scatter.2

commit v4 on v3

--- a/solution.py
+++ b/solution.py
@@ -241,10 +241,15 @@
     return slots == places
 
 
-def enter_kernel(slot_ref, rows_ref, weight_ref, picked_ref, act_ref, slope_ref):
+def enter_kernel(slot_ref, rows_ref, weight_t_ref, picked_ref, act_ref, slope_ref, weight_ref):
     hidden = act_ref.shape[2]
+
+    @pl.when(pl.program_id(0) == 0)
+    def _():
+        weight_ref[...] = weight_t_ref[...].T
+
     for chunk in row_chunks(rows_ref.shape[1]):
-        product = dot_t(rows_ref[0, chunk, :], weight_ref[...])
+        product = dot32(rows_ref[0, chunk, :], weight_ref[...])
         act, slope, silu_val = silu_parts(product[:, :hidden], product[:, hidden:])
         act_ref[0, chunk, :] = act
         slope_ref[0, chunk, :hidden] = slope
@@ -271,6 +276,7 @@
             jax.ShapeDtypeStruct((count, tokens, hidden), jnp.bfloat16),
             jax.ShapeDtypeStruct((count, tokens, 2 * hidden), jnp.bfloat16),
         ],
+        scratch_shapes=[pltpu.VMEM((width, 2 * hidden), jnp.bfloat16)],
         compiler_params=kernel_params(),
         cost_estimate=cost(
             2 * count * tokens * width * (capacity + 2 * hidden),
@@ -475,6 +481,28 @@
         cost_estimate=cost(2 * width * count * columns, 2 * width * (columns + count)),
         name="qkv_grad",
     )(rows_t, query_grad, key_value_grad, gain_term)
+
+
+def rows_grad_kernel(left_ref, right_ref, out_ref):
+    out_ref[...] = t_dot(left_ref[...], right_ref[...]).astype(jnp.bfloat16)
+
+
+def rows_grad(left, right):
+    count, high = left.shape
+    wide = right.shape[1]
+    return pl.pallas_call(
+        rows_grad_kernel,
+        grid=(high // 256,),
+        in_specs=[
+            pl.BlockSpec((count, 256), lambda m: (0, m)),
+            pl.BlockSpec((count, wide), lambda m: (0, 0)),
+        ],
+        out_specs=pl.BlockSpec((256, wide), lambda m: (m, 0)),
+        out_shape=jax.ShapeDtypeStruct((high, wide), jnp.bfloat16),
+        compiler_params=kernel_params(),
+        cost_estimate=cost(2 * count * high * wide, 2 * (count * (high + wide) + high * wide)),
+        name="rows_grad",
+    )(left, right)
 
 
 def combine_kernel(scaled, pieces, arrivals, added, unit_ref, info_ref, act_ref, weight_ref, *rest):
@@ -562,27 +590,30 @@
 def weight_grad_kernel(part_ref, left_ref, right_ref, *rest):
     *arrived_refs, out_ref, sum_ref = rest
     step = pl.program_id(0)
-    product = t_dot(left_ref[...], right_ref[...])
+    last = pl.num_programs(0) - 1
 
     @pl.when(step == 0)
     def _():
-        sum_ref[...] = product
-
-    @pl.when(step > 0)
+        for chunk in row_chunks(sum_ref.shape[0]):
+            sum_ref[chunk, :] = t_dot(left_ref[:, chunk], right_ref[...])
+
+    @pl.when((step > 0) & (step < last))
     def _():
-        sum_ref[...] += product
-
-    @pl.when(step == pl.num_programs(0) - 1)
+        for chunk in row_chunks(sum_ref.shape[0]):
+            sum_ref[chunk, :] += t_dot(left_ref[:, chunk], right_ref[...])
+
+    @pl.when((step > 0) & (step == last))
     def _():
-        total = sum_ref[...]
-        for arrived_ref in arrived_refs:
-            total = total + arrived_ref[...].astype(jnp.float32)
-        out_ref[...] = total.astype(out_ref.dtype)
+        for chunk in row_chunks(sum_ref.shape[0]):
+            total = sum_ref[chunk, :] + t_dot(left_ref[:, chunk], right_ref[...])
+            for arrived_ref in arrived_refs:
+                total = total + arrived_ref[chunk, :].astype(jnp.float32)
+            out_ref[chunk, :] = total.astype(out_ref.dtype)
 
 
 def weight_grad(left, right, axis, part, out_dtype, arrived=()):
     count = left.shape[0]
-    high = min(count, 1024)
+    high = min(count // 2, 1024)
     widths = [left.shape[1], right.shape[1]]
     widths[axis] //= 2
     at = (lambda k, p: (k, p[0]), lambda k, p: (k, 0))
@@ -660,6 +691,7 @@
         self.take(first)
         second = part((other, 2, 2 * (self.late_from[0] - 2)))[0]
         second, self.late_units = tie(second, other)
+        second, self.swapped[0] = tie(second, self.swapped[0])
         self.take(second)
 
     def take(self, total):
@@ -703,55 +735,6 @@
     for ring, arrived, ring.swapped in zip(rings, moved, swapped):
         ring.arrived = tuple(arrived)
     return result
-
-
-class SpreadSum:
-    def __init__(self, term):
-        self.line = ChipRing()
-        rows = term.shape[0] // (4 * self.line.chips)
-        self.term = term.reshape(2, self.line.chips, 2, rows, term.shape[1])
-        self.arrived = self.line.swap_cores(self.pick(self.term, 1 - self.line.core, 2))
-
-    def pick(self, array, index, axis):
-        return lax.dynamic_index_in_dim(array, index, axis, keepdims=False)
-
-    def add(self, *values):
-        return sum(value.astype(jnp.float32) for value in values)
-
-    def cores_done(self):
-        own = self.pick(self.term, self.line.core, 2)
-        return self.add(own, self.arrived).astype(jnp.bfloat16)
-
-    def ctx_start(self, value):
-        self.value = value
-        return ctx_send(self.pick(value, 1 - lax.axis_index("ctx"), 0), 0)
-
-    def ctx_done(self, arrived):
-        own = self.pick(self.value, lax.axis_index("ctx"), 0)
-        return self.add(own, arrived).astype(jnp.bfloat16)
-
-    def finish(self, value, pieces):
-        done = []
-        targets = self.line.table()
-        columns = value.shape[2] // 2
-        halves = [value[..., :columns], value[..., columns:]]
-        arrived = ([], [])
-        for step in range(1, self.line.chips + 1):
-            totals = [
-                self.add(self.pick(halves[way], targets[2 * (step - 1) + way], 0), *arrived[way])
-                for way in range(2)
-            ]
-            if step == self.line.chips:
-                return jnp.concatenate(totals, axis=1), done
-            totals = [total.astype(jnp.bfloat16) for total in totals]
-            if step <= len(pieces):
-                operands, work = pieces[step - 1]
-                totals, operands = tie(totals, operands)
-            moved = self.line.move(totals)
-            if step <= len(pieces):
-                moved, result = tie(moved, work(*operands))
-                done.append(result)
-            arrived = tuple([value] for value in moved)
 
 
 def ctx_fetch(part, axis):
@@ -912,10 +895,10 @@
     normed_two = (middle * inverse_two * ffn_gain).astype(jnp.bfloat16)
 
     rows_all = lax.all_gather(normed_two, "exp", axis=0, tiled=True)
-    rows_all, gate_w, up_w, grad_low, slot_rows, token_info = tie(
+    rows_all, gate_w, up_w, grad_sent, slot_rows, token_info = tie(
         rows_all, gate_w, up_w, grad_low, slot_rows, token_info
     )
-    grad_all = lax.all_gather(grad_low, "exp", axis=0, tiled=True)
+    grad_all = lax.all_gather(grad_sent, "exp", axis=0, tiled=True)
 
     def blocks(rows):
         return rows.reshape(exp_count, tokens, MODEL_WIDTH)
@@ -1056,8 +1039,32 @@
     shared_down_arrived = ctx_send(shared_down_theirs, 0)
     expert_down_grad = ring_step(rings, total(1), expert_act, grad_expert, down_arrived)[None]
     expert_gate_grad = ring_step(rings, total(0), received, grad_eg, gate_arrived)[None]
-    if pair:
-        ring_step(rings, lambda: ())
+    shared_in_grad, sum_sd = ring_step(
+        rings,
+        lambda a, b, c, d, e, f: (
+            ctx_total(a, b, 0, c).astype(jnp.bfloat16),
+            ctx_total(d, e, 0, f),
+        ),
+        rows_all,
+        shared_back,
+        shared_in_arrived,
+        shared_act,
+        grad_all,
+        shared_down_arrived,
+    )
+    sum_sd = sum_sd[:own_hidden]
+    shared_in_grad = lax.all_to_all(
+        shared_in_grad.reshape(exp_count, own_rows, 2 * padded),
+        "exp",
+        split_axis=0,
+        concat_axis=0,
+        tiled=True,
+    ).reshape(exp_count, own_rows, 2, ctx_count, padded_own)[..., :own_hidden]
+    shared_in_grad = (
+        jnp.transpose(shared_in_grad, (2, 1, 3, 0, 4))
+        .reshape(2, own_rows, exp_count * ctx_count * own_hidden)
+        .astype(jnp.float32)
+    )
     expert_up_grad = ring_step(rings, total(0), received, grad_eu, up_arrived)[None]
     if pair:
         grad_two = grad_ring.finish()
@@ -1067,27 +1074,13 @@
     gain_term = jnp.pad(ffn_gain_term[:, None], ((0, 0), (0, 127))).astype(jnp.bfloat16)
     grad_middle = grad_low.astype(jnp.float32) + norm_back(grad_two, middle, inverse_two, ffn_gain)
     grad_middle_low = grad_middle.astype(jnp.bfloat16)
-    middle_column = QUERY_WIDTH // 2 if pair else QUERY_WIDTH
-    if pair:
-        output_sum = SpreadSum(
-            t_dot(grad_middle_low, attended_low[:, middle_column:]).astype(jnp.bfloat16)
-        )
-    output_term = t_dot(grad_middle_low, attended_low[:, :middle_column]).astype(jnp.bfloat16)
+    output_term = rows_grad(grad_middle_low, attended_low)
     sum_o = lax.psum_scatter(output_term, both, scatter_dimension=0, tiled=True)
     attended_gradient = dot_t(grad_middle_low, full_output).astype(jnp.bfloat16)
-    if pair:
-        sum_o = sum_o.astype(jnp.float32)
-        swapped, attended_gradient = tie(output_sum.cores_done(), attended_gradient)
-        swapped = output_sum.ctx_start(swapped)
 
     grad_query_raw, key_terms, value_terms = attend_back(
         offset_array, query, key_value, attended_gradient, tables, key_tables
     )
-    if pair:
-        grad_query_raw, key_terms, value_terms, swapped = tie(
-            grad_query_raw, key_terms, value_terms, swapped
-        )
-        swapped = output_sum.ctx_done(swapped)
     key_value_grad = jnp.concatenate([key_terms, value_terms], axis=1)
     if pair:
         own = lax.dynamic_slice_in_dim(key_value_grad, offset, tokens, axis=0)
@@ -1108,29 +1101,6 @@
     )
     attn_gain_grad = jnp.sum(sum_in[:, :edge] * attn_in.astype(jnp.float32), axis=1) / own_gain
 
-    rest = [
-        ((rows_all, shared_back, shared_in_arrived), total(0)),
-        ((shared_act, grad_all, shared_down_arrived), total(0)),
-    ]
-    if pair:
-        other_sum, rest = output_sum.finish(swapped, rest)
-        sum_o = jnp.concatenate([sum_o, other_sum], axis=1)
-    else:
-        rest = [work(*operands) for operands, work in rest]
-    shared_in_grad = rest[0].astype(jnp.bfloat16)
-    sum_sd = rest[1][:own_hidden]
-    shared_in_grad = lax.all_to_all(
-        shared_in_grad.reshape(exp_count, own_rows, 2 * padded),
-        "exp",
-        split_axis=0,
-        concat_axis=0,
-        tiled=True,
-    ).reshape(exp_count, own_rows, 2, ctx_count, padded_own)[..., :own_hidden]
-    shared_in_grad = (
-        jnp.transpose(shared_in_grad, (2, 1, 3, 0, 4))
-        .reshape(2, own_rows, exp_count * ctx_count * own_hidden)
-        .astype(jnp.float32)
-    )
     return (
         output[None],
         input_grad[None],

time: 1790 us -> 1860 us (1.039)
  waiting for transfers between devices: 519 us -> 711 us
  between operations: 48.2 us -> 17.1 us
  starting transfers between devices: 93.9 us -> 65.8 us
  Pallas kernels: 885 us -> 866 us
    reduce_scatter x1, waiting for transfers between devices: 50 us -> 194 us  [on_device(): lax.psum_scatter(in_term, both, scatter_dimension=0, tiled=True)]
    ppermute x7 -> x6, waiting for transfers between devices: 35.2 us -> 118 us  [ctx_send(): return lax.ppermute(theirs, 'ctx', [(0, 1), (1, 0)])]
    ppermute x42 -> x28, starting transfers between devices: 63 us -> 28.5 us  [move(): lax.ppermute(total, 'exp', way)]
    ppermute x42 -> x28, waiting for transfers between devices: 70.7 us -> 43.7 us  [move(): lax.ppermute(total, 'exp', way)]
    ppermute x6 -> x5, waiting for transfers between devices: 24.4 us -> 0.01 us  [swap_cores(): return lax.ppermute(value, 'exp', self.swap)]
    pallas_call x10, Pallas kernels: 233 us -> 209 us  [weight_grad(): pl.pallas_call(weight_grad_kernel, grid_spec=pltpu.PrefetchScalarGridSpec...]
    unnamed x157 -> x131, local copies, waits for them, and re-layouts: 41.9 us -> 31.5 us
  transfers between devices with their start and end apart: 69 -> 53, of which waited for: 37 -> 33; matrix products, arithmetic and copies ran while one was open for 8% -> 7% of each run, Pallas kernels for 44% -> 42%
where the time goes in v4:
time: 1860 us; the launch traced here: 1850 us
  Pallas kernels  866 us (47%)
  waiting for transfers between devices  711 us (38%)
  local copies, waits for them, and re-layouts  80.5 us (4%)
  other arithmetic  68.9 us (4%)
  starting transfers between devices  65.8 us (4%)
  matrix products  40.1 us (2%)
    pallas_call x10, Pallas kernels, weight_grad(): pl.pallas_call(weight_grad_kernel, grid_spec=pltpu.PrefetchScalarGridSpec...  209 us
    ppermute x6, waiting for transfers between devices, ctx_fetch(): return lax.ppermute(part, 'ctx', [(0, 1), (1, 0)])  195 us
    pallas_call x21, Pallas kernels, combine(): pl.pallas_call(functools.partial(combine_kernel, scaled, len(rows), len(a...  194 us
    reduce_scatter x1, waiting for transfers between devices, on_device(): lax.psum_scatter(in_term, both, scatter_dimension=0, tiled=True)  194 us
    ppermute x6, waiting for transfers between devices, ctx_send(): return lax.ppermute(theirs, 'ctx', [(0, 1), (1, 0)])  118 us
    pallas_call x4, Pallas kernels, expert_grad_rows(): pl.pallas_call(expert_rows_kernel, grid=(count // 2 // high,), in_specs=[...  90.3 us
    pallas_call x1, Pallas kernels, expert_in(): pl.pallas_call(expert_in_kernel, grid=(count // high, hidden // wide), in...  75.6 us
    all_gather x1, waiting for transfers between devices, on_device(): lax.all_gather(jnp.concatenate([attn_in, routing.reshape(own_rows, routin...  60.2 us
  transfers between devices with their start and end apart: 53, of which 33 were waited for; matrix products, arithmetic and copies ran while one was open for 7% of the time, Pallas kernels for 42%

profile of v4, /device:TPU:0, one launch (start us, length us, event | category | flops | bytes accessed | tf_op | source)
XLA Modules:
  0.0 1850.0 jit_solution(11754907280486542543)
XLA Ops:
  33.8 25.9 %all-to-all-done = bf16[16,80,384]{2,1,0:T(8,128)(2,1)} async-done(((bf16[16,80,384]{2,1,0:T(8,128)(2,1)}), bf16[16,80,384]{2,1,0:T(8,128)(2,1)}, u32[]{:S(2)}, u32[]{:S(2)}) %all-to-all-start) | async-done | bytes 983072 | tf_op jit(solution)/shard_map/all_to_all | solution.py:849
  74.2 31.0 %collective-permute-done = bf16[1280,512]{0,1:T(8,128)(2,1)S(1)} collective-permute-done((bf16[1280,512]{0,1:T(8,128)(2,1)S(1)}, bf16[1280,512]{0,1:T(8,128)(2,1)S(1)}, u32[]{:S(2)}, u32[]{:S(2)}) %collective-permute-start) | collective-permute-done | bytes 1310752 | tf_op jit(solution)/shard_map/ppermute | solution.py:743
  105.5 60.2 %all-gather.5.cloned.1.call-done.weight_ref = bf16[2560,3712]{1,0:T(8,128)(2,1)} async-done(((bf16[80,3712]{1,0:T(8,128)(2,1)}), bf16[2560,3712]{1,0:T(8,128)(2,1)}) %all-gather.5.cloned.1.call-update) | async-done | bytes 19005456 | tf_op jit(solution)/shard_map/all_gather | solution.py:825
  209.0 29.0 %attend.1.right_ref = bf16[512,2560]{1,0:T(8,128)(2,1)} custom-call(s32[1]{0:T(128)} %bitcast.3.offset_ref, bf16[512,2560]{1,0:T(8,128)(2,1)} %project.2.query_ref, bf16[1024,1024]{1,0:T(8,128)(2,1)} %copy-done.16, bf16[1024,1024]{1,0:T(8,128)(2,1)} %copy-done.16), custom_call_target="tpu_custom_call" | custom-call | flops 5368709120 | bytes 7340032 | tf_op jit(solution)/shard_map/attend/pallas_call | solution.py:138
  238.0 32.5 %all-gather.7.cloned.1.call-done = bf16[2560,2560]{1,0:T(8,128)(2,1)} async-done(((bf16[80,2560]{1,0:T(8,128)(2,1)}), bf16[2560,2560]{1,0:T(8,128)(2,1)}) %all-gather.7.cloned.1.call-update) | async-done | bytes 13107216 | tf_op jit(solution)/shard_map/all_gather | solution.py:878
  298.4 75.8 %collective-permute-done.3 = bf16[1280,1536]{1,0:T(8,128)(2,1)} collective-permute-done((bf16[1280,1536]{1,0:T(8,128)(2,1)}, bf16[1280,1536]{1,0:T(8,128)(2,1)}, u32[]{:S(2)}, u32[]{:S(2)}) %collective-permute-start.3) | collective-permute-done | bytes 3932192 | tf_op jit(solution)/shard_map/ppermute | solution.py:743
  385.5 72.3 %collective-permute-done.4 = bf16[1280,1536]{1,0:T(8,128)(2,1)} collective-permute-done((bf16[1280,1536]{1,0:T(8,128)(2,1)}, bf16[1280,1536]{1,0:T(8,128)(2,1)}, u32[]{:S(2)}, u32[]{:S(2)}) %collective-permute-start.4) | collective-permute-done | bytes 3932192 | tf_op jit(solution)/shard_map/ppermute | solution.py:743
  469.2 22.7 %all-gather.9.cloned.1.call-done.left_ref = bf16[8192,2560]{1,0:T(8,128)(2,1)} async-done(((bf16[512,2560]{1,0:T(8,128)(2,1)}), bf16[8192,2560]{1,0:T(8,128)(2,1)}) %all-gather.9.cloned.1.call-update) | async-done | bytes 41943056 | tf_op jit(solution)/shard_map/all_gather | solution.py:897
  506.3 41.0 %enter.1 = (bf16[16,256,2560]{2,1,0:T(8,128)(2,1)}, bf16[16,512,256]{2,1,0:T(8,128)(2,1)}, bf16[16,512,512]{2,1,0:T(8,128)(2,1)}) custom-call(f32[16,2,512]{2,1,0:T(2,128)} %pad_maximum_fusion.10.slot_ref, bf16[16,512,2560]{2,1,0:T(8,128)(2,1)} %bitcast.137, bf16[512,2560]{1,0:T(8,128)(2,1)} %bitcast.126), custom_call_target="tpu_custom_call" | custom-call | flops 32212254720 | bytes 62914560 | tf_op jit(solution)/shard_map/enter/pallas_call | solution.py:265
  547.4 75.6 %expert_in.1 = (bf16[4096,1536]{1,0:T(8,128)(2,1)}, bf16[4096,1536]{1,0:T(8,128)(2,1)}, bf16[4096,1536]{1,0:T(8,128)(2,1)}) custom-call(bf16[4096,2560]{1,0:T(8,128)(2,1)} %bitcast.158, bf16[2560,1536]{1,0:T(8,128)(2,1)} %constant_dynamic-update-slice_fusion.3.gate_ref, bf16[2560,1536]{1,0:T(8,128)(2,1)} %constant_dynamic-update-slice_fusion.2.up_ref), custom_call_target="tpu_custom_call" | custom-call | flops 64424509440 | bytes 58720256 | tf_op jit(solution)/shard_map/expert_in/pallas_call | solution.py:343
  624.9 40.5 %expert_out.1 = bf16[4096,2560]{1,0:T(8,128)(2,1)} custom-call(s32[2]{0:T(128)} %iota_xor_fusion.part_ref, bf16[4096,1536]{1,0:T(8,128)(2,1)} %get-tuple-element.417.act_ref.left_ref, bf16[1536,1280]{1,0:T(8,128)(2,1)} %bitcast.142, bf16[1536,1280]{1,0:T(8,128)(2,1)} %copy-done.8), custom_call_target="tpu_custom_call" | custom-call | flops 32212254720 | bytes 46137344 | tf_op jit(solution)/shard_map/expert_out/pallas_call | solution.py:368
  703.0 36.5 %enter_back.1 = (bf16[16,256,2560]{2,1,0:T(8,128)(2,1)}, bf16[16,512,512]{2,1,0:T(8,128)(2,1)}) custom-call(f32[16,2,512]{2,1,0:T(2,128)} %pad_maximum_fusion.10.slot_ref, bf16[16,512,2560]{2,1,0:T(8,128)(2,1)} %bitcast.138, bf16[256,2560]{1,0:T(8,128)(2,1)} %copy-done.1, bf16[16,512,512]{2,1,0:T(8,128)(2,1)} %get-tuple-element.275.slope_ref), custom_call_target="tpu_custom_call" | custom-call | flops 21474836480 | bytes 62914560 | tf_op jit(solution)/shard_map/enter_back/pallas_call | solution.py:307
  768.0 26.4 %expert_back.2 = (bf16[4096,1536]{1,0:T(8,128)(2,1)}, bf16[4096,1536]{1,0:T(8,128)(2,1)}) custom-call(s32[2]{0:T(128)} %iota_xor_fusion.part_ref, bf16[4096,2560]{1,0:T(8,128)(2,1)} %bitcast.120, bf16[4096,2560]{1,0:T(8,128)(2,1)} %bitcast.121, bf16[1536,1280]{1,0:T(8,128)(2,1)} %bitcast.143, bf16[1536,1280]{1,0:T(8,128)(2,1)} %copy-done.8, ...), custom_call_target="tpu_custom_call" | custom-call | flops 16106127360 | bytes 35651584 | tf_op jit(solution)/shard_map/expert_back/pallas_call | solution.py:403
  805.7 26.5 %expert_back.3 = (bf16[4096,1536]{1,0:T(8,128)(2,1)}, bf16[4096,1536]{1,0:T(8,128)(2,1)}) custom-call(s32[2]{0:T(128)} %iota_xor_fusion.part_ref, bf16[4096,2560]{1,0:T(8,128)(2,1)} %bitcast.122, bf16[4096,2560]{1,0:T(8,128)(2,1)} %bitcast.123, bf16[1536,1280]{1,0:T(8,128)(2,1)} %bitcast.144, ...), custom_call_target="tpu_custom_call", output_to_operand_aliasing={{0}: (7, {}), {1}: (8, {})} | custom-call | flops 16106127360 | bytes 35651584 | tf_op jit(solution)/shard_map/expert_back/pallas_call | solution.py:403
  922.1 22.6 %expert_grad_rows.6.rest_0_ = bf16[4096,1280]{1,0:T(8,128)(2,1)} custom-call(bf16[4096,1536]{1,0:T(8,128)(2,1)} %get-tuple-element.429.gate_grad_ref.right_ref, bf16[4096,1536]{1,0:T(8,128)(2,1)} %get-tuple-element.455.up_grad_ref.right_ref, bf16[2560,1536]{1,0:T(8,128)(2,1)} %constant_dynamic-update-slice_fusion.3.gate_ref, ...), custom_call_target="tpu_custom_call" | custom-call | flops 16106127360 | bytes 25690112 | tf_op jit(solution)/shard_map/expert_grad_rows/pallas_call | solution.py:440
  983.9 22.8 %expert_grad_rows.7 = bf16[4096,1280]{1,0:T(8,128)(2,1)} custom-call(bf16[4096,1536]{1,0:T(8,128)(2,1)} %get-tuple-element.429.gate_grad_ref.right_ref, bf16[4096,1536]{1,0:T(8,128)(2,1)} %get-tuple-element.455.up_grad_ref.right_ref, bf16[2560,1536]{1,0:T(8,128)(2,1)} %constant_dynamic-update-slice_fusion.3.gate_ref, ...), custom_call_target="tpu_custom_call", output_to_operand_aliasing={{}: (4, {})} | custom-call | flops 16106127360 | bytes 25690112 | tf_op jit(solution)/shard_map/expert_grad_rows/pallas_call | solution.py:440
  1013.1 30.0 %combine.33 = bf16[14,512,1280]{2,1,0:T(8,128)(2,1)} custom-call(s32[16]{0:T(128)} %get-tuple-element.378.unit_ref, f32[16,512,128]{2,1,0:T(8,128)} %pad.24.info_ref, bf16[16,512,512]{2,1,0:T(8,128)(2,1)} %get-tuple-element.367.act_ref, bf16[512,2560]{1,0:T(8,128)(2,1)} %bitcast.128, bf16[16,256,1280]{2,1,0:T(8,128)(2,1)} %bitcast.107, ...), custom_call_target="tpu_custom_call" | custom-call | flops 14092861440 | bytes 27525120 | tf_op jit(solution)/shard_map/combine/pallas_call | solution.py:575
  1186.3 24.4 %weight_grad.15 = f32[1536,1280]{1,0:T(8,128)} custom-call(s32[1]{0:T(128)} %bitcast.30.part_ref, bf16[4096,1536]{1,0:T(8,128)(2,1)} %get-tuple-element.417.act_ref.left_ref, bf16[4096,2560]{1,0:T(8,128)(2,1)} %bitcast.125, bf16[1536,1280]{1,0:T(8,128)(2,1)} %collective-permute-done.31.rest_0_), custom_call_target="tpu_custom_call" | custom-call | flops 16106127360 | bytes 30932992 | tf_op jit(solution)/shard_map/weight_grad/pallas_call | solution.py:621
  1224.8 24.4 %weight_grad.16 = f32[1280,1536]{1,0:T(8,128)} custom-call(s32[1]{0:T(128)} %bitcast.30.part_ref, bf16[4096,2560]{1,0:T(8,128)(2,1)} %bitcast.161, bf16[4096,1536]{1,0:T(8,128)(2,1)} %get-tuple-element.429.gate_grad_ref.right_ref, bf16[1280,1536]{1,0:T(8,128)(2,1)} %collective-permute-done.34.rest_0_), custom_call_target="tpu_custom_call" | custom-call | flops 16106127360 | bytes 30932992 | tf_op jit(solution)/shard_map/weight_grad/pallas_call | solution.py:621
  1260.3 81.3 %collective-permute-done.38.rest_0_ = bf16[128,2560]{1,0:T(8,128)(2,1)} collective-permute-done((bf16[128,2560]{1,0:T(8,128)(2,1)}, bf16[128,2560]{1,0:T(8,128)(2,1)}, u32[]{:S(2)}, u32[]{:S(2)}) %collective-permute-start.38) | collective-permute-done | bytes 655392 | tf_op jit(solution)/shard_map/ppermute | solution.py:774
  1395.3 24.4 %weight_grad.19 = f32[1280,1536]{1,0:T(8,128)} custom-call(s32[1]{0:T(128)} %bitcast.30.part_ref, bf16[4096,2560]{1,0:T(8,128)(2,1)} %bitcast.162, bf16[4096,1536]{1,0:T(8,128)(2,1)} %get-tuple-element.455.up_grad_ref.right_ref, bf16[1280,1536]{1,0:T(8,128)(2,1)} %collective-permute-done.41.rest_0_), custom_call_target="tpu_custom_call" | custom-call | flops 16106127360 | bytes 30932992 | tf_op jit(solution)/shard_map/weight_grad/pallas_call | solution.py:621
  1474.7 48.7 %attend_back.1 = (bf16[512,2560]{1,0:T(8,128)(2,1)}, f32[1024,512]{1,0:T(8,128)}, f32[1024,512]{1,0:T(8,128)}) custom-call(s32[1]{0:T(128)} %bitcast.3.offset_ref, bf16[512,2560]{1,0:T(8,128)(2,1)} %project.2.query_ref, bf16[1024,1024]{1,0:T(8,128)(2,1)} %copy-done.16, bf16[1024,1024]{1,0:T(8,128)(2,1)} %copy-done.16, ...), custom_call_target="tpu_custom_call" | custom-call | flops 13421772800 | bytes 14155776 | tf_op jit(solution)/shard_map/attend_back/pallas_call | solution.py:200
  1534.6 37.2 %collective-permute-done.44 = bf16[512,1024]{1,0:T(8,128)(2,1)} collective-permute-done((bf16[512,1024]{1,0:T(8,128)(2,1)}, bf16[512,1024]{1,0:T(8,128)(2,1)}, u32[]{:S(2)}, u32[]{:S(2)}) %collective-permute-start.44) | collective-permute-done | bytes 1048608 | tf_op jit(solution)/shard_map/ppermute | solution.py:774
  1644.8 193.8 %reduce-scatter.3.cloned.1.call-done = bf16[80,3712]{1,0:T(8,128)(2,1)} async-done(((bf16[2560,3712]{1,0:T(8,128)(2,1)}), bf16[80,3712]{1,0:T(8,128)(2,1)}) %reduce-scatter.3.cloned.1.call-update) | async-done | bytes 593936 | tf_op jit(solution)/shard_map/reduce_scatter | solution.py:1098
  (349 shorter events, 727.5 us)
Async XLA Ops:
  7.2 158.6 %all-gather.5.cloned.1.call-start = ((), (), s32[]{:S(2)}) async-start(), calls=%async_computation.4 | async-start | bytes 19599360 | tf_op jit(solution)/shard_map/all_gather | solution.py:825
  29.8 240.7 %all-gather.7.cloned.1.call-start = ((), (), s32[]{:S(2)}) async-start(), calls=%async_computation.5 | async-start | bytes 13516800 | tf_op jit(solution)/shard_map/all_gather | solution.py:878
  31.0 40.7 %collective-permute-start.1 = (bf16[128,2560]{1,0:T(8,128)(2,1)S(1)}, bf16[128,2560]{1,0:T(8,128)(2,1)}, u32[]{:S(2)}, u32[]{:S(2)}) collective-permute-start(bf16[128,2560]{1,0:T(8,128)(2,1)S(1)} %pad.23), channel_id=1, source_target_pairs={{0,16},{16,0},{1,17},{17,1},{2,18},{18,2},{3,19},{19,3},{4,20},{20... | collective-permute-start | bytes 1966088 | tf_op jit(solution)/shard_map/ppermute | solution.py:743
  165.8 326.1 %all-gather.9.cloned.1.call-start = ((), (), s32[]{:S(2)}) async-start(), calls=%async_computation.6 | async-start | bytes 44564480 | tf_op jit(solution)/shard_map/all_gather | solution.py:897
  286.0 415.0 %all-gather.11.cloned.1.call-start = ((), (), s32[]{:S(2)}) async-start(), calls=%async_computation.7 | async-start | bytes 44564480 | tf_op jit(solution)/shard_map/all_gather | solution.py:901
  286.0 88.2 %collective-permute-start.3 = (bf16[1280,1536]{1,0:T(8,128)(2,1)}, bf16[1280,1536]{1,0:T(8,128)(2,1)}, u32[]{:S(2)}, u32[]{:S(2)}) collective-permute-start(bf16[1280,1536]{1,0:T(8,128)(2,1)} %bitcast.150), channel_id=1, source_target_pairs={{0,16},{16,0},{1,17},{17,1},{2,18},{18,2},{3,19},{19,3},{4,20},{20... | collective-permute-start | bytes 11796488 | tf_op jit(solution)/shard_map/ppermute | solution.py:743
  288.7 169.1 %collective-permute-start.4 = (bf16[1280,1536]{1,0:T(8,128)(2,1)}, bf16[1280,1536]{1,0:T(8,128)(2,1)}, u32[]{:S(2)}, u32[]{:S(2)}) collective-permute-start(bf16[1280,1536]{1,0:T(8,128)(2,1)} %bitcast.152), channel_id=1, source_target_pairs={{0,16},{16,0},{1,17},{17,1},{2,18},{18,2},{3,19},{19,3},{4,20},{20... | collective-permute-start | bytes 11796488 | tf_op jit(solution)/shard_map/ppermute | solution.py:743
  492.0 1150.9 %reduce-scatter.5.cloned.1.call-start = ((), (), s32[]{:S(2)}) async-start(), calls=%async_computation.9 | async-start | bytes 13516800 | tf_op jit(solution)/shard_map/reduce_scatter | solution.py:1078
  504.9 118.1 %collective-permute-start.5 = (bf16[1536,1280]{1,0:T(8,128)(2,1)}, bf16[1536,1280]{1,0:T(8,128)(2,1)S(1)}, u32[]{:S(2)}, u32[]{:S(2)}) collective-permute-start(bf16[1536,1280]{1,0:T(8,128)(2,1)} %bitcast.141), channel_id=1, source_target_pairs={{0,16},{16,0},{1,17},{17,1},{2,18},{18,2},{3,19},{19,3},{4,20},{20... | collective-permute-start | bytes 11796488 | tf_op jit(solution)/shard_map/ppermute | solution.py:743
  678.9 60.6 %collective-permute-start.9 = (bf16[4,512,1280]{2,1,0:T(8,128)(2,1)}, bf16[4,512,1280]{2,1,0:T(8,128)(2,1)}, u32[]{:S(2)}, u32[]{:S(2)}) collective-permute-start(bf16[4,512,1280]{2,1,0:T(8,128)(2,1)} %combine.22), channel_id=1, source_target_pairs={{0,1},{1,0},{2,3},{3,2},{4,5},{5,4},{6,7},{7,6},{8,9},{9,8},{10,11... | collective-permute-start | bytes 15728648 | tf_op jit(solution)/shard_map/ppermute | solution.py:677
  748.7 45.7 %collective-permute-start.10 = (bf16[1,512,1280]{2,1,0:T(8,128)(2,1)}, bf16[1,512,1280]{2,1,0:T(8,128)(2,1)S(1)}, u32[]{:S(2)}, u32[]{:S(2)}) collective-permute-start(bf16[1,512,1280]{2,1,0:T(8,128)(2,1)} %get-tuple-element.287), channel_id=1, source_target_pairs={{0,4},{1,5},{4,8},{5,9},{8,12},{9,13},{12,14},{13,15},{14,10},{15,... | collective-permute-start | bytes 3932168 | tf_op jit(solution)/shard_map/ppermute | solution.py:674
  750.2 44.2 %collective-permute-start.11 = (bf16[1,512,1280]{2,1,0:T(8,128)(2,1)}, bf16[1,512,1280]{2,1,0:T(8,128)(2,1)S(1)}, u32[]{:S(2)}, u32[]{:S(2)}) collective-permute-start(bf16[1,512,1280]{2,1,0:T(8,128)(2,1)} %get-tuple-element.288), channel_id=1, source_target_pairs={{4,0},{5,1},{8,4},{9,5},{12,8},{13,9},{14,12},{15,13},{10,14},{11,... | collective-permute-start | bytes 3932168 | tf_op jit(solution)/shard_map/ppermute | solution.py:674
  794.5 40.4 %collective-permute-start.14 = (bf16[10,512,1280]{2,1,0:T(8,128)(2,1)}, bf16[10,512,1280]{2,1,0:T(8,128)(2,1)}, u32[]{:S(2)}, u32[]{:S(2)}) collective-permute-start(bf16[10,512,1280]{2,1,0:T(8,128)(2,1)} %combine.25), channel_id=1, source_target_pairs={{0,1},{1,0},{2,3},{3,2},{4,5},{5,4},{6,7},{7,6},{8,9},{9,8},{10,11... | collective-permute-start | bytes 39321608 | tf_op jit(solution)/shard_map/ppermute | solution.py:677
  1043.2 41.6 %collective-permute-start.26 = (bf16[14,512,1280]{2,1,0:T(8,128)(2,1)}, bf16[14,512,1280]{2,1,0:T(8,128)(2,1)}, u32[]{:S(2)}, u32[]{:S(2)}) collective-permute-start(bf16[14,512,1280]{2,1,0:T(8,128)(2,1)} %combine.33), channel_id=1, source_target_pairs={{0,1},{1,0},{2,3},{3,2},{4,5},{5,4},{6,7},{7,6},{8,9},{9,8},{10,11... | collective-permute-start | bytes 55050248 | tf_op jit(solution)/shard_map/ppermute | solution.py:677
  1043.7 140.5 %collective-permute-start.31 = (bf16[1536,1280]{1,0:T(8,128)(2,1)}, bf16[1536,1280]{1,0:T(8,128)(2,1)}, u32[]{:S(2)}, u32[]{:S(2)}) collective-permute-start(bf16[1536,1280]{1,0:T(8,128)(2,1)} %weight_grad.10), channel_id=1, source_target_pairs={{0,16},{16,0},{1,17},{17,1},{2,18},{18,2},{3,19},{19,3},{4,20},{20... | collective-permute-start | bytes 11796488 | tf_op jit(solution)/shard_map/ppermute | solution.py:774
  1096.4 126.3 %collective-permute-start.34 = (bf16[1280,1536]{1,0:T(8,128)(2,1)}, bf16[1280,1536]{1,0:T(8,128)(2,1)}, u32[]{:S(2)}, u32[]{:S(2)}) collective-permute-start(bf16[1280,1536]{1,0:T(8,128)(2,1)} %weight_grad.11), channel_id=1, source_target_pairs={{0,16},{16,0},{1,17},{17,1},{2,18},{18,2},{3,19},{19,3},{4,20},{20... | collective-permute-start | bytes 11796488 | tf_op jit(solution)/shard_map/ppermute | solution.py:774
  1134.8 38.9 %collective-permute-start.29 = (bf16[1,512,1280]{2,1,0:T(8,128)(2,1)}, bf16[1,512,1280]{2,1,0:T(8,128)(2,1)S(1)}, u32[]{:S(2)}, u32[]{:S(2)}) collective-permute-start(bf16[1,512,1280]{2,1,0:T(8,128)(2,1)} %get-tuple-element.403), channel_id=1, source_target_pairs={{0,4},{1,5},{4,8},{5,9},{8,12},{9,13},{12,14},{13,15},{14,10},{15,... | collective-permute-start | bytes 3932168 | tf_op jit(solution)/shard_map/ppermute | solution.py:674
  1136.9 256.3 %collective-permute-start.41 = (bf16[1280,1536]{1,0:T(8,128)(2,1)}, bf16[1280,1536]{1,0:T(8,128)(2,1)}, u32[]{:S(2)}, u32[]{:S(2)}) collective-permute-start(bf16[1280,1536]{1,0:T(8,128)(2,1)} %weight_grad.12), channel_id=1, source_target_pairs={{0,16},{16,0},{1,17},{17,1},{2,18},{18,2},{3,19},{19,3},{4,20},{20... | collective-permute-start | bytes 11796488 | tf_op jit(solution)/shard_map/ppermute | solution.py:774
  1186.3 155.3 %collective-permute-start.37 = (bf16[1280,512]{1,0:T(8,128)(2,1)S(1)}, bf16[1280,512]{1,0:T(8,128)(2,1)S(1)}, u32[]{:S(2)}, u32[]{:S(2)}) collective-permute-start(bf16[1280,512]{1,0:T(8,128)(2,1)S(1)} %copy-done.35), channel_id=1, source_target_pairs={{0,16},{16,0},{1,17},{17,1},{2,18},{18,2},{3,19},{19,3},{4,20},{20... | collective-permute-start | bytes 3932168 | tf_op jit(solution)/shard_map/ppermute | solution.py:774
  1212.7 128.9 %collective-permute-start.38 = (bf16[128,2560]{1,0:T(8,128)(2,1)}, bf16[128,2560]{1,0:T(8,128)(2,1)}, u32[]{:S(2)}, u32[]{:S(2)}) collective-permute-start(bf16[128,2560]{1,0:T(8,128)(2,1)} %weight_grad.14), channel_id=1, source_target_pairs={{0,16},{16,0},{1,17},{17,1},{2,18},{18,2},{3,19},{19,3},{4,20},{20... | collective-permute-start | bytes 1966088 | tf_op jit(solution)/shard_map/ppermute | solution.py:774
  1341.7 40.9 %collective-permute-start.39 = (bf16[1,512,1280]{2,1,0:T(8,128)(2,1)}, bf16[1,512,1280]{2,1,0:T(8,128)(2,1)S(1)}, u32[]{:S(2)}, u32[]{:S(2)}) collective-permute-start(bf16[1,512,1280]{2,1,0:T(8,128)(2,1)} %get-tuple-element.438), channel_id=1, source_target_pairs={{0,4},{1,5},{4,8},{5,9},{8,12},{9,13},{12,14},{13,15},{14,10},{15,... | collective-permute-start | bytes 3932168 | tf_op jit(solution)/shard_map/ppermute | solution.py:674
  1343.4 39.2 %collective-permute-start.40 = (bf16[1,512,1280]{2,1,0:T(8,128)(2,1)}, bf16[1,512,1280]{2,1,0:T(8,128)(2,1)S(1)}, u32[]{:S(2)}, u32[]{:S(2)}) collective-permute-start(bf16[1,512,1280]{2,1,0:T(8,128)(2,1)} %get-tuple-element.439), channel_id=1, source_target_pairs={{4,0},{5,1},{8,4},{9,5},{12,8},{13,9},{14,12},{15,13},{10,14},{11,... | collective-permute-start | bytes 3932168 | tf_op jit(solution)/shard_map/ppermute | solution.py:674
  1459.3 379.3 %reduce-scatter.3.cloned.1.call-start = ((), (), s32[]{:S(2)}) async-start(), calls=%async_computation.8 | async-start | bytes 19599360 | tf_op jit(solution)/shard_map/reduce_scatter | solution.py:1098
  1529.0 42.8 %collective-permute-start.44 = (bf16[512,1024]{1,0:T(8,128)(2,1)}, bf16[512,1024]{1,0:T(8,128)(2,1)}, u32[]{:S(2)}, u32[]{:S(2)}) collective-permute-start(bf16[512,1024]{1,0:T(8,128)(2,1)} %dynamic-slice_convert_fusion), channel_id=1, source_target_pairs={{0,16},{16,0},{1,17},{17,1},{2,18},{18,2},{3,19},{19,3},{4,20},{20... | collective-permute-start | bytes 3145736 | tf_op jit(solution)/shard_map/ppermute | solution.py:774
  (93 other events, 1979.0 us)
Sparse Core Ops, SparseCore 0:
  11.6 154.1 all-gather.4
  168.6 101.8 all-gather.6
  286.1 205.7 all-gather.8
  493.4 207.5 all-gather.10
  1459.4 162.1 reduce-scatter.4
  1623.9 214.6 reduce-scatter.2

commit v5 on v4

--- a/solution.py
+++ b/solution.py
@@ -726,21 +726,27 @@
         )[0][0]
 
 
-def ring_step(rings, work, *operands):
+def ring_step(rings, work, *operands, also=()):
     totals = [ring.totals() for ring in rings]
     totals, operands = tie(totals, operands)
     moved = [ring.line.move(total) for ring, total in zip(rings, totals)]
     swapped = [ring.swapped for ring in rings]
-    moved, swapped, result = tie(moved, swapped, work(*operands))
+    moved, swapped, result, also = tie(moved, swapped, work(*operands), also)
     for ring, arrived, ring.swapped in zip(rings, moved, swapped):
         ring.arrived = tuple(arrived)
-    return result
+    return (result, *also) if also else result
 
 
 def ctx_fetch(part, axis):
     if lax.axis_size("ctx") != 2:
         return lax.all_gather(part, "ctx", axis=axis, tiled=True)
     return lax.ppermute(part, "ctx", [(0, 1), (1, 0)])
+
+
+def ctx_half(array, mine):
+    half = array.shape[1] // 2
+    index = lax.axis_index("ctx")
+    return lax.dynamic_slice_in_dim(array, (index if mine else 1 - index) * half, half, axis=1)
 
 
 def ctx_join(part, other, axis):
@@ -879,7 +885,6 @@
     key_value = ctx_gather(
         project(normed_one, full_in, tables, QUERY_HEADS // KEY_VALUE_HEADS, 2, 1), 0
     )
-    normed_one_t = normed_one.T
     query = project(normed_one, full_in, tables, 0, QUERY_HEADS // KEY_VALUE_HEADS, QUERY_HEADS)
     attended_low = attend(offset_array, query, key_value)
 
@@ -944,7 +949,7 @@
     shared_act = flat(shared_act)
     rings = []
     if pair:
-        out_ring = ExpRing(out_part, jnp.bfloat16, (middle[None],))
+        out_ring = ExpRing(out_part, jnp.bfloat16, (middle[None],), late_from=(9,))
         rings = [out_ring]
     grad_expert, shared_back = ring_step(
         rings,
@@ -956,18 +961,13 @@
     )
     grad_expert = flat(grad_expert)
     grad_eu = ()
-    out_late = (out_ring.late_units,) if pair else ()
-
-    def late(work, here):
-        if not (pair and here):
-            return work
-        return lambda units, *operands: (work(*operands), out_ring.late(0, units))
-
+    early = ()
+    if pair:
+        early = (ctx_send(ctx_half(normed_one, False), 0), ctx_send(attended_low, 0))
     for half in range(2):
         grad_eu = ring_step(
             rings,
-            late(lambda *operands: expert_back(*operands[:6], half, operands[6:]), half == 0),
-            *out_late,
+            lambda *operands: expert_back(*operands[:6], half, operands[6:]),
             down_parts,
             grad_expert,
             down_part,
@@ -975,11 +975,10 @@
             expert_slope,
             expert_silu,
             *grad_eu,
+            also=early if half == 0 else (),
         )
         if pair and half == 0:
-            grad_eu, rest = grad_eu
-            out_ring.take(rest)
-            out_late = ()
+            grad_eu, normed_other, attended_other = grad_eu
     grad_eg, grad_eu = grad_eu
     pieces = [(), ()]
     theirs = lambda axis: lambda left, right: ctx_theirs(left, right, axis)
@@ -1039,20 +1038,78 @@
     shared_down_arrived = ctx_send(shared_down_theirs, 0)
     expert_down_grad = ring_step(rings, total(1), expert_act, grad_expert, down_arrived)[None]
     expert_gate_grad = ring_step(rings, total(0), received, grad_eg, gate_arrived)[None]
-    shared_in_grad, sum_sd = ring_step(
-        rings,
-        lambda a, b, c, d, e, f: (
-            ctx_total(a, b, 0, c).astype(jnp.bfloat16),
-            ctx_total(d, e, 0, f),
-        ),
-        rows_all,
-        shared_back,
-        shared_in_arrived,
-        shared_act,
-        grad_all,
-        shared_down_arrived,
-    )
-    sum_sd = sum_sd[:own_hidden]
+    if pair:
+        ring_step(rings, lambda: ())
+    expert_up_grad = ring_step(rings, total(0), received, grad_eu, up_arrived)[None]
+    if pair:
+        grad_two = grad_ring.finish()
+    else:
+        grad_two = sum_over_exp(grad_part)
+    ffn_gain_term = jnp.sum(grad_two * middle * inverse_two, axis=0)
+    grad_middle = grad_low.astype(jnp.float32) + norm_back(grad_two, middle, inverse_two, ffn_gain)
+    grad_middle_low = grad_middle.astype(jnp.bfloat16)
+    attended_gradient = dot_t(grad_middle_low, full_output).astype(jnp.bfloat16)
+    if pair:
+        middle_other = ctx_send(ctx_half(grad_middle_low, False), 0)
+        gain_half = ffn_gain_term.reshape(2, -1)
+        gain_other = ctx_send(lax.dynamic_index_in_dim(gain_half, 1 - lax.axis_index("ctx"), 0), 0)
+        gain_half = lax.dynamic_index_in_dim(gain_half, lax.axis_index("ctx"), 0)
+        attended_gradient, gain_other = tie(attended_gradient, gain_other)
+        gain_term = (gain_half + gain_other).T
+    else:
+        gain_term = ffn_gain_term[:, None]
+    gain_term = jnp.pad(gain_term, ((0, 0), (0, 127))).astype(jnp.bfloat16)
+
+    grad_query_raw, key_terms, value_terms = attend_back(
+        offset_array, query, key_value, attended_gradient, tables, key_tables
+    )
+    key_value_grad = jnp.concatenate([key_terms, value_terms], axis=1)
+    if pair:
+        grad_query_raw, key_value_grad, middle_other = tie(
+            grad_query_raw, key_value_grad, middle_other
+        )
+        key_value_other = ctx_send(key_value_grad.astype(jnp.bfloat16), 0)
+        query_other = ctx_send(grad_query_raw, 0)
+        output_term = rows_grad(
+            jnp.concatenate([ctx_half(grad_middle_low, True), middle_other], axis=0),
+            jnp.concatenate([attended_low, attended_other], axis=0),
+        )
+        sum_o = lax.psum_scatter(output_term, "exp", scatter_dimension=0, tiled=True)
+        key_value_all = (key_value_grad + key_value_other.astype(jnp.float32)).astype(jnp.bfloat16)
+        key_value_raw = lax.dynamic_slice_in_dim(key_value_all, offset, tokens, axis=0)
+        key_value_both = jnp.concatenate(
+            [
+                key_value_raw,
+                lax.dynamic_slice_in_dim(key_value_all, tokens - offset, tokens, axis=0),
+            ],
+            axis=0,
+        )
+        in_term = qkv_grad(
+            jnp.concatenate([ctx_half(normed_one, True), normed_other], axis=0).T,
+            jnp.concatenate([grad_query_raw, query_other], axis=0),
+            key_value_both,
+            gain_term,
+        )
+        sum_in = lax.psum_scatter(in_term, "exp", scatter_dimension=0, tiled=True)
+    else:
+        key_value_raw = ctx_send(key_value_grad.astype(jnp.bfloat16), 0)
+        in_term = qkv_grad(normed_one.T, grad_query_raw, key_value_raw, gain_term)
+        sum_in = lax.psum_scatter(in_term, both, scatter_dimension=0, tiled=True)
+        output_term = rows_grad(grad_middle_low, attended_low)
+        sum_o = lax.psum_scatter(output_term, both, scatter_dimension=0, tiled=True)
+    sum_in = sum_in.astype(jnp.float32)
+    grad_raw = jnp.concatenate(
+        [grad_query_raw, key_value_raw, jnp.zeros((tokens, routing_columns), jnp.bfloat16)], axis=1
+    )
+    grad_one = dot_t(grad_raw, full_in)
+    input_grad = grad_middle + norm_back(grad_one, input_rows, inverse_one, attn_gain)
+    own_gain = lax.dynamic_slice_in_dim(
+        attn_gain, (lax.axis_index("ctx") * exp_count + exp_index) * own_rows, own_rows
+    )
+    attn_gain_grad = jnp.sum(sum_in[:, :edge] * attn_in.astype(jnp.float32), axis=1) / own_gain
+
+    shared_in_grad = ctx_total(rows_all, shared_back, 0, shared_in_arrived).astype(jnp.bfloat16)
+    sum_sd = ctx_total(shared_act, grad_all, 0, shared_down_arrived)[:own_hidden]
     shared_in_grad = lax.all_to_all(
         shared_in_grad.reshape(exp_count, own_rows, 2 * padded),
         "exp",
@@ -1065,42 +1122,6 @@
         .reshape(2, own_rows, exp_count * ctx_count * own_hidden)
         .astype(jnp.float32)
     )
-    expert_up_grad = ring_step(rings, total(0), received, grad_eu, up_arrived)[None]
-    if pair:
-        grad_two = grad_ring.finish()
-    else:
-        grad_two = sum_over_exp(grad_part)
-    ffn_gain_term = jnp.sum(grad_two * middle * inverse_two, axis=0)
-    gain_term = jnp.pad(ffn_gain_term[:, None], ((0, 0), (0, 127))).astype(jnp.bfloat16)
-    grad_middle = grad_low.astype(jnp.float32) + norm_back(grad_two, middle, inverse_two, ffn_gain)
-    grad_middle_low = grad_middle.astype(jnp.bfloat16)
-    output_term = rows_grad(grad_middle_low, attended_low)
-    sum_o = lax.psum_scatter(output_term, both, scatter_dimension=0, tiled=True)
-    attended_gradient = dot_t(grad_middle_low, full_output).astype(jnp.bfloat16)
-
-    grad_query_raw, key_terms, value_terms = attend_back(
-        offset_array, query, key_value, attended_gradient, tables, key_tables
-    )
-    key_value_grad = jnp.concatenate([key_terms, value_terms], axis=1)
-    if pair:
-        own = lax.dynamic_slice_in_dim(key_value_grad, offset, tokens, axis=0)
-        other = lax.dynamic_slice_in_dim(key_value_grad, tokens - offset, tokens, axis=0)
-        key_value_raw = own + ctx_send(other.astype(jnp.bfloat16), 0).astype(jnp.float32)
-    else:
-        key_value_raw = ctx_send(key_value_grad.astype(jnp.bfloat16), 0)
-    key_value_raw = key_value_raw.astype(jnp.bfloat16)
-    in_term = qkv_grad(normed_one_t, grad_query_raw, key_value_raw, gain_term)
-    grad_raw = jnp.concatenate(
-        [grad_query_raw, key_value_raw, jnp.zeros((tokens, routing_columns), jnp.bfloat16)], axis=1
-    )
-    grad_one = dot_t(grad_raw, full_in)
-    input_grad = grad_middle + norm_back(grad_one, input_rows, inverse_one, attn_gain)
-    sum_in = lax.psum_scatter(in_term, both, scatter_dimension=0, tiled=True).astype(jnp.float32)
-    own_gain = lax.dynamic_slice_in_dim(
-        attn_gain, (lax.axis_index("ctx") * exp_count + exp_index) * own_rows, own_rows
-    )
-    attn_gain_grad = jnp.sum(sum_in[:, :edge] * attn_in.astype(jnp.float32), axis=1) / own_gain
-
     return (
         output[None],
         input_grad[None],

time: 1860 us -> 1710 us (0.919)
  waiting for transfers between devices: 711 us -> 553 us
  other arithmetic: 68.9 us -> 93 us
    reduce_scatter x2, waiting for transfers between devices: 194 us -> 4.62 us  [the longest x1 4.6 us: on_device(): sum_in = lax.psum_scatter(in_term, 'exp', scatter_dimension=0, tiled=True)]
    ppermute x28, waiting for transfers between devices: 43.7 us -> 63.7 us  [move(): lax.ppermute(total, 'exp', way)]
    ppermute x6 -> x11, waiting for transfers between devices: 118 us -> 122 us  [ctx_send(): return lax.ppermute(theirs, 'ctx', [(0, 1), (1, 0)])]
    pallas_call x21 -> x20, Pallas kernels: 194 us -> 192 us  [combine(): pl.pallas_call(functools.partial(combine_kernel, scaled, len(rows), len(a...]
  transfers between devices with their start and end apart: 53 -> 57, of which waited for: 33 -> 41; matrix products, arithmetic and copies ran while one was open for 7% -> 8% of each run, Pallas kernels for 42% -> 45%
where the time goes in v5:
time: 1710 us; the launch traced here: 1700 us
  Pallas kernels  863 us (50%)
  waiting for transfers between devices  553 us (32%)
  other arithmetic  93 us (5%)
  local copies, waits for them, and re-layouts  78.8 us (5%)
  starting transfers between devices  62.5 us (4%)
  matrix products  36.8 us (2%)
    pallas_call x10, Pallas kernels, weight_grad(): pl.pallas_call(weight_grad_kernel, grid_spec=pltpu.PrefetchScalarGridSpec...  210 us
    ppermute x6, waiting for transfers between devices, ctx_fetch(): return lax.ppermute(part, 'ctx', [(0, 1), (1, 0)])  196 us
    pallas_call x20, Pallas kernels, combine(): pl.pallas_call(functools.partial(combine_kernel, scaled, len(rows), len(a...  192 us
    ppermute x11, waiting for transfers between devices, ctx_send(): return lax.ppermute(theirs, 'ctx', [(0, 1), (1, 0)])  122 us
    pallas_call x4, Pallas kernels, expert_grad_rows(): pl.pallas_call(expert_rows_kernel, grid=(count // 2 // high,), in_specs=[...  90.6 us
    pallas_call x1, Pallas kernels, expert_in(): pl.pallas_call(expert_in_kernel, grid=(count // high, hidden // wide), in...  75.8 us
    ppermute x28, waiting for transfers between devices, move(): lax.ppermute(total, 'exp', way)  63.7 us
    all_gather x1, waiting for transfers between devices, on_device(): lax.all_gather(jnp.concatenate([attn_in, routing.reshape(own_rows, routin...  60.5 us
  transfers between devices with their start and end apart: 57, of which 41 were waited for; matrix products, arithmetic and copies ran while one was open for 8% of the time, Pallas kernels for 45%

profile of v5, /device:TPU:0, one launch (start us, length us, event | category | flops | bytes accessed | tf_op | source)
XLA Modules:
  0.0 1703.8 jit_solution(16786881474068849312)
XLA Ops:
  33.6 26.0 %all-to-all-done = bf16[16,80,384]{2,1,0:T(8,128)(2,1)} async-done(((bf16[16,80,384]{2,1,0:T(8,128)(2,1)}), bf16[16,80,384]{2,1,0:T(8,128)(2,1)}, u32[]{:S(2)}, u32[]{:S(2)}) %all-to-all-start) | async-done | bytes 983072 | tf_op jit(solution)/shard_map/all_to_all | solution.py:855
  74.2 31.1 %collective-permute-done = bf16[1280,512]{0,1:T(8,128)(2,1)S(1)} collective-permute-done((bf16[1280,512]{0,1:T(8,128)(2,1)S(1)}, bf16[1280,512]{0,1:T(8,128)(2,1)S(1)}, u32[]{:S(2)}, u32[]{:S(2)}) %collective-permute-start) | collective-permute-done | bytes 1310752 | tf_op jit(solution)/shard_map/ppermute | solution.py:743
  105.6 60.5 %all-gather.5.cloned.1.call-done.weight_ref = bf16[2560,3712]{1,0:T(8,128)(2,1)} async-done(((bf16[80,3712]{1,0:T(8,128)(2,1)}), bf16[2560,3712]{1,0:T(8,128)(2,1)}) %all-gather.5.cloned.1.call-update) | async-done | bytes 19005456 | tf_op jit(solution)/shard_map/all_gather | solution.py:831
  209.3 29.1 %attend.1 = bf16[512,2560]{1,0:T(8,128)(2,1)} custom-call(s32[1]{0:T(128)} %bitcast.3.offset_ref, bf16[512,2560]{1,0:T(8,128)(2,1)} %project.2.query_ref, bf16[1024,1024]{1,0:T(8,128)(2,1)} %copy-done.16, bf16[1024,1024]{1,0:T(8,128)(2,1)} %copy-done.16), custom_call_target="tpu_custom_call" | custom-call | flops 5368709120 | bytes 7340032 | tf_op jit(solution)/shard_map/attend/pallas_call | solution.py:138
  238.4 32.3 %all-gather.7.cloned.1.call-done = bf16[2560,2560]{1,0:T(8,128)(2,1)} async-done(((bf16[80,2560]{1,0:T(8,128)(2,1)}), bf16[2560,2560]{1,0:T(8,128)(2,1)}) %all-gather.7.cloned.1.call-update) | async-done | bytes 13107216 | tf_op jit(solution)/shard_map/all_gather | solution.py:884
  298.6 75.8 %collective-permute-done.3 = bf16[1280,1536]{1,0:T(8,128)(2,1)} collective-permute-done((bf16[1280,1536]{1,0:T(8,128)(2,1)}, bf16[1280,1536]{1,0:T(8,128)(2,1)}, u32[]{:S(2)}, u32[]{:S(2)}) %collective-permute-start.3) | collective-permute-done | bytes 3932192 | tf_op jit(solution)/shard_map/ppermute | solution.py:743
  385.8 72.2 %collective-permute-done.4 = bf16[1280,1536]{1,0:T(8,128)(2,1)} collective-permute-done((bf16[1280,1536]{1,0:T(8,128)(2,1)}, bf16[1280,1536]{1,0:T(8,128)(2,1)}, u32[]{:S(2)}, u32[]{:S(2)}) %collective-permute-start.4) | collective-permute-done | bytes 3932192 | tf_op jit(solution)/shard_map/ppermute | solution.py:743
  498.2 41.0 %enter.1 = (bf16[16,256,2560]{2,1,0:T(8,128)(2,1)}, bf16[16,512,256]{2,1,0:T(8,128)(2,1)}, bf16[16,512,512]{2,1,0:T(8,128)(2,1)}) custom-call(f32[16,2,512]{2,1,0:T(2,128)} %pad_maximum_fusion.15.slot_ref, bf16[16,512,2560]{2,1,0:T(8,128)(2,1)} %bitcast.139, bf16[512,2560]{1,0:T(8,128)(2,1)} %bitcast.128), custom_call_target="tpu_custom_call" | custom-call | flops 32212254720 | bytes 62914560 | tf_op jit(solution)/shard_map/enter/pallas_call | solution.py:265
  539.2 75.8 %expert_in.1 = (bf16[4096,1536]{1,0:T(8,128)(2,1)}, bf16[4096,1536]{1,0:T(8,128)(2,1)}, bf16[4096,1536]{1,0:T(8,128)(2,1)}) custom-call(bf16[4096,2560]{1,0:T(8,128)(2,1)} %bitcast.160, bf16[2560,1536]{1,0:T(8,128)(2,1)} %constant_dynamic-update-slice_fusion.1.gate_ref, bf16[2560,1536]{1,0:T(8,128)(2,1)} %constant_dynamic-update-slice_fusion.up_ref), custom_call_target="tpu_custom_call" | custom-call | flops 64424509440 | bytes 58720256 | tf_op jit(solution)/shard_map/expert_in/pallas_call | solution.py:343
  616.8 40.5 %expert_out.1 = bf16[4096,2560]{1,0:T(8,128)(2,1)} custom-call(s32[2]{0:T(128)} %iota_xor_fusion.part_ref, bf16[4096,1536]{1,0:T(8,128)(2,1)} %get-tuple-element.408.act_ref.left_ref, bf16[1536,1280]{1,0:T(8,128)(2,1)} %bitcast.143, bf16[1536,1280]{1,0:T(8,128)(2,1)} %copy-done.8), custom_call_target="tpu_custom_call" | custom-call | flops 32212254720 | bytes 46137344 | tf_op jit(solution)/shard_map/expert_out/pallas_call | solution.py:368
  662.9 23.3 %combine.21 = bf16[14,512,1280]{2,1,0:T(8,128)(2,1)} custom-call(s32[16]{0:T(128)} %get-tuple-element.369.unit_ref, f32[16,512,128]{2,1,0:T(8,128)} %pad.24.info_ref, bf16[16,512,256]{2,1,0:T(8,128)(2,1)} %get-tuple-element.246.act_ref, bf16[256,2560]{1,0:T(8,128)(2,1)} %copy-done.1, bf16[16,256,2560]{2,1,0:T(8,128)(2,1)} %bitcast.89), custom_call_target="tpu_custom_call" | custom-call | flops 9395240960 | bytes 27525120 | tf_op jit(solution)/shard_map/combine/pallas_call | solution.py:575
  717.8 36.5 %enter_back.1 = (bf16[16,256,2560]{2,1,0:T(8,128)(2,1)}, bf16[16,512,512]{2,1,0:T(8,128)(2,1)}) custom-call(f32[16,2,512]{2,1,0:T(2,128)} %pad_maximum_fusion.15.slot_ref, bf16[16,512,2560]{2,1,0:T(8,128)(2,1)} %bitcast.140, bf16[256,2560]{1,0:T(8,128)(2,1)} %copy-done.1, bf16[16,512,512]{2,1,0:T(8,128)(2,1)} %get-tuple-element.269.slope_ref), custom_call_target="tpu_custom_call" | custom-call | flops 21474836480 | bytes 62914560 | tf_op jit(solution)/shard_map/enter_back/pallas_call | solution.py:307
  764.0 26.5 %expert_back.2 = (bf16[4096,1536]{1,0:T(8,128)(2,1)}, bf16[4096,1536]{1,0:T(8,128)(2,1)}) custom-call(s32[2]{0:T(128)} %iota_xor_fusion.part_ref, bf16[4096,2560]{1,0:T(8,128)(2,1)} %bitcast.122, bf16[4096,2560]{1,0:T(8,128)(2,1)} %bitcast.123, bf16[1536,1280]{1,0:T(8,128)(2,1)} %bitcast.144, bf16[1536,1280]{1,0:T(8,128)(2,1)} %copy-done.8, ...), custom_call_target="tpu_custom_call" | custom-call | flops 16106127360 | bytes 35651584 | tf_op jit(solution)/shard_map/expert_back/pallas_call | solution.py:403
  803.5 26.4 %expert_back.3 = (bf16[4096,1536]{1,0:T(8,128)(2,1)}, bf16[4096,1536]{1,0:T(8,128)(2,1)}) custom-call(s32[2]{0:T(128)} %iota_xor_fusion.part_ref, bf16[4096,2560]{1,0:T(8,128)(2,1)} %bitcast.124, bf16[4096,2560]{1,0:T(8,128)(2,1)} %bitcast.125, bf16[1536,1280]{1,0:T(8,128)(2,1)} %bitcast.145, ...), custom_call_target="tpu_custom_call", output_to_operand_aliasing={{0}: (7, {}), {1}: (8, {})} | custom-call | flops 16106127360 | bytes 35651584 | tf_op jit(solution)/shard_map/expert_back/pallas_call | solution.py:403
  918.0 22.7 %expert_grad_rows.6.rest_0_ = bf16[4096,1280]{1,0:T(8,128)(2,1)} custom-call(bf16[4096,1536]{1,0:T(8,128)(2,1)} %get-tuple-element.420.gate_grad_ref.right_ref, bf16[4096,1536]{1,0:T(8,128)(2,1)} %get-tuple-element.436.up_grad_ref.right_ref, bf16[2560,1536]{1,0:T(8,128)(2,1)} %constant_dynamic-update-slice_fusion.1.gate_ref, ...), custom_call_target="tpu_custom_call" | custom-call | flops 16106127360 | bytes 25690112 | tf_op jit(solution)/shard_map/expert_grad_rows/pallas_call | solution.py:440
  978.9 22.8 %expert_grad_rows.7 = bf16[4096,1280]{1,0:T(8,128)(2,1)} custom-call(bf16[4096,1536]{1,0:T(8,128)(2,1)} %get-tuple-element.420.gate_grad_ref.right_ref, bf16[4096,1536]{1,0:T(8,128)(2,1)} %get-tuple-element.436.up_grad_ref.right_ref, bf16[2560,1536]{1,0:T(8,128)(2,1)} %constant_dynamic-update-slice_fusion.1.gate_ref, ...), custom_call_target="tpu_custom_call", output_to_operand_aliasing={{}: (4, {})} | custom-call | flops 16106127360 | bytes 25690112 | tf_op jit(solution)/shard_map/expert_grad_rows/pallas_call | solution.py:440
  1008.1 30.0 %combine.31 = bf16[14,512,1280]{2,1,0:T(8,128)(2,1)} custom-call(s32[16]{0:T(128)} %get-tuple-element.369.unit_ref, f32[16,512,128]{2,1,0:T(8,128)} %pad.24.info_ref, bf16[16,512,512]{2,1,0:T(8,128)(2,1)} %get-tuple-element.358.act_ref, bf16[512,2560]{1,0:T(8,128)(2,1)} %bitcast.130, bf16[16,256,1280]{2,1,0:T(8,128)(2,1)} %bitcast.109, ...), custom_call_target="tpu_custom_call" | custom-call | flops 14092861440 | bytes 27525120 | tf_op jit(solution)/shard_map/combine/pallas_call | solution.py:575
  1180.2 24.5 %weight_grad.15 = f32[1536,1280]{1,0:T(8,128)} custom-call(s32[1]{0:T(128)} %bitcast.30.part_ref, bf16[4096,1536]{1,0:T(8,128)(2,1)} %get-tuple-element.408.act_ref.left_ref, bf16[4096,2560]{1,0:T(8,128)(2,1)} %bitcast.127, bf16[1536,1280]{1,0:T(8,128)(2,1)} %collective-permute-done.32.rest_0_), custom_call_target="tpu_custom_call" | custom-call | flops 16106127360 | bytes 30932992 | tf_op jit(solution)/shard_map/weight_grad/pallas_call | solution.py:621
  1219.7 24.7 %weight_grad.16 = f32[1280,1536]{1,0:T(8,128)} custom-call(s32[1]{0:T(128)} %bitcast.30.part_ref, bf16[4096,2560]{1,0:T(8,128)(2,1)} %bitcast.163, bf16[4096,1536]{1,0:T(8,128)(2,1)} %get-tuple-element.420.gate_grad_ref.right_ref, bf16[1280,1536]{1,0:T(8,128)(2,1)} %collective-permute-done.35.rest_0_), custom_call_target="tpu_custom_call" | custom-call | flops 16106127360 | bytes 30932992 | tf_op jit(solution)/shard_map/weight_grad/pallas_call | solution.py:621
  1296.5 24.2 %weight_grad.17 = f32[1280,1536]{1,0:T(8,128)} custom-call(s32[1]{0:T(128)} %bitcast.30.part_ref, bf16[4096,2560]{1,0:T(8,128)(2,1)} %bitcast.164, bf16[4096,1536]{1,0:T(8,128)(2,1)} %get-tuple-element.436.up_grad_ref.right_ref, bf16[1280,1536]{1,0:T(8,128)(2,1)} %collective-permute-done.40.rest_0_), custom_call_target="tpu_custom_call" | custom-call | flops 16106127360 | bytes 30932992 | tf_op jit(solution)/shard_map/weight_grad/pallas_call | solution.py:621
  1361.2 48.2 %attend_back.1 = (bf16[512,2560]{1,0:T(8,128)(2,1)}, f32[1024,512]{1,0:T(8,128)}, f32[1024,512]{1,0:T(8,128)}) custom-call(s32[1]{0:T(128)} %bitcast.3.offset_ref, bf16[512,2560]{1,0:T(8,128)(2,1)} %project.2.query_ref, bf16[1024,1024]{1,0:T(8,128)(2,1)} %copy-done.16, bf16[1024,1024]{1,0:T(8,128)(2,1)} %copy-done.16, ...), custom_call_target="tpu_custom_call" | custom-call | flops 13421772800 | bytes 14155776 | tf_op jit(solution)/shard_map/attend_back/pallas_call | solution.py:200
  1439.2 41.1 %collective-permute-done.45 = bf16[1024,1024]{1,0:T(8,128)(2,1)} collective-permute-done((bf16[1024,1024]{1,0:T(8,128)(2,1)}, bf16[1024,1024]{1,0:T(8,128)(2,1)}, u32[]{:S(2)}, u32[]{:S(2)}) %collective-permute-start.45) | collective-permute-done | bytes 2097184 | tf_op jit(solution)/shard_map/ppermute | solution.py:780
  1486.6 45.6 %collective-permute-done.46 = bf16[512,2560]{1,0:T(8,128)(2,1)} collective-permute-done((bf16[512,2560]{1,0:T(8,128)(2,1)}, bf16[512,2560]{1,0:T(8,128)(2,1)}, u32[]{:S(2)}, u32[]{:S(2)}) %collective-permute-start.46) | collective-permute-done | bytes 2621472 | tf_op jit(solution)/shard_map/ppermute | solution.py:780
  1554.8 25.3 %collective-permute-done.47.rest_0_ = bf16[1280,512]{1,0:T(8,128)(2,1)S(1)} collective-permute-done((bf16[1280,512]{1,0:T(8,128)(2,1)S(1)}, bf16[1280,512]{1,0:T(8,128)(2,1)S(1)}, u32[]{:S(2)}, u32[]{:S(2)}) %collective-permute-start.47) | collective-permute-done | bytes 1310752 | tf_op jit(solution)/shard_map/ppermute | solution.py:780
  (369 shorter events, 780.8 us)
Async XLA Ops:
  7.2 158.9 %all-gather.5.cloned.1.call-start = ((), (), s32[]{:S(2)}) async-start(), calls=%async_computation.4 | async-start | bytes 19599360 | tf_op jit(solution)/shard_map/all_gather | solution.py:831
  30.0 240.8 %all-gather.7.cloned.1.call-start = ((), (), s32[]{:S(2)}) async-start(), calls=%async_computation.5 | async-start | bytes 13516800 | tf_op jit(solution)/shard_map/all_gather | solution.py:884
  30.9 40.7 %collective-permute-start.1 = (bf16[128,2560]{1,0:T(8,128)(2,1)}, bf16[128,2560]{1,0:T(8,128)(2,1)}, u32[]{:S(2)}, u32[]{:S(2)}) collective-permute-start(bf16[128,2560]{1,0:T(8,128)(2,1)} %pad.23), channel_id=1, source_target_pairs={{0,16},{16,0},{1,17},{17,1},{2,18},{18,2},{3,19},{19,3},{4,20},{20... | collective-permute-start | bytes 1966088 | tf_op jit(solution)/shard_map/ppermute | solution.py:743
  68.0 37.3 %collective-permute-start = (bf16[1280,512]{0,1:T(8,128)(2,1)S(1)}, bf16[1280,512]{0,1:T(8,128)(2,1)S(1)}, u32[]{:S(2)}, u32[]{:S(2)}) collective-permute-start(bf16[1280,512]{0,1:T(8,128)(2,1)S(1)} %bitcast.147), channel_id=1, source_target_pairs={{0,16},{16,0},{1,17},{17,1},{2,18},{18,2},{3,19},{19,3},{4,20},{20... | collective-permute-start | bytes 3932168 | tf_op jit(solution)/shard_map/ppermute | solution.py:743
  166.1 326.0 %all-gather.9.cloned.1.call-start = ((), (), s32[]{:S(2)}) async-start(), calls=%async_computation.6 | async-start | bytes 44564480 | tf_op jit(solution)/shard_map/all_gather | solution.py:902
  286.2 429.6 %all-gather.11.cloned.1.call-start = ((), (), s32[]{:S(2)}) async-start(), calls=%async_computation.7 | async-start | bytes 44564480 | tf_op jit(solution)/shard_map/all_gather | solution.py:906
  286.2 88.2 %collective-permute-start.3 = (bf16[1280,1536]{1,0:T(8,128)(2,1)}, bf16[1280,1536]{1,0:T(8,128)(2,1)}, u32[]{:S(2)}, u32[]{:S(2)}) collective-permute-start(bf16[1280,1536]{1,0:T(8,128)(2,1)} %bitcast.150), channel_id=1, source_target_pairs={{0,16},{16,0},{1,17},{17,1},{2,18},{18,2},{3,19},{19,3},{4,20},{20... | collective-permute-start | bytes 11796488 | tf_op jit(solution)/shard_map/ppermute | solution.py:743
  288.9 169.1 %collective-permute-start.4 = (bf16[1280,1536]{1,0:T(8,128)(2,1)}, bf16[1280,1536]{1,0:T(8,128)(2,1)}, u32[]{:S(2)}, u32[]{:S(2)}) collective-permute-start(bf16[1280,1536]{1,0:T(8,128)(2,1)} %bitcast.152), channel_id=1, source_target_pairs={{0,16},{16,0},{1,17},{17,1},{2,18},{18,2},{3,19},{19,3},{4,20},{20... | collective-permute-start | bytes 11796488 | tf_op jit(solution)/shard_map/ppermute | solution.py:743
  492.1 1193.5 %reduce-scatter.5.cloned.1.call-start = ((), (), s32[]{:S(2)}) async-start(), calls=%async_computation.9 | async-start | bytes 6963200 | tf_op jit(solution)/shard_map/reduce_scatter | solution.py:1077
  496.7 118.2 %collective-permute-start.5 = (bf16[1536,1280]{1,0:T(8,128)(2,1)}, bf16[1536,1280]{1,0:T(8,128)(2,1)S(1)}, u32[]{:S(2)}, u32[]{:S(2)}) collective-permute-start(bf16[1536,1280]{1,0:T(8,128)(2,1)} %bitcast.142), channel_id=1, source_target_pairs={{0,16},{16,0},{1,17},{17,1},{2,18},{18,2},{3,19},{19,3},{4,20},{20... | collective-permute-start | bytes 11796488 | tf_op jit(solution)/shard_map/ppermute | solution.py:743
  686.2 68.0 %collective-permute-start.9 = (bf16[14,512,1280]{2,1,0:T(8,128)(2,1)}, bf16[14,512,1280]{2,1,0:T(8,128)(2,1)}, u32[]{:S(2)}, u32[]{:S(2)}) collective-permute-start(bf16[14,512,1280]{2,1,0:T(8,128)(2,1)} %combine.21), channel_id=1, source_target_pairs={{0,1},{1,0},{2,3},{3,2},{4,5},{5,4},{6,7},{7,6},{8,9},{9,8},{10,11... | collective-permute-start | bytes 55050248 | tf_op jit(solution)/shard_map/ppermute | solution.py:677
  688.2 102.3 %collective-permute-start.12 = (bf16[512,1280]{1,0:T(8,128)(2,1)}, bf16[512,1280]{1,0:T(8,128)(2,1)}, u32[]{:S(2)}, u32[]{:S(2)}) collective-permute-start(bf16[512,1280]{1,0:T(8,128)(2,1)} %get-tuple-element.467), channel_id=1, source_target_pairs={{0,16},{16,0},{1,17},{17,1},{2,18},{18,2},{3,19},{19,3},{4,20},{20... | collective-permute-start | bytes 3932168 | tf_op jit(solution)/shard_map/ppermute | solution.py:780
  689.0 101.5 %collective-permute-start.13 = (bf16[512,2560]{1,0:T(8,128)(2,1)}, bf16[512,2560]{1,0:T(8,128)(2,1)S(1)}, u32[]{:S(2)}, u32[]{:S(2)}) collective-permute-start(bf16[512,2560]{1,0:T(8,128)(2,1)} %attend.1), channel_id=1, source_target_pairs={{0,16},{16,0},{1,17},{17,1},{2,18},{18,2},{3,19},{19,3},{4,20},{20... | collective-permute-start | bytes 7864328 | tf_op jit(solution)/shard_map/ppermute | solution.py:780
  715.8 38.5 %collective-permute-start.7 = (bf16[1,512,1280]{2,1,0:T(8,128)(2,1)}, bf16[1,512,1280]{2,1,0:T(8,128)(2,1)}, u32[]{:S(2)}, u32[]{:S(2)}) collective-permute-start(bf16[1,512,1280]{2,1,0:T(8,128)(2,1)} %get-tuple-element.263), channel_id=1, source_target_pairs={{0,4},{1,5},{4,8},{5,9},{8,12},{9,13},{12,14},{13,15},{14,10},{15,... | collective-permute-start | bytes 3932168 | tf_op jit(solution)/shard_map/ppermute | solution.py:674
  1038.1 41.6 %collective-permute-start.27 = (bf16[14,512,1280]{2,1,0:T(8,128)(2,1)}, bf16[14,512,1280]{2,1,0:T(8,128)(2,1)}, u32[]{:S(2)}, u32[]{:S(2)}) collective-permute-start(bf16[14,512,1280]{2,1,0:T(8,128)(2,1)} %combine.31), channel_id=1, source_target_pairs={{0,1},{1,0},{2,3},{3,2},{4,5},{5,4},{6,7},{7,6},{8,9},{9,8},{10,11... | collective-permute-start | bytes 55050248 | tf_op jit(solution)/shard_map/ppermute | solution.py:677
  1038.7 139.5 %collective-permute-start.32 = (bf16[1536,1280]{1,0:T(8,128)(2,1)}, bf16[1536,1280]{1,0:T(8,128)(2,1)}, u32[]{:S(2)}, u32[]{:S(2)}) collective-permute-start(bf16[1536,1280]{1,0:T(8,128)(2,1)} %weight_grad.10), channel_id=1, source_target_pairs={{0,16},{16,0},{1,17},{17,1},{2,18},{18,2},{3,19},{19,3},{4,20},{20... | collective-permute-start | bytes 11796488 | tf_op jit(solution)/shard_map/ppermute | solution.py:780
  1091.2 126.3 %collective-permute-start.35 = (bf16[1280,1536]{1,0:T(8,128)(2,1)}, bf16[1280,1536]{1,0:T(8,128)(2,1)}, u32[]{:S(2)}, u32[]{:S(2)}) collective-permute-start(bf16[1280,1536]{1,0:T(8,128)(2,1)} %weight_grad.11), channel_id=1, source_target_pairs={{0,16},{16,0},{1,17},{17,1},{2,18},{18,2},{3,19},{19,3},{4,20},{20... | collective-permute-start | bytes 11796488 | tf_op jit(solution)/shard_map/ppermute | solution.py:780
  1129.8 37.9 %collective-permute-start.30 = (bf16[1,512,1280]{2,1,0:T(8,128)(2,1)}, bf16[1,512,1280]{2,1,0:T(8,128)(2,1)S(1)}, u32[]{:S(2)}, u32[]{:S(2)}) collective-permute-start(bf16[1,512,1280]{2,1,0:T(8,128)(2,1)} %get-tuple-element.394), channel_id=1, source_target_pairs={{0,4},{1,5},{4,8},{5,9},{8,12},{9,13},{12,14},{13,15},{14,10},{15,... | collective-permute-start | bytes 3932168 | tf_op jit(solution)/shard_map/ppermute | solution.py:674
  1131.9 162.6 %collective-permute-start.40 = (bf16[1280,1536]{1,0:T(8,128)(2,1)}, bf16[1280,1536]{1,0:T(8,128)(2,1)}, u32[]{:S(2)}, u32[]{:S(2)}) collective-permute-start(bf16[1280,1536]{1,0:T(8,128)(2,1)} %weight_grad.12), channel_id=1, source_target_pairs={{0,16},{16,0},{1,17},{17,1},{2,18},{18,2},{3,19},{19,3},{4,20},{20... | collective-permute-start | bytes 11796488 | tf_op jit(solution)/shard_map/ppermute | solution.py:780
  1358.8 55.3 %collective-permute-start.44 = (bf16[512,1280]{1,0:T(8,128)(2,1)S(1)}, bf16[512,1280]{1,0:T(8,128)(2,1)S(1)}, u32[]{:S(2)}, u32[]{:S(2)}) collective-permute-start(bf16[512,1280]{1,0:T(8,128)(2,1)S(1)} %get-tuple-element.465), channel_id=1, source_target_pairs={{0,16},{16,0},{1,17},{17,1},{2,18},{18,2},{3,19},{19,3},{4,20},{20... | collective-permute-start | bytes 3932168 | tf_op jit(solution)/shard_map/ppermute | solution.py:780
  1427.5 264.8 %reduce-scatter.3.cloned.1.call-start = ((), (), s32[]{:S(2)}) async-start(), calls=%async_computation.8 | async-start | bytes 10096640 | tf_op jit(solution)/shard_map/reduce_scatter | solution.py:1093
  1431.4 48.9 %collective-permute-start.45 = (bf16[1024,1024]{1,0:T(8,128)(2,1)}, bf16[1024,1024]{1,0:T(8,128)(2,1)}, u32[]{:S(2)}, u32[]{:S(2)}) collective-permute-start(bf16[1024,1024]{1,0:T(8,128)(2,1)} %convert_element_type.136), channel_id=1, source_target_pairs={{0,16},{16,0},{1,17},{17,1},{2,18},{18,2},{3,19},{19,3},{4,20},{20... | collective-permute-start | bytes 6291464 | tf_op jit(solution)/shard_map/ppermute | solution.py:780
  1432.6 99.6 %collective-permute-start.46 = (bf16[512,2560]{1,0:T(8,128)(2,1)}, bf16[512,2560]{1,0:T(8,128)(2,1)}, u32[]{:S(2)}, u32[]{:S(2)}) collective-permute-start(bf16[512,2560]{1,0:T(8,128)(2,1)} %get-tuple-element.445), channel_id=1, source_target_pairs={{0,16},{16,0},{1,17},{17,1},{2,18},{18,2},{3,19},{19,3},{4,20},{20... | collective-permute-start | bytes 7864328 | tf_op jit(solution)/shard_map/ppermute | solution.py:780
  1602.9 47.9 %all-to-all-start.1 = ((bf16[16,80,512]{2,1,0:T(8,128)(2,1)}), bf16[16,80,512]{2,1,0:T(8,128)(2,1)S(1)}, u32[]{:S(2)}, u32[]{:S(2)}) async-start(bf16[16,80,512]{2,1,0:T(8,128)(2,1)} %bitcast.36), calls=%async_computation.3 | async-start | bytes 2621440 | tf_op jit(solution)/shard_map/all_to_all | solution.py:1113
  (98 other events, 1492.9 us)
Sparse Core Ops, SparseCore 0:
  11.6 154.4 all-gather.4
  169.0 101.7 all-gather.6
  286.3 205.7 all-gather.8
  493.6 222.1 all-gather.10
  1427.6 85.3 reduce-scatter.4
  1552.5 139.7 reduce-scatter.2

commit v6 on v5

--- a/solution.py
+++ b/solution.py
@@ -1043,6 +1043,9 @@
     expert_up_grad = ring_step(rings, total(0), received, grad_eu, up_arrived)[None]
     if pair:
         grad_two = grad_ring.finish()
+        grad_two, shared_in_arrived, shared_down_arrived = tie(
+            grad_two, shared_in_arrived, shared_down_arrived
+        )
     else:
         grad_two = sum_over_exp(grad_part)
     ffn_gain_term = jnp.sum(grad_two * middle * inverse_two, axis=0)
@@ -1060,6 +1063,8 @@
         gain_term = ffn_gain_term[:, None]
     gain_term = jnp.pad(gain_term, ((0, 0), (0, 127))).astype(jnp.bfloat16)
 
+    shared_in_grad = ctx_total(rows_all, shared_back, 0, shared_in_arrived)
+    sum_sd = ctx_total(shared_act, grad_all, 0, shared_down_arrived)
     grad_query_raw, key_terms, value_terms = attend_back(
         offset_array, query, key_value, attended_gradient, tables, key_tables
     )
@@ -1075,6 +1080,7 @@
             jnp.concatenate([attended_low, attended_other], axis=0),
         )
         sum_o = lax.psum_scatter(output_term, "exp", scatter_dimension=0, tiled=True)
+        query_other, shared_in_grad, sum_sd = tie(query_other, shared_in_grad, sum_sd)
         key_value_all = (key_value_grad + key_value_other.astype(jnp.float32)).astype(jnp.bfloat16)
         key_value_raw = lax.dynamic_slice_in_dim(key_value_all, offset, tokens, axis=0)
         key_value_both = jnp.concatenate(
@@ -1108,8 +1114,8 @@
     )
     attn_gain_grad = jnp.sum(sum_in[:, :edge] * attn_in.astype(jnp.float32), axis=1) / own_gain
 
-    shared_in_grad = ctx_total(rows_all, shared_back, 0, shared_in_arrived).astype(jnp.bfloat16)
-    sum_sd = ctx_total(shared_act, grad_all, 0, shared_down_arrived)[:own_hidden]
+    shared_in_grad = shared_in_grad.astype(jnp.bfloat16)
+    sum_sd = sum_sd[:own_hidden]
     shared_in_grad = lax.all_to_all(
         shared_in_grad.reshape(exp_count, own_rows, 2 * padded),
         "exp",

time: 1710 us -> 1710 us (level)
    ppermute x11, waiting for transfers between devices: 122 us -> 55.2 us  [ctx_send(): return lax.ppermute(theirs, 'ctx', [(0, 1), (1, 0)])]
    reduce_scatter x1, waiting for transfers between devices: 4.6 us -> 65.9 us  [on_device(): sum_in = lax.psum_scatter(in_term, 'exp', scatter_dimension=0, tiled=True)]
  transfers between devices with their start and end apart: 57 -> 57, of which waited for: 41 -> 39; matrix products, arithmetic and copies ran while one was open for 8% -> 8% of each run, Pallas kernels for 45% -> 46%
where the time goes in v6:
time: 1710 us; the launch traced here: 1700 us
  Pallas kernels  864 us (51%)
  waiting for transfers between devices  548 us (32%)
  other arithmetic  88.1 us (5%)
  local copies, waits for them, and re-layouts  74.7 us (4%)
  starting transfers between devices  62.8 us (4%)
  matrix products  41.5 us (2%)
  between operations  17.1 us (1%)
    pallas_call x10, Pallas kernels, weight_grad(): pl.pallas_call(weight_grad_kernel, grid_spec=pltpu.PrefetchScalarGridSpec...  211 us
    ppermute x6, waiting for transfers between devices, ctx_fetch(): return lax.ppermute(part, 'ctx', [(0, 1), (1, 0)])  196 us
    pallas_call x20, Pallas kernels, combine(): pl.pallas_call(functools.partial(combine_kernel, scaled, len(rows), len(a...  193 us
    pallas_call x4, Pallas kernels, expert_grad_rows(): pl.pallas_call(expert_rows_kernel, grid=(count // 2 // high,), in_specs=[...  90.5 us
    pallas_call x1, Pallas kernels, expert_in(): pl.pallas_call(expert_in_kernel, grid=(count // high, hidden // wide), in...  75.7 us
    reduce_scatter x1, waiting for transfers between devices, on_device(): sum_in = lax.psum_scatter(in_term, 'exp', scatter_dimension=0, tiled=True)  65.9 us
    all_gather x1, waiting for transfers between devices, on_device(): lax.all_gather(jnp.concatenate([attn_in, routing.reshape(own_rows, routin...  60.5 us
    ppermute x28, waiting for transfers between devices, move(): lax.ppermute(total, 'exp', way)  59.6 us
  transfers between devices with their start and end apart: 57, of which 39 were waited for; matrix products, arithmetic and copies ran while one was open for 8% of the time, Pallas kernels for 46%

profile of v6, /device:TPU:0, one launch (start us, length us, event | category | flops | bytes accessed | tf_op | source)
XLA Modules:
  0.0 1696.4 jit_solution(5602266181080437451)
XLA Ops:
  33.6 26.0 %all-to-all-done = bf16[16,80,384]{2,1,0:T(8,128)(2,1)} async-done(((bf16[16,80,384]{2,1,0:T(8,128)(2,1)}), bf16[16,80,384]{2,1,0:T(8,128)(2,1)}, u32[]{:S(2)}, u32[]{:S(2)}) %all-to-all-start) | async-done | bytes 983072 | tf_op jit(solution)/shard_map/all_to_all | solution.py:855
  74.2 31.1 %collective-permute-done = bf16[1280,512]{0,1:T(8,128)(2,1)S(1)} collective-permute-done((bf16[1280,512]{0,1:T(8,128)(2,1)S(1)}, bf16[1280,512]{0,1:T(8,128)(2,1)S(1)}, u32[]{:S(2)}, u32[]{:S(2)}) %collective-permute-start) | collective-permute-done | bytes 1310752 | tf_op jit(solution)/shard_map/ppermute | solution.py:743
  105.6 60.5 %all-gather.5.cloned.1.call-done.weight_ref = bf16[2560,3712]{1,0:T(8,128)(2,1)} async-done(((bf16[80,3712]{1,0:T(8,128)(2,1)}), bf16[2560,3712]{1,0:T(8,128)(2,1)}) %all-gather.5.cloned.1.call-update) | async-done | bytes 19005456 | tf_op jit(solution)/shard_map/all_gather | solution.py:831
  209.3 29.0 %attend.1 = bf16[512,2560]{1,0:T(8,128)(2,1)} custom-call(s32[1]{0:T(128)} %bitcast.3.offset_ref, bf16[512,2560]{1,0:T(8,128)(2,1)} %project.2.query_ref, bf16[1024,1024]{1,0:T(8,128)(2,1)} %copy-done.20, bf16[1024,1024]{1,0:T(8,128)(2,1)} %copy-done.20), custom_call_target="tpu_custom_call" | custom-call | flops 5368709120 | bytes 7340032 | tf_op jit(solution)/shard_map/attend/pallas_call | solution.py:138
  238.3 32.4 %all-gather.7.cloned.1.call-done = bf16[2560,2560]{1,0:T(8,128)(2,1)} async-done(((bf16[80,2560]{1,0:T(8,128)(2,1)}), bf16[2560,2560]{1,0:T(8,128)(2,1)}) %all-gather.7.cloned.1.call-update) | async-done | bytes 13107216 | tf_op jit(solution)/shard_map/all_gather | solution.py:884
  298.6 75.8 %collective-permute-done.3 = bf16[1280,1536]{1,0:T(8,128)(2,1)} collective-permute-done((bf16[1280,1536]{1,0:T(8,128)(2,1)}, bf16[1280,1536]{1,0:T(8,128)(2,1)}, u32[]{:S(2)}, u32[]{:S(2)}) %collective-permute-start.3) | collective-permute-done | bytes 3932192 | tf_op jit(solution)/shard_map/ppermute | solution.py:743
  385.7 72.3 %collective-permute-done.4 = bf16[1280,1536]{1,0:T(8,128)(2,1)} collective-permute-done((bf16[1280,1536]{1,0:T(8,128)(2,1)}, bf16[1280,1536]{1,0:T(8,128)(2,1)}, u32[]{:S(2)}, u32[]{:S(2)}) %collective-permute-start.4) | collective-permute-done | bytes 3932192 | tf_op jit(solution)/shard_map/ppermute | solution.py:743
  469.4 22.7 %all-gather.9.cloned.1.call-done.left_ref = bf16[8192,2560]{1,0:T(8,128)(2,1)} async-done(((bf16[512,2560]{1,0:T(8,128)(2,1)}), bf16[8192,2560]{1,0:T(8,128)(2,1)}) %all-gather.9.cloned.1.call-update) | async-done | bytes 41943056 | tf_op jit(solution)/shard_map/all_gather | solution.py:902
  498.1 41.0 %enter.1 = (bf16[16,256,2560]{2,1,0:T(8,128)(2,1)}, bf16[16,512,256]{2,1,0:T(8,128)(2,1)}, bf16[16,512,512]{2,1,0:T(8,128)(2,1)}) custom-call(f32[16,2,512]{2,1,0:T(2,128)} %pad_maximum_fusion.15.slot_ref, bf16[16,512,2560]{2,1,0:T(8,128)(2,1)} %bitcast.128, bf16[512,2560]{1,0:T(8,128)(2,1)} %bitcast.117), custom_call_target="tpu_custom_call" | custom-call | flops 32212254720 | bytes 62914560 | tf_op jit(solution)/shard_map/enter/pallas_call | solution.py:265
  539.1 75.7 %expert_in.1 = (bf16[4096,1536]{1,0:T(8,128)(2,1)}, bf16[4096,1536]{1,0:T(8,128)(2,1)}, bf16[4096,1536]{1,0:T(8,128)(2,1)}) custom-call(bf16[4096,2560]{1,0:T(8,128)(2,1)} %bitcast.152, bf16[2560,1536]{1,0:T(8,128)(2,1)} %constant_dynamic-update-slice_fusion.1.gate_ref, bf16[2560,1536]{1,0:T(8,128)(2,1)} %constant_dynamic-update-slice_fusion.up_ref), custom_call_target="tpu_custom_call" | custom-call | flops 64424509440 | bytes 58720256 | tf_op jit(solution)/shard_map/expert_in/pallas_call | solution.py:343
  616.7 40.6 %expert_out.1 = bf16[4096,2560]{1,0:T(8,128)(2,1)} custom-call(s32[2]{0:T(128)} %iota_xor_fusion.part_ref, bf16[4096,1536]{1,0:T(8,128)(2,1)} %get-tuple-element.414.act_ref.left_ref, bf16[1536,1280]{1,0:T(8,128)(2,1)} %bitcast.136, bf16[1536,1280]{1,0:T(8,128)(2,1)} %copy-done.8), custom_call_target="tpu_custom_call" | custom-call | flops 32212254720 | bytes 46137344 | tf_op jit(solution)/shard_map/expert_out/pallas_call | solution.py:368
  662.9 23.3 %combine.21 = bf16[14,512,1280]{2,1,0:T(8,128)(2,1)} custom-call(s32[16]{0:T(128)} %get-tuple-element.375.unit_ref, f32[16,512,128]{2,1,0:T(8,128)} %pad.24.info_ref, bf16[16,512,256]{2,1,0:T(8,128)(2,1)} %get-tuple-element.252.act_ref, bf16[256,2560]{1,0:T(8,128)(2,1)} %copy-done.1, bf16[16,256,2560]{2,1,0:T(8,128)(2,1)} %bitcast.78), custom_call_target="tpu_custom_call" | custom-call | flops 9395240960 | bytes 27525120 | tf_op jit(solution)/shard_map/combine/pallas_call | solution.py:575
  717.8 36.5 %enter_back.1 = (bf16[16,256,2560]{2,1,0:T(8,128)(2,1)}, bf16[16,512,512]{2,1,0:T(8,128)(2,1)}) custom-call(f32[16,2,512]{2,1,0:T(2,128)} %pad_maximum_fusion.15.slot_ref, bf16[16,512,2560]{2,1,0:T(8,128)(2,1)} %bitcast.129, bf16[256,2560]{1,0:T(8,128)(2,1)} %copy-done.1, bf16[16,512,512]{2,1,0:T(8,128)(2,1)} %get-tuple-element.275.slope_ref), custom_call_target="tpu_custom_call" | custom-call | flops 21474836480 | bytes 62914560 | tf_op jit(solution)/shard_map/enter_back/pallas_call | solution.py:307
  764.0 26.6 %expert_back.2 = (bf16[4096,1536]{1,0:T(8,128)(2,1)}, bf16[4096,1536]{1,0:T(8,128)(2,1)}) custom-call(s32[2]{0:T(128)} %iota_xor_fusion.part_ref, bf16[4096,2560]{1,0:T(8,128)(2,1)} %bitcast.111, bf16[4096,2560]{1,0:T(8,128)(2,1)} %bitcast.112, bf16[1536,1280]{1,0:T(8,128)(2,1)} %bitcast.137, bf16[1536,1280]{1,0:T(8,128)(2,1)} %copy-done.8, ...), custom_call_target="tpu_custom_call" | custom-call | flops 16106127360 | bytes 35651584 | tf_op jit(solution)/shard_map/expert_back/pallas_call | solution.py:403
  803.5 26.3 %expert_back.3 = (bf16[4096,1536]{1,0:T(8,128)(2,1)}, bf16[4096,1536]{1,0:T(8,128)(2,1)}) custom-call(s32[2]{0:T(128)} %iota_xor_fusion.part_ref, bf16[4096,2560]{1,0:T(8,128)(2,1)} %bitcast.113, bf16[4096,2560]{1,0:T(8,128)(2,1)} %bitcast.114, bf16[1536,1280]{1,0:T(8,128)(2,1)} %bitcast.138, ...), custom_call_target="tpu_custom_call", output_to_operand_aliasing={{0}: (7, {}), {1}: (8, {})} | custom-call | flops 16106127360 | bytes 35651584 | tf_op jit(solution)/shard_map/expert_back/pallas_call | solution.py:403
  918.2 22.7 %expert_grad_rows.6.rest_0_ = bf16[4096,1280]{1,0:T(8,128)(2,1)} custom-call(bf16[4096,1536]{1,0:T(8,128)(2,1)} %get-tuple-element.426.gate_grad_ref.right_ref, bf16[4096,1536]{1,0:T(8,128)(2,1)} %get-tuple-element.442.up_grad_ref.right_ref, bf16[2560,1536]{1,0:T(8,128)(2,1)} %constant_dynamic-update-slice_fusion.1.gate_ref, ...), custom_call_target="tpu_custom_call" | custom-call | flops 16106127360 | bytes 25690112 | tf_op jit(solution)/shard_map/expert_grad_rows/pallas_call | solution.py:440
  979.2 22.8 %expert_grad_rows.7 = bf16[4096,1280]{1,0:T(8,128)(2,1)} custom-call(bf16[4096,1536]{1,0:T(8,128)(2,1)} %get-tuple-element.426.gate_grad_ref.right_ref, bf16[4096,1536]{1,0:T(8,128)(2,1)} %get-tuple-element.442.up_grad_ref.right_ref, bf16[2560,1536]{1,0:T(8,128)(2,1)} %constant_dynamic-update-slice_fusion.1.gate_ref, ...), custom_call_target="tpu_custom_call", output_to_operand_aliasing={{}: (4, {})} | custom-call | flops 16106127360 | bytes 25690112 | tf_op jit(solution)/shard_map/expert_grad_rows/pallas_call | solution.py:440
  1008.5 30.0 %combine.31 = bf16[14,512,1280]{2,1,0:T(8,128)(2,1)} custom-call(s32[16]{0:T(128)} %get-tuple-element.375.unit_ref, f32[16,512,128]{2,1,0:T(8,128)} %pad.24.info_ref, bf16[16,512,512]{2,1,0:T(8,128)(2,1)} %get-tuple-element.364.act_ref, bf16[512,2560]{1,0:T(8,128)(2,1)} %bitcast.119, bf16[16,256,1280]{2,1,0:T(8,128)(2,1)} %bitcast.98, ...), custom_call_target="tpu_custom_call" | custom-call | flops 14092861440 | bytes 27525120 | tf_op jit(solution)/shard_map/combine/pallas_call | solution.py:575
  1180.7 24.5 %weight_grad.15 = f32[1536,1280]{1,0:T(8,128)} custom-call(s32[1]{0:T(128)} %bitcast.30.part_ref, bf16[4096,1536]{1,0:T(8,128)(2,1)} %get-tuple-element.414.act_ref.left_ref, bf16[4096,2560]{1,0:T(8,128)(2,1)} %bitcast.116, bf16[1536,1280]{1,0:T(8,128)(2,1)} %collective-permute-done.32.rest_0_), custom_call_target="tpu_custom_call" | custom-call | flops 16106127360 | bytes 30932992 | tf_op jit(solution)/shard_map/weight_grad/pallas_call | solution.py:621
  1220.2 24.8 %weight_grad.16 = f32[1280,1536]{1,0:T(8,128)} custom-call(s32[1]{0:T(128)} %bitcast.30.part_ref, bf16[4096,2560]{1,0:T(8,128)(2,1)} %bitcast.155, bf16[4096,1536]{1,0:T(8,128)(2,1)} %get-tuple-element.426.gate_grad_ref.right_ref, bf16[1280,1536]{1,0:T(8,128)(2,1)} %collective-permute-done.35.rest_0_), custom_call_target="tpu_custom_call" | custom-call | flops 16106127360 | bytes 30932992 | tf_op jit(solution)/shard_map/weight_grad/pallas_call | solution.py:621
  1297.7 24.2 %weight_grad.17 = f32[1280,1536]{1,0:T(8,128)} custom-call(s32[1]{0:T(128)} %bitcast.30.part_ref, bf16[4096,2560]{1,0:T(8,128)(2,1)} %bitcast.156, bf16[4096,1536]{1,0:T(8,128)(2,1)} %get-tuple-element.442.up_grad_ref.right_ref, bf16[1280,1536]{1,0:T(8,128)(2,1)} %collective-permute-done.40.rest_0_), custom_call_target="tpu_custom_call" | custom-call | flops 16106127360 | bytes 30932992 | tf_op jit(solution)/shard_map/weight_grad/pallas_call | solution.py:621
  1364.2 48.2 %attend_back.1 = (bf16[512,2560]{1,0:T(8,128)(2,1)}, f32[1024,512]{1,0:T(8,128)}, f32[1024,512]{1,0:T(8,128)}) custom-call(s32[1]{0:T(128)} %bitcast.3.offset_ref, bf16[512,2560]{1,0:T(8,128)(2,1)} %project.2.query_ref, bf16[1024,1024]{1,0:T(8,128)(2,1)} %copy-done.20, bf16[1024,1024]{1,0:T(8,128)(2,1)} %copy-done.20, ...), custom_call_target="tpu_custom_call" | custom-call | flops 13421772800 | bytes 14155776 | tf_op jit(solution)/shard_map/attend_back/pallas_call | solution.py:200
  1489.6 47.4 %collective-permute-done.48 = bf16[512,2560]{1,0:T(8,128)(2,1)S(1)} collective-permute-done((bf16[512,2560]{1,0:T(8,128)(2,1)}, bf16[512,2560]{1,0:T(8,128)(2,1)S(1)}, u32[]{:S(2)}, u32[]{:S(2)}) %collective-permute-start.48) | collective-permute-done | bytes 2621472 | tf_op jit(solution)/shard_map/ppermute | solution.py:780
  1619.1 65.9 %reduce-scatter.3.cloned.1.call-done = bf16[80,3712]{1,0:T(8,128)(2,1)} async-done(((bf16[1280,3712]{1,0:T(8,128)(2,1)}), bf16[80,3712]{1,0:T(8,128)(2,1)}) %reduce-scatter.3.cloned.1.call-update) | async-done | bytes 593936 | tf_op jit(solution)/shard_map/reduce_scatter | solution.py:1099
  (365 shorter events, 749.2 us)
Async XLA Ops:
  7.2 158.9 %all-gather.5.cloned.1.call-start = ((), (), s32[]{:S(2)}) async-start(), calls=%async_computation.4 | async-start | bytes 19599360 | tf_op jit(solution)/shard_map/all_gather | solution.py:831
  30.0 240.7 %all-gather.7.cloned.1.call-start = ((), (), s32[]{:S(2)}) async-start(), calls=%async_computation.5 | async-start | bytes 13516800 | tf_op jit(solution)/shard_map/all_gather | solution.py:884
  30.9 40.7 %collective-permute-start.1 = (bf16[128,2560]{1,0:T(8,128)(2,1)}, bf16[128,2560]{1,0:T(8,128)(2,1)}, u32[]{:S(2)}, u32[]{:S(2)}) collective-permute-start(bf16[128,2560]{1,0:T(8,128)(2,1)} %pad.23), channel_id=1, source_target_pairs={{0,16},{16,0},{1,17},{17,1},{2,18},{18,2},{3,19},{19,3},{4,20},{20... | collective-permute-start | bytes 1966088 | tf_op jit(solution)/shard_map/ppermute | solution.py:743
  166.1 326.0 %all-gather.9.cloned.1.call-start = ((), (), s32[]{:S(2)}) async-start(), calls=%async_computation.6 | async-start | bytes 44564480 | tf_op jit(solution)/shard_map/all_gather | solution.py:902
  286.2 429.6 %all-gather.11.cloned.1.call-start = ((), (), s32[]{:S(2)}) async-start(), calls=%async_computation.7 | async-start | bytes 44564480 | tf_op jit(solution)/shard_map/all_gather | solution.py:906
  286.2 88.2 %collective-permute-start.3 = (bf16[1280,1536]{1,0:T(8,128)(2,1)}, bf16[1280,1536]{1,0:T(8,128)(2,1)}, u32[]{:S(2)}, u32[]{:S(2)}) collective-permute-start(bf16[1280,1536]{1,0:T(8,128)(2,1)} %bitcast.144), channel_id=1, source_target_pairs={{0,16},{16,0},{1,17},{17,1},{2,18},{18,2},{3,19},{19,3},{4,20},{20... | collective-permute-start | bytes 11796488 | tf_op jit(solution)/shard_map/ppermute | solution.py:743
  288.9 169.1 %collective-permute-start.4 = (bf16[1280,1536]{1,0:T(8,128)(2,1)}, bf16[1280,1536]{1,0:T(8,128)(2,1)}, u32[]{:S(2)}, u32[]{:S(2)}) collective-permute-start(bf16[1280,1536]{1,0:T(8,128)(2,1)} %bitcast.146), channel_id=1, source_target_pairs={{0,16},{16,0},{1,17},{17,1},{2,18},{18,2},{3,19},{19,3},{4,20},{20... | collective-permute-start | bytes 11796488 | tf_op jit(solution)/shard_map/ppermute | solution.py:743
  492.1 1125.0 %reduce-scatter.5.cloned.1.call-start = ((), (), s32[]{:S(2)}) async-start(), calls=%async_computation.9 | async-start | bytes 6963200 | tf_op jit(solution)/shard_map/reduce_scatter | solution.py:1082
  496.7 118.1 %collective-permute-start.5 = (bf16[1536,1280]{1,0:T(8,128)(2,1)}, bf16[1536,1280]{1,0:T(8,128)(2,1)S(1)}, u32[]{:S(2)}, u32[]{:S(2)}) collective-permute-start(bf16[1536,1280]{1,0:T(8,128)(2,1)} %bitcast.135), channel_id=1, source_target_pairs={{0,16},{16,0},{1,17},{17,1},{2,18},{18,2},{3,19},{19,3},{4,20},{20... | collective-permute-start | bytes 11796488 | tf_op jit(solution)/shard_map/ppermute | solution.py:743
  686.2 68.0 %collective-permute-start.9 = (bf16[14,512,1280]{2,1,0:T(8,128)(2,1)}, bf16[14,512,1280]{2,1,0:T(8,128)(2,1)}, u32[]{:S(2)}, u32[]{:S(2)}) collective-permute-start(bf16[14,512,1280]{2,1,0:T(8,128)(2,1)} %combine.21), channel_id=1, source_target_pairs={{0,1},{1,0},{2,3},{3,2},{4,5},{5,4},{6,7},{7,6},{8,9},{9,8},{10,11... | collective-permute-start | bytes 55050248 | tf_op jit(solution)/shard_map/ppermute | solution.py:677
  688.2 102.3 %collective-permute-start.12 = (bf16[512,1280]{1,0:T(8,128)(2,1)}, bf16[512,1280]{1,0:T(8,128)(2,1)}, u32[]{:S(2)}, u32[]{:S(2)}) collective-permute-start(bf16[512,1280]{1,0:T(8,128)(2,1)} %get-tuple-element.479), channel_id=1, source_target_pairs={{0,16},{16,0},{1,17},{17,1},{2,18},{18,2},{3,19},{19,3},{4,20},{20... | collective-permute-start | bytes 3932168 | tf_op jit(solution)/shard_map/ppermute | solution.py:780
  689.0 101.5 %collective-permute-start.13 = (bf16[512,2560]{1,0:T(8,128)(2,1)}, bf16[512,2560]{1,0:T(8,128)(2,1)S(1)}, u32[]{:S(2)}, u32[]{:S(2)}) collective-permute-start(bf16[512,2560]{1,0:T(8,128)(2,1)} %attend.1), channel_id=1, source_target_pairs={{0,16},{16,0},{1,17},{17,1},{2,18},{18,2},{3,19},{19,3},{4,20},{20... | collective-permute-start | bytes 7864328 | tf_op jit(solution)/shard_map/ppermute | solution.py:780
  715.8 38.5 %collective-permute-start.7 = (bf16[1,512,1280]{2,1,0:T(8,128)(2,1)}, bf16[1,512,1280]{2,1,0:T(8,128)(2,1)}, u32[]{:S(2)}, u32[]{:S(2)}) collective-permute-start(bf16[1,512,1280]{2,1,0:T(8,128)(2,1)} %get-tuple-element.269), channel_id=1, source_target_pairs={{0,4},{1,5},{4,8},{5,9},{8,12},{9,13},{12,14},{13,15},{14,10},{15,... | collective-permute-start | bytes 3932168 | tf_op jit(solution)/shard_map/ppermute | solution.py:674
  1038.5 41.5 %collective-permute-start.27 = (bf16[14,512,1280]{2,1,0:T(8,128)(2,1)}, bf16[14,512,1280]{2,1,0:T(8,128)(2,1)}, u32[]{:S(2)}, u32[]{:S(2)}) collective-permute-start(bf16[14,512,1280]{2,1,0:T(8,128)(2,1)} %combine.31), channel_id=1, source_target_pairs={{0,1},{1,0},{2,3},{3,2},{4,5},{5,4},{6,7},{7,6},{8,9},{9,8},{10,11... | collective-permute-start | bytes 55050248 | tf_op jit(solution)/shard_map/ppermute | solution.py:677
  1039.0 139.6 %collective-permute-start.32 = (bf16[1536,1280]{1,0:T(8,128)(2,1)}, bf16[1536,1280]{1,0:T(8,128)(2,1)}, u32[]{:S(2)}, u32[]{:S(2)}) collective-permute-start(bf16[1536,1280]{1,0:T(8,128)(2,1)} %weight_grad.10), channel_id=1, source_target_pairs={{0,16},{16,0},{1,17},{17,1},{2,18},{18,2},{3,19},{19,3},{4,20},{20... | collective-permute-start | bytes 11796488 | tf_op jit(solution)/shard_map/ppermute | solution.py:780
  1091.6 126.5 %collective-permute-start.35 = (bf16[1280,1536]{1,0:T(8,128)(2,1)}, bf16[1280,1536]{1,0:T(8,128)(2,1)}, u32[]{:S(2)}, u32[]{:S(2)}) collective-permute-start(bf16[1280,1536]{1,0:T(8,128)(2,1)} %weight_grad.11), channel_id=1, source_target_pairs={{0,16},{16,0},{1,17},{17,1},{2,18},{18,2},{3,19},{19,3},{4,20},{20... | collective-permute-start | bytes 11796488 | tf_op jit(solution)/shard_map/ppermute | solution.py:780
  1132.1 163.6 %collective-permute-start.40 = (bf16[1280,1536]{1,0:T(8,128)(2,1)}, bf16[1280,1536]{1,0:T(8,128)(2,1)}, u32[]{:S(2)}, u32[]{:S(2)}) collective-permute-start(bf16[1280,1536]{1,0:T(8,128)(2,1)} %weight_grad.12), channel_id=1, source_target_pairs={{0,16},{16,0},{1,17},{17,1},{2,18},{18,2},{3,19},{19,3},{4,20},{20... | collective-permute-start | bytes 11796488 | tf_op jit(solution)/shard_map/ppermute | solution.py:780
  1266.7 70.3 %collective-permute-start.43 = (bf16[1280,512]{1,0:T(8,128)(2,1)}, bf16[1280,512]{1,0:T(8,128)(2,1)S(1)}, u32[]{:S(2)}, u32[]{:S(2)}) collective-permute-start(bf16[1280,512]{1,0:T(8,128)(2,1)} %weight_grad.13), channel_id=1, source_target_pairs={{0,16},{16,0},{1,17},{17,1},{2,18},{18,2},{3,19},{19,3},{4,20},{20... | collective-permute-start | bytes 3932168 | tf_op jit(solution)/shard_map/ppermute | solution.py:780
  1267.0 69.9 %collective-permute-start.44 = (bf16[128,2560]{1,0:T(8,128)(2,1)}, bf16[128,2560]{1,0:T(8,128)(2,1)}, u32[]{:S(2)}, u32[]{:S(2)}) collective-permute-start(bf16[128,2560]{1,0:T(8,128)(2,1)} %weight_grad.14), channel_id=1, source_target_pairs={{0,16},{16,0},{1,17},{17,1},{2,18},{18,2},{3,19},{19,3},{4,20},{20... | collective-permute-start | bytes 1966088 | tf_op jit(solution)/shard_map/ppermute | solution.py:780
  1363.5 53.7 %collective-permute-start.46 = (bf16[512,1280]{1,0:T(8,128)(2,1)S(1)}, bf16[512,1280]{1,0:T(8,128)(2,1)S(1)}, u32[]{:S(2)}, u32[]{:S(2)}) collective-permute-start(bf16[512,1280]{1,0:T(8,128)(2,1)S(1)} %get-tuple-element.477), channel_id=1, source_target_pairs={{0,16},{16,0},{1,17},{17,1},{2,18},{18,2},{3,19},{19,3},{4,20},{20... | collective-permute-start | bytes 3932168 | tf_op jit(solution)/shard_map/ppermute | solution.py:780
  1430.4 254.6 %reduce-scatter.3.cloned.1.call-start = ((), (), s32[]{:S(2)}) async-start(), calls=%async_computation.8 | async-start | bytes 10096640 | tf_op jit(solution)/shard_map/reduce_scatter | solution.py:1099
  1434.4 48.9 %collective-permute-start.47 = (bf16[1024,1024]{1,0:T(8,128)(2,1)}, bf16[1024,1024]{1,0:T(8,128)(2,1)}, u32[]{:S(2)}, u32[]{:S(2)}) collective-permute-start(bf16[1024,1024]{1,0:T(8,128)(2,1)} %convert_element_type.136), channel_id=1, source_target_pairs={{0,16},{16,0},{1,17},{17,1},{2,18},{18,2},{3,19},{19,3},{4,20},{20... | collective-permute-start | bytes 6291464 | tf_op jit(solution)/shard_map/ppermute | solution.py:780
  1440.1 96.9 %collective-permute-start.48 = (bf16[512,2560]{1,0:T(8,128)(2,1)}, bf16[512,2560]{1,0:T(8,128)(2,1)S(1)}, u32[]{:S(2)}, u32[]{:S(2)}) collective-permute-start(bf16[512,2560]{1,0:T(8,128)(2,1)} %get-tuple-element.454), channel_id=1, source_target_pairs={{0,16},{16,0},{1,17},{17,1},{2,18},{18,2},{3,19},{19,3},{4,20},{20... | collective-permute-start | bytes 7864328 | tf_op jit(solution)/shard_map/ppermute | solution.py:780
  1566.6 42.1 %all-to-all-start.1 = ((bf16[16,80,512]{2,1,0:T(8,128)(2,1)}), bf16[16,80,512]{2,1,0:T(8,128)(2,1)}, u32[]{:S(2)}, u32[]{:S(2)}) async-start(bf16[16,80,512]{2,1,0:T(8,128)(2,1)} %bitcast.142), calls=%async_computation.3 | async-start | bytes 2621440 | tf_op jit(solution)/shard_map/all_to_all | solution.py:1119
  (96 other events, 1773.6 us)
Sparse Core Ops, SparseCore 0:
  11.6 154.4 all-gather.4
  169.0 101.7 all-gather.6
  286.3 205.7 all-gather.8
  493.5 222.1 all-gather.10
  1430.5 85.3 reduce-scatter.4
  1554.8 130.0 reduce-scatter.2
